TPU v7x, 256 devices: a whole 4x4x8 slice. The times are simulated.
256 devices in a mesh: gx: 32 (over x, y, core), gy: 8 (over z).
Axes of the slice: x: 4, y: 4, z: 8, core: 2. Of those that a mesh axis runs over, the one named last changes fastest.
Arguments:
- velocity: float32 [3, 1024, 256, 128], P(None, 'gx', 'gy'), may hold values from -5 to 5
- point_cells: int32 [3, 32, 8, 256], P(None, 'gx', 'gy'), may hold values from 0 to 1023, as said below
- point_offsets: float32 [3, 32, 8, 256], P(None, 'gx', 'gy'), may hold values from 0 to 1
- point_count: int32 [32, 8], P('gx', 'gy'), may hold values from 32 to 256, as said below
- drag: float32 [32, 8, 256], P('gx', 'gy'), may hold values from 30 to 300
- blade_speed: float32 [32, 8, 256], P('gx', 'gy'), may hold values from 0.5 to 2
Outputs:
- new_velocity: float32 [3, 1024, 256, 128], P(None, 'gx', 'gy')
- pressure: float32 [1024, 256, 128], P('gx', 'gy')
Inputs may be any that keep to these rules, and one draw needn't show every extreme that they name: Every point's cell lies in the grid block of the device that holds the point: point_cells[0, i, j, s] is in [i * 32, (i + 1) * 32), point_cells[1, i, j, s] in [j * 32, (j + 1) * 32), point_cells[2] in [0, 128). `point_count`: some device is full in every draw; loads are skewed.
All inputs are finite; a program needn't handle non-finite values.
Results may differ from a plain program's by a relative error of at most 0.0003.
Values sent between devices are 32-bit elements; how exact they have to be, the bound alone decides.
No kernel may reach another device: no remote copies, remote signals or barrier semaphores. Data moves between devices by JAX's collectives and lax.ppermute only.
A program may use at most 192 MiB of HBM per device.

v0:
```python
import functools

import jax
import jax.numpy as jnp
from jax import lax
from jax.experimental import pallas as pl
from jax.experimental.pallas import tpu as pltpu
from jax.sharding import PartitionSpec as P

AXES = ("gx", "gy")
NGX, NGY = 32, 8
W = 32
P_ = 256
F32 = jnp.float32
BF16 = jnp.bfloat16
VMEM = pltpu.VMEM
LIMIT = 40 * 1024 * 1024


def swap(x, fx, fy):
    perm = [(i * NGY + j, fx(i) * NGY + fy(j)) for i in range(NGX) for j in range(NGY)]
    return lax.ppermute(x, AXES, perm)


def same(i):
    return i


def pair(i):
    return i ^ 1


def other(n):
    return lambda i: (i + 1) % n if i % 2 else (i - 1) % n


def swap_gx(a, b):
    return swap(a, pair, same), swap(b, other(NGX), same)


def swap_gy(c, d):
    return swap(c, same, pair), swap(d, same, other(NGY))


def call(kernel, out_shapes, scratch, *args, flops=10_000_000):
    nbytes = sum(a.size * 4 for a in args) + sum(4 * functools.reduce(lambda x, y: x * y, s) for s in out_shapes)
    specs = [pl.BlockSpec(memory_space=pltpu.SMEM)] + [pl.BlockSpec(memory_space=VMEM)] * (len(args) - 1)
    return pl.pallas_call(
        kernel,
        out_shape=[jax.ShapeDtypeStruct(s, F32) for s in out_shapes],
        in_specs=specs,
        out_specs=[pl.BlockSpec(memory_space=VMEM)] * len(out_shapes),
        scratch_shapes=scratch,
        compiler_params=pltpu.CompilerParams(vmem_limit_bytes=LIMIT),
        cost_estimate=pl.CostEstimate(flops=flops, bytes_accessed=nbytes, transcendentals=0),
    )(*args)


def rows(lo, hi, unroll, body):
    n = hi - lo
    main = n // unroll
    if main > 1:

        def step(t, c):
            for u in range(unroll):
                body(lo + t * unroll + u, u)
            return c

        lax.fori_loop(0, main, step, 0)
        lo = lo + main * unroll
    for i in range(lo, hi):
        body(i, (i - lo) % unroll)


def place(info):
    ix, iy = info[0], info[1]
    return ix, iy, ix % 2, iy % 2


def okf(cond):
    return jnp.where(cond, 1.0, 0.0).astype(F32)


def hi_lo(par, a, b):
    return jnp.where(par == 0, a, b), jnp.where(par == 0, b, a)


def lanes(shape=(1, 128)):
    return lax.broadcasted_iota(jnp.int32, shape, len(shape) - 1)


def z_masks(s):
    lane = lanes()
    return okf(lane >= s), okf(lane < 128 - s)


def neighbours(ref, i, v, s, zm, ym=None):
    size = v.shape[0]
    up = pltpu.roll(v, 1, 0)
    down = pltpu.roll(v, size - 1, 0)
    if ym is not None:
        up, down = up * ym[0], down * ym[1]
    low = pltpu.roll(v, s, 1) * zm[0]
    high = pltpu.roll(v, 128 - s, 1) * zm[1]
    return (ref[i - 1] + ref[i + 1]) + (up + down) + (low + high)


def x_in(start, i, size):
    g = start + i
    return okf((g >= 0) & (g < size))


def y_edge(size):
    r = lax.broadcasted_iota(jnp.int32, (size, 1), 0)
    return okf(r > 0), okf(r < size - 1)


def y_domain(size, own, hi, start, total):
    r = lax.broadcasted_iota(jnp.int32, (size, 128), 0)
    g = start + jnp.where(r < own + hi, r, r - size)
    return okf((g >= 0) & (g < total))


def double_sweep(dst, b, lo, hi, s, dom, start, size, ym=None, unroll=2):
    zm = z_masks(s)

    def body(i, u):
        v = b[i]
        c = x_in(start, i, size) * (1.0 / 49.0)
        out = (8.0 * v + neighbours(b, i, v, s, zm, ym)) * c
        if dom is not None:
            out = out * dom[...]
        dst[i] = out

    rows(lo, hi, unroll, body)


def sweep(dst, v_ref, b, lo, hi, s, dom, start, size, ym=None, unroll=2):
    zm = z_masks(s)

    def body(i, u):
        v = v_ref[i]
        c = x_in(start, i, size) * (1.0 / 7.0)
        out = (v + b[i] + neighbours(v_ref, i, v, s, zm, ym)) * c
        if dom is not None:
            out = out * dom[...]
        dst[i] = out

    rows(lo, hi, unroll, body)


def z_pairs(t, s):
    lane = lanes(t.shape)
    return t + jnp.where((lane & s) == 0, pltpu.roll(t, 128 - s, 1), pltpu.roll(t, s, 1))


def restrict_rows(emit, v_ref, b, tmp, klo, khi, base, s, keep, ym=None, unroll=2):
    zm = z_masks(s)

    def body(k, u):
        i = base + 2 * k
        total = None
        for d in range(2):
            v = v_ref[i + d]
            r = b[i + d] - 6.0 * v + neighbours(v_ref, i + d, v, s, zm, ym)
            total = r if total is None else total + r
        tmp[u, 0 : total.shape[0], :] = total
        both = tmp[u, pl.ds(0, keep, stride=2), :] + tmp[u, pl.ds(1, keep, stride=2), :]
        emit(k, u, z_pairs(both, s) * 0.5)

    rows(klo, khi, unroll, body)


def correct(dst, v_ref, e_ref, tmp, klo, khi, base, pieces, size, dom, start, total, get=None, unroll=2):
    def body(k, u):
        e = e_ref[k] if get is None else get(k)
        for at, count, to in pieces:
            part = e[at : at + count]
            tmp[u, pl.ds(to, count, stride=2), :] = part
            tmp[u, pl.ds(to + 1, count, stride=2), :] = part
        wide = tmp[u, 0:size, :]
        for d in range(2):
            i = base + 2 * k + d
            out = v_ref[i] + wide
            if dom is not None:
                out = out * dom[...]
            dst[i] = out * x_in(start, i, total)

    rows(klo, khi, unroll, body)


def split3(x):
    hi = x.astype(BF16)
    lo = (x - hi.astype(F32)).astype(BF16)
    return hi, lo


def dot(a, b):
    return jnp.dot(a, b, preferred_element_type=F32)


def vec(ref, at):
    return jnp.concatenate([ref[at : at + 1, :], ref[at + 1 : at + 2, :]], axis=1)


def tap_norm(off):
    total = jnp.zeros_like(off)
    for k in range(-3, 5):
        u = (k - off) / 1.5
        total = total + jnp.exp(-u * u)
    return 1.0 / total


def taps(coord, cell, off, inv, ok=None):
    d = coord - cell
    u = (d - off) / 1.5
    hit = (d >= -3.0) & (d <= 4.0)
    if ok is not None:
        hit = hit & ok
    return jnp.where(hit, jnp.exp(-u * u) * inv, 0.0)


def row_coord(n, shift):
    return (lax.broadcasted_iota(jnp.int32, (n, 1), 0) + shift).astype(F32)


def cyc_coord(n, split):
    r = lax.broadcasted_iota(jnp.int32, (n, 1), 0)
    return jnp.where(r < split, r, r - n).astype(F32)


def pack_gy(info, vel, pts, c_out, d_out):
    ix, iy, px, py = place(info)

    def body(t, u):
        c = t // W
        x = t - c * W
        top = vel[c, x, W - 4 : W, :]
        bottom = vel[c, x, 0:4, :]
        to_hi, to_lo = top, bottom
        c_out[t] = jnp.where(py == 0, to_hi, to_lo)
        d_out[t] = jnp.where(py == 0, to_lo, to_hi)

    rows(0, 3 * W, 4, body)
    for k in range(3):
        c_out[3 * W + k] = pts[4 * k : 4 * k + 4, :]
        d_out[3 * W + k] = pts[4 * k : 4 * k + 4, :]


def pack_gx(info, vel, pts, c_in, d_in, a_out, b_out):
    ix, iy, px, py = place(info)
    ok_hi, ok_lo = okf(iy < NGY - 1), okf(iy > 0)
    off_a = jnp.where(px == 0, W - 4, 0)
    off_b = W - 4 - off_a
    for out, off in ((a_out, off_a), (b_out, off_b)):
        for c in range(3):
            for k in range(4):
                x = off + k
                e = c * 4 + k
                hi, lo = hi_lo(py, c_in[c * W + x], d_in[c * W + x])
                out[e, 0:W, :] = vel[c, x]
                out[e, W : W + 4, :] = hi * ok_hi
                out[e, W + 4 : W + 8, :] = lo * ok_lo
        out[12, 0:12, :] = pts[...]
        for k in range(3):
            hi, lo = hi_lo(py, c_in[3 * W + k], d_in[3 * W + k])
            out[12, 12 + 4 * k : 16 + 4 * k, :] = hi
            out[12, 24 + 4 * k : 28 + 4 * k, :] = lo
        out[12, 36:40, :] = jnp.zeros((4, 128), F32)


def force_kernel(info, vel, pts, sect, c_in, d_in, a_in, b_in, g_out, f_out, c_out, d_out, wide, wxs, dxs, acc):
    ix, iy, px, py = place(info)
    ok_hi, ok_lo = okf(iy < NGY - 1), okf(iy > 0)
    okx_hi, okx_lo = okf(ix < NGX - 1), okf(ix > 0)

    def fill(t, u):
        c = t // W
        x = t - c * W
        hi, lo = hi_lo(py, c_in[t], d_in[t])
        wide[c, x + 4, 0:W, :] = vel[c, x]
        wide[c, x + 4, W : W + 4, :] = hi * ok_hi
        wide[c, x + 4, W + 4 : W + 8, :] = lo * ok_lo

    rows(0, 3 * W, 2, fill)
    for c in range(3):
        for k in range(4):
            e = c * 4 + k
            hi, lo = hi_lo(px, a_in[e], b_in[e])
            wide[c, W + 4 + k] = hi * okx_hi
            wide[c, k] = lo * okx_lo

    start_x = (ix * W).astype(F32)
    start_y = (iy * W).astype(F32)
    cx = vec(pts, 0) - start_x
    cy = vec(pts, 2) - start_y
    cz = vec(pts, 4)
    ox, oy, oz = vec(pts, 6), vec(pts, 8), vec(pts, 10)
    nx, ny, nz = tap_norm(ox), tap_norm(oy), tap_norm(oz)
    z = row_coord(128, 0)

    wz = taps(z, cz, oz, nz)
    wz_hi, wz_lo = split3(wz)
    wz3 = jnp.concatenate([wz_hi, wz_lo, wz_hi], axis=0)
    wxs[0:40, :] = taps(row_coord(40, -4), cx, ox, nx)
    wy40 = taps(cyc_coord(40, 36), cy, oy, ny)
    for c in range(3):
        acc[c] = jnp.zeros((40, P_), F32)

    def sample(t, carry):
        for c in range(3):
            part = wide[c, pl.ds(t * 8, 8)].reshape(320, 128)
            hi, lo = split3(part)
            r = dot(jnp.concatenate([hi, hi, lo], axis=1), wz3).reshape(8, 40, P_)
            s = acc[c]
            for k in range(8):
                s = s + r[k] * wxs[pl.ds(t * 8 + k, 1), :]
            acc[c] = s
        return carry

    lax.fori_loop(0, 5, sample, 0)
    sampled = [jnp.sum(acc[c] * wy40, axis=0, keepdims=True) for c in range(3)]
    drag, blade = vec(sect, 0), vec(sect, 2)
    slot = lax.broadcasted_iota(jnp.int32, (1, P_), 1)
    live = okf(slot < info[2])
    speed = jnp.sqrt(sampled[0] * sampled[0] + sampled[1] * sampled[1] + sampled[2] * sampled[2] + blade * blade)
    pull = -(drag * speed * live)
    force = [pull * s for s in sampled]
    for c in range(3):
        f_out[2 * c : 2 * c + 1, :] = force[c][:, 0:128]
        f_out[2 * c + 1 : 2 * c + 2, :] = force[c][:, 128:256]
    f_out[6:8, :] = jnp.zeros((2, 128), F32)

    def axis_taps(coord, cell, off, inv, start, size):
        def at(shift):
            q = coord + shift
            ok = (q + start >= 0.0) & (q + start < size)
            return taps(q, cell, off, inv, ok)

        return at(0.0), at(1.0) - at(-1.0)

    wx, dx = axis_taps(row_coord(48, -5), cx, ox, nx, start_x, float(W * NGX))
    wy, dy = axis_taps(cyc_coord(48, 40), cy, oy, ny, start_y, float(W * NGY))
    wzz, dz = axis_taps(z, cz, oz, nz, 0.0, 128.0)
    wxs[...] = wx
    dxs[...] = dx
    r1_hi, r1_lo = split3(-0.5 * wzz.T)
    r2_hi, r2_lo = split3(-0.5 * dz.T)
    right = jnp.concatenate([r1_hi, r2_hi, r1_lo, r2_lo, r1_hi, r2_hi], axis=0)
    fy_dy = force[1] * dy
    fx_wy = force[0] * wy
    fz_wy = force[2] * wy

    def spread(t, carry):
        l1, l2 = [], []
        for k in range(7):
            i = t * 7 + k
            row_w = wxs[pl.ds(i, 1), :]
            row_d = dxs[pl.ds(i, 1), :]
            l1.append(row_d * fx_wy + row_w * fy_dy)
            l2.append(row_w * fz_wy)
        l1_hi, l1_lo = split3(jnp.concatenate(l1, axis=0))
        l2_hi, l2_lo = split3(jnp.concatenate(l2, axis=0))
        left = jnp.concatenate([l1_hi, l2_hi, l1_hi, l2_hi, l1_lo, l2_lo], axis=1)
        g_out[pl.ds(t * 7, 7)] = dot(left, right).reshape(7, 48, 128)
        return carry

    lax.fori_loop(0, 6, spread, 0)

    zm = z_masks(1)

    def rhs(x, u):
        vx = wide[0, x + 5, 0:W, :] - wide[0, x + 3, 0:W, :]
        vy = wide[1, x + 4]
        vy = pltpu.roll(vy, 39, 0)[0:W] - pltpu.roll(vy, 1, 0)[0:W]
        vz = wide[2, x + 4, 0:W, :]
        vz = pltpu.roll(vz, 127, 1) * zm[1] - pltpu.roll(vz, 1, 1) * zm[0]
        g_out[x + 5, 0:W, :] = g_out[x + 5, 0:W, :] - 0.5 * (vx + vy + vz)

    rows(0, W, 2, rhs)

    def pack(i, u):
        g = g_out[i]
        to_hi = g[24:40]
        to_lo = jnp.concatenate([g[40:48], g[0:8]], axis=0)
        c_out[i] = jnp.where(py == 0, to_hi, to_lo)
        d_out[i] = jnp.where(py == 0, to_lo, to_hi)

    rows(0, 42, 2, pack)


def merge_g(info, g, c_in, d_in, h_out, a_out, b_out):
    ix, iy, px, py = place(info)
    ok_hi, ok_lo = okf(iy < NGY - 1), okf(iy > 0)

    def body(i, u):
        hi, lo = hi_lo(py, c_in[i], d_in[i])
        hi, lo = hi * ok_hi, lo * ok_lo
        v = g[i]
        h_out[i, 0:8, :] = v[0:8] + lo[8:16]
        h_out[i, 8:24, :] = v[8:24]
        h_out[i, 24:40, :] = v[24:40] + hi
        h_out[i, 40:48, :] = v[40:48] + lo[0:8]

    rows(0, 42, 2, body)
    off_a = jnp.where(px == 0, 31, 0)
    off_b = 31 - off_a

    def pack(k, u):
        a_out[k] = h_out[off_a + k]
        b_out[k] = h_out[off_b + k]

    rows(0, 11, 2, pack)


def emit_level1(c_out, tmp1, v2, b, tmp):
    lane = lanes((16, 128))

    def emit(k, u, r):
        tmp1[k] = r

    restrict_rows(emit, v2, b, tmp, 0, 16, 6, 1, 16)
    for k in range(8):
        c_out[k] = jnp.where((lane & 1) == 0, tmp1[2 * k], tmp1[2 * k + 1])


def down0(info, h, a_in, b_in, f, b_out, v_out, c_out, dom, tmp, tmp1):
    ix, iy, px, py = place(info)
    okx_hi, okx_lo = okf(ix < NGX - 1), okf(ix > 0)
    dom[...] = y_domain(48, W, 8, iy * W, W * NGY)
    start = ix * W - 6

    def inner(i, u):
        b_out[i] = h[i - 1] * dom[...] * x_in(start, i, W * NGX)

    rows(1, 43, 2, inner)
    zero = jnp.zeros((48, 128), F32)
    b_out[0] = zero
    b_out[43] = zero

    def rim(k, u):
        hi, lo = hi_lo(px, a_in[k], b_in[k])
        b_out[k] = b_out[k] + lo * dom[...] * (okx_lo * x_in(start, k, W * NGX))
        j = k + 33
        b_out[j] = b_out[j] + hi * dom[...] * (okx_hi * x_in(start, j, W * NGX))

    rows(0, 11, 1, rim)
    v_out[0] = zero
    v_out[43] = zero
    double_sweep(v_out, b_out, 1, 43, 1, dom, start, W * NGX)
    emit_level1(c_out, tmp1, v_out, b_out, tmp)
    c_out[8, 0:8, :] = f[...]
    c_out[8, 8:16, :] = jnp.zeros((8, 128), F32)


def pack1_gx(info, own, c_in, d_in, a_out, b_out):
    ix, iy, px, py = place(info)
    ok_hi, ok_lo = okf(iy < NGY - 1), okf(iy > 0)
    off_a = jnp.where(px == 0, 3, 0)
    off_b = 3 - off_a
    for out, off in ((a_out, off_a), (b_out, off_b)):
        for k in range(6):
            e = off + k if k < 5 else 8
            hi, lo = hi_lo(py, c_in[e], d_in[e])
            out[k, 0:16, :] = own[e]
            out[k, 16:32, :] = hi * ok_hi
            out[k, 32:48, :] = lo * ok_lo


def down1(info, own, c_in, d_in, a_in, b_in, b1, v1, b2, v2, packed, dom1, dom2, tmp, tmp3):
    ix, iy, px, py = place(info)
    ok_hi, ok_lo = okf(iy < NGY - 1), okf(iy > 0)
    okx_hi, okx_lo = okf(ix < NGX - 1), okf(ix > 0)
    n1x, n1y = W * NGX // 2, W * NGY // 2
    dom1[...] = y_domain(48, 16, 16, iy * 16, n1y)
    dom2[...] = y_domain(24, 8, 8, iy * 8, n1y // 2)
    even = (lanes((48, 128)) & 1) == 0

    def unpack(at, p):
        b1[at] = jnp.where(even, p, pltpu.roll(p, 1, 1))
        b1[at + 1] = jnp.where(even, pltpu.roll(p, 127, 1), p)

    for k in range(8):
        hi, lo = hi_lo(py, c_in[k], d_in[k])
        unpack(10 + 2 * k, jnp.concatenate([own[k], hi * ok_hi, lo * ok_lo], axis=0))
    for k in range(5):
        hi, lo = hi_lo(px, a_in[k], b_in[k])
        unpack(2 * k, lo * okx_lo)
        unpack(26 + 2 * k, hi * okx_hi)
    zero1 = jnp.zeros((48, 128), F32)
    v1[0] = zero1
    v1[35] = zero1
    start1 = ix * 16 - 10
    double_sweep(v1, b1, 1, 35, 2, dom1, start1, n1x)
    start2 = ix * 8 - 4

    def emit2(k, u, r):
        b2[k] = r * dom2[...] * x_in(start2, k, n1x // 2)

    restrict_rows(emit2, v1, b1, tmp, 0, 16, 2, 2, 24)
    zero2 = jnp.zeros((24, 128), F32)
    v2[0] = zero2
    v2[15] = zero2
    double_sweep(v2, b2, 1, 15, 4, dom2, start2, n1x // 2)

    def emit3(k, u, r):
        tmp3[k] = r

    restrict_rows(emit3, v2, b2, tmp, 0, 4, 4, 4, 8)
    row = lax.broadcasted_iota(jnp.int32, (8, 128), 0)
    lane = lanes((8, 128)) & 7
    first = okf((lane == row) & (row < 4))
    second = okf((lane == row + 4) & (row < 4))
    for q in range(2):
        s = tmp3[2 * q] * first + tmp3[2 * q + 1] * second
        packed[q : q + 1, :] = jnp.sum(s, axis=0, keepdims=True)


def coarse_up(info, g, b1, v1, b2, v2, s):
    ix, iy, px, py = place(info)
    n3x = NGX * 4

    def load(d, u):
        at = ix - 7 + d
        ok = okf((at >= 0) & (at < NGX))
        at = jnp.clip(at, 0, NGX - 1)
        base = d * 16
        s.px[pl.ds(pl.multiple_of(base, 8), 8), :] = g[at, pl.ds(0, 8, stride=2), :] * ok
        s.px[pl.ds(pl.multiple_of(base + 8, 8), 8), :] = g[at, pl.ds(1, 8, stride=2), :] * ok

    rows(0, 15, 1, load)
    src = lax.broadcasted_iota(jnp.int32, (128, 1024), 0)
    dst = lax.broadcasted_iota(jnp.int32, (128, 1024), 1)
    pick = okf(src == ((dst & 127) >> 3) * 8 + (dst >> 7)).astype(BF16)
    x = s.px[...]
    x_hi, x_lo = split3(x)
    x_lo2 = (x - x_hi.astype(F32) - x_lo.astype(F32)).astype(BF16)
    s.pu[...] = dot(x_hi, pick) + dot(x_lo, pick) + dot(x_lo2, pick)

    def place3(d, u):
        for q in range(2):
            for j in range(8):
                part = s.pu[pl.ds(pl.multiple_of(d * 16 + q * 8, 8), 8), j * 128 : (j + 1) * 128]
                s.b3[d * 4 + 2 * q + (j >> 2), pl.ds(j & 3, 8, stride=4), :] = part

    rows(0, 15, 1, place3)
    e3, e4, e5 = y_edge(32), y_edge(16), y_edge(8)
    start3, start4, start5 = (ix - 7) * 4, (ix - 7) * 2, ix - 7
    z3, z4, z5 = jnp.zeros((32, 128), F32), jnp.zeros((16, 128), F32), jnp.zeros((8, 128), F32)
    for r, z, n in ((s.v3, z3, 60), (s.b4, z4, 30), (s.v4, z4, 30), (s.b5, z5, 15), (s.v5, z5, 15), (s.w5, z5, 15)):
        r[0] = z
        r[n - 1] = z
    double_sweep(s.v3, s.b3, 1, 59, 8, None, start3, n3x, e3)

    def emit4(k, u, r):
        s.b4[k] = r * x_in(start4, k, n3x // 2)

    restrict_rows(emit4, s.v3, s.b3, s.tmp, 1, 29, 0, 8, 16, e3)
    double_sweep(s.v4, s.b4, 1, 29, 16, None, start4, n3x // 2, e4)

    def emit5(k, u, r):
        s.b5[k] = r * x_in(start5, k, NGX)

    restrict_rows(emit5, s.v4, s.b4, s.tmp, 1, 14, 0, 16, 8, e4)
    double_sweep(s.v5, s.b5, 1, 14, 32, None, start5, NGX, e5)
    sweep(s.w5, s.v5, s.b5, 1, 14, 32, None, start5, NGX, e5)
    sweep(s.v5, s.w5, s.b5, 1, 14, 32, None, start5, NGX, e5)

    correct(s.w4, s.v4, s.v5, s.tmp, 5, 10, 0, ((0, 8, 0),), 16, None, start4, n3x // 2)
    sweep(s.v4, s.w4, s.b4, 11, 19, 16, None, start4, n3x // 2, e4)
    correct(s.w3, s.v3, s.v4, s.tmp, 12, 18, 0, ((0, 16, 0),), 32, None, start3, n3x)
    sweep(s.v3, s.w3, s.b3, 26, 34, 8, None, start3, n3x, e3)

    s.dom2[...] = y_domain(24, 8, 8, iy * 8, NGY * 8)
    s.dom1[...] = y_domain(48, 16, 16, iy * 16, NGY * 16)
    turn = lax.rem(32 - 4 * iy, 32)

    def shifted(k):
        return pltpu.roll(s.v3[k + 26], turn, 0)

    start2, start1 = ix * 8 - 4, ix * 16 - 10
    n2x, n1x = n3x * 2, n3x * 4
    correct(s.w2, v2, None, s.tmp, 0, 8, 0, ((0, 8, 0), (28, 4, 16)), 24, s.dom2, start2, n2x, shifted)
    sweep(s.e2, s.w2, b2, 2, 14, 4, s.dom2, start2, n2x)
    correct(s.w1, v1, s.e2, s.tmp, 2, 14, 2, ((0, 24, 0),), 48, s.dom1, start1, n1x)
    sweep(s.e1, s.w1, b1, 7, 29, 2, s.dom1, start1, n1x)


class Bag:
    pass


COARSE = (
    ("px", (240, 128)),
    ("pu", (240, 1024)),
    ("b3", (60, 32, 128)),
    ("v3", (60, 32, 128)),
    ("w3", (60, 32, 128)),
    ("b4", (30, 16, 128)),
    ("v4", (30, 16, 128)),
    ("w4", (30, 16, 128)),
    ("b5", (15, 8, 128)),
    ("v5", (15, 8, 128)),
    ("w5", (15, 8, 128)),
    ("w2", (16, 24, 128)),
    ("e2", (16, 24, 128)),
    ("w1", (36, 48, 128)),
    ("e1", (36, 48, 128)),
    ("w0", (44, 48, 128)),
    ("x0", (44, 48, 128)),
    ("dom0", (48, 128)),
    ("dom1", (48, 128)),
    ("dom2", (24, 128)),
    ("tmp", (4, 48, 128)),
    ("tmp1", (16, 16, 128)),
)
COARSE_SCRATCH = [pltpu.VMEM(shape, F32) for name, shape in COARSE]


def bag(refs):
    s = Bag()
    for (name, shape), ref in zip(COARSE, refs):
        setattr(s, name, ref)
    return s


PIECES0 = ((0, 20, 0), (44, 4, 40))


def middle(info, g, b0, v0, b1, v1, b2, v2, v_out, c_out, *scratch):
    s = bag(scratch)
    ix, iy, px, py = place(info)
    coarse_up(info, g, b1, v1, b2, v2, s)
    s.dom0[...] = y_domain(48, W, 8, iy * W, W * NGY)
    start, size = ix * W - 6, W * NGX
    correct(s.w0, v0, s.e1, s.tmp, 7, 29, -14, PIECES0, 48, s.dom0, start, size)
    sweep(s.x0, s.w0, b0, 2, 42, 1, s.dom0, start, size)
    sweep(s.w0, s.x0, b0, 3, 41, 1, s.dom0, start, size)
    sweep(v_out, s.w0, b0, 4, 40, 1, s.dom0, start, size)
    zero = jnp.zeros((48, 128), F32)
    for i in (0, 1, 2, 3, 40, 41, 42, 43):
        v_out[i] = zero
    emit_level1(c_out, s.tmp1, v_out, b0, s.tmp)


def final(info, g, b0, v0, b1, v1, b2, v2, pushed, vel_out, p_out, *scratch):
    s = bag(scratch)
    ix, iy, px, py = place(info)
    coarse_up(info, g, b1, v1, b2, v2, s)
    s.dom0[...] = y_domain(48, W, 8, iy * W, W * NGY)
    start, size = ix * W - 6, W * NGX
    correct(s.w0, v0, s.e1, s.tmp, 9, 27, -14, PIECES0, 48, s.dom0, start, size)
    sweep(s.x0, s.w0, b0, 5, 39, 1, s.dom0, start, size)
    zm = z_masks(1)

    def body(x, u):
        p = s.x0[x + 6]
        own = p[0:W]
        p_out[x] = own
        gx = s.x0[x + 7, 0:W, :] - s.x0[x + 5, 0:W, :]
        gy = pltpu.roll(p, 47, 0)[0:W] - pltpu.roll(p, 1, 0)[0:W]
        gz = pltpu.roll(own, 127, 1) * zm[1] - pltpu.roll(own, 1, 1) * zm[0]
        vel_out[0, x] = pushed[0, x] - 0.5 * gx
        vel_out[1, x] = pushed[1, x] - 0.5 * gy
        vel_out[2, x] = pushed[2, x] - 0.5 * gz

    rows(0, W, 2, body)


def push_kernel(info, vel, pts, f, c_in, d_in, a_in, b_in, c1, d1, a1, b1, out, wxs, pbuf):
    ix, iy, px, py = place(info)
    ok = {-1: (okf(ix > 0), okf(iy > 0)), 0: (1.0, 1.0), 1: (okf(ix < NGX - 1), okf(iy < NGY - 1))}
    start_x = (ix * W).astype(F32)
    start_y = (iy * W).astype(F32)

    def store(slot, points, forces):
        pbuf[slot, 0:12, :] = points
        pbuf[slot, 12:18, :] = forces

    def cat3(ref):
        return jnp.concatenate([ref[3 * W], ref[3 * W + 1], ref[3 * W + 2]], axis=0)

    hi, lo = hi_lo(py, cat3(c_in), cat3(d_in))
    fhi, flo = hi_lo(py, c1[8, 0:6, :], d1[8, 0:6, :])
    store(0, pts[...], f[0:6, :])
    store(1, hi, fhi)
    store(2, lo, flo)
    xhi, xlo = hi_lo(px, a_in[12], b_in[12])
    ghi, glo = hi_lo(px, a1[5], b1[5])
    for n, (q, fq) in enumerate(((xhi, ghi), (xlo, glo))):
        for m in range(3):
            store(3 + 3 * n + m, q[12 * m : 12 * m + 12], fq[16 * m : 16 * m + 6])

    order = ((0, 0), (0, 1), (0, -1), (1, 0), (1, 1), (1, -1), (-1, 0), (-1, 1), (-1, -1))
    for slot, (ox_, oy_) in enumerate(order):
        q = pbuf.at[slot]
        cx, cy, cz = vec(q, 0) - start_x, vec(q, 2) - start_y, vec(q, 4)
        ox, oy, oz = vec(q, 6), vec(q, 8), vec(q, 10)
        keep = ok[ox_][0] * ok[oy_][1]
        force = [vec(q, 12 + 2 * c) * keep for c in range(3)]
        wxs[...] = taps(row_coord(32, 0), cx, ox, tap_norm(ox))
        y0, yn = {0: (0, 32), 1: (24, 8), -1: (0, 8)}[oy_]
        wy = taps(row_coord(yn, y0), cy, oy, tap_norm(oy))
        wz = taps(row_coord(128, 0), cz, oz, tap_norm(oz)).T
        r_hi, r_lo = split3(wz)
        right = jnp.concatenate([r_hi, r_lo, r_hi], axis=0)
        fy = [force[c] * wy for c in range(3)]
        x0, xn = {0: (0, 32), 1: (28, 4), -1: (0, 4)}[ox_]
        step = min(xn, 4 if oy_ == 0 else 16)

        def spread(t, carry, x0=x0, step=step, fy=fy, right=right, y0=y0, yn=yn, slot=slot):
            at = x0 + t * step
            left = []
            for k in range(step):
                row = wxs[pl.ds(at + k, 1), :]
                left += [row * fy[c] for c in range(3)]
            hi, lo = split3(jnp.concatenate(left, axis=0))
            r = dot(jnp.concatenate([hi, hi, lo], axis=1), right).reshape(step, 3, yn, 128)
            for k in range(step):
                for c in range(3):
                    base = vel if slot == 0 else out
                    out[c, at + k, y0 : y0 + yn, :] = base[c, at + k, y0 : y0 + yn, :] + r[k, c]
            return carry

        lax.fori_loop(0, xn // step, spread, 0)


def gather3(packed):
    everyone = jnp.broadcast_to(packed[None], (NGX * NGY, 2, 128))
    return lax.all_to_all(everyone, AXES, 0, 0, tiled=True).reshape(NGX, 16, 128)


def level_one(info, own):
    c1, d1 = swap_gy(own, own)
    a1, b1 = call(pack1_gx, [(6, 48, 128)] * 2, [], info, own, c1, d1)
    a1, b1 = swap_gx(a1, b1)
    outs = call(
        down1,
        [(36, 48, 128), (36, 48, 128), (16, 24, 128), (16, 24, 128), (2, 128)],
        [VMEM((48, 128), F32), VMEM((24, 128), F32), VMEM((4, 48, 128), F32), VMEM((4, 8, 128), F32)],
        info, own, c1, d1, a1, b1,
    )
    return (c1, d1, a1, b1), outs[:4], gather3(outs[4])


def per_device(velocity, point_cells, point_offsets, point_count, drag, blade_speed):
    info = jnp.stack([lax.axis_index("gx"), lax.axis_index("gy"), point_count.reshape(())]).astype(jnp.int32)
    pts = jnp.concatenate([point_cells.astype(F32).reshape(6, 128), point_offsets.reshape(6, 128)], axis=0)
    sect = jnp.concatenate([drag.reshape(2, 128), blade_speed.reshape(2, 128)], axis=0)

    c0, d0 = call(pack_gy, [(99, 4, 128)] * 2, [], info, velocity, pts)
    c0, d0 = swap_gy(c0, d0)
    a0, b0 = call(pack_gx, [(13, 40, 128)] * 2, [], info, velocity, pts, c0, d0)
    a0, b0 = swap_gx(a0, b0)
    g, f, cg, dg = call(
        force_kernel,
        [(42, 48, 128), (8, 128), (42, 16, 128), (42, 16, 128)],
        [VMEM((3, 40, 40, 128), F32), VMEM((48, P_), F32), VMEM((48, P_), F32), VMEM((3, 40, P_), F32)],
        info, velocity, pts, sect, c0, d0, a0, b0,
    )
    cg, dg = swap_gy(cg, dg)
    h, ag, bg = call(merge_g, [(42, 48, 128), (11, 48, 128), (11, 48, 128)], [], info, g, cg, dg)
    ag, bg = swap_gx(ag, bg)
    rhs, v0, own1 = call(
        down0,
        [(44, 48, 128), (44, 48, 128), (9, 16, 128)],
        [VMEM((48, 128), F32), VMEM((4, 48, 128), F32), VMEM((16, 16, 128), F32)],
        info, h, ag, bg, f,
    )
    (c1, d1, a1, b1), levels, gathered = level_one(info, own1)
    (pushed,) = call(
        push_kernel,
        [(3, W, W, 128)],
        [VMEM((32, P_), F32), VMEM((9, 24, 128), F32)],
        info, velocity, pts, f, c0, d0, a0, b0, c1, d1, a1, b1,
    )
    v0, own1 = call(middle, [(44, 48, 128), (8, 16, 128)], COARSE_SCRATCH, info, gathered, rhs, v0, *levels)
    own1 = jnp.concatenate([own1, jnp.zeros((1, 16, 128), F32)], axis=0)
    unused, levels, gathered = level_one(info, own1)
    vel_out, p_out = call(
        final, [(3, W, W, 128), (W, W, 128)], COARSE_SCRATCH, info, gathered, rhs, v0, *levels, pushed
    )
    return vel_out, p_out


def solution(mesh):
    placed = (
        P(None, "gx", "gy", None),
        P(None, "gx", "gy", None),
        P(None, "gx", "gy", None),
        P("gx", "gy"),
        P("gx", "gy", None),
        P("gx", "gy", None),
    )
    return jax.shard_map(
        per_device,
        mesh=mesh,
        in_specs=placed,
        out_specs=(P(None, "gx", "gy", None), P("gx", "gy", None)),
        check_vma=False,
    )
```

profile of v0, /device:TPU:1, one launch (start us, length us, event | category | flops | bytes accessed | tf_op | source)
XLA Modules:
  0.0 197.3 jit_solution(16050624528086959025)
XLA Ops:
  2.8 1.4 copy-done
  4.2 1.3 shard_map.77
  5.5 2.6 %collective-permute-start = (f32[99,4,128]{2,1,0:T(4,128)S(1)}, f32[99,4,128]{2,1,0:T(4,128)S(1)}, u32[]{:S(2)}, u32[]{:S(2)}) collective-permute-start(f32[99,4,128]{2,1,0:T(4,128)S(1)} %get-tuple-element.32), channel_id=1, source_target_pairs={{0,1},{1,0},{2,3},{3,2},{4,5},{5,4},{6,7},{7,6},{8,9},{9,8},{10,11... | collective-permute-start | bytes 608264 | tf_op jit(solution)/shard_map/ppermute | solution.py:22
  8.1 4.7 %collective-permute-start.1 = (f32[99,4,128]{2,1,0:T(4,128)S(1)}, f32[99,4,128]{2,1,0:T(4,128)S(1)}, u32[]{:S(2)}, u32[]{:S(2)}) collective-permute-start(f32[99,4,128]{2,1,0:T(4,128)S(1)} %get-tuple-element.33), channel_id=1, source_target_pairs={{0,7},{1,2},{2,1},{3,4},{4,3},{5,6},{6,5},{7,0},{8,15},{9,10},{10,... | collective-permute-start | bytes 608264 | tf_op jit(solution)/shard_map/ppermute | solution.py:22
  12.7 4.4 %collective-permute-done.1.d_in = f32[99,4,128]{2,1,0:T(4,128)S(1)} collective-permute-done((f32[99,4,128]{2,1,0:T(4,128)S(1)}, f32[99,4,128]{2,1,0:T(4,128)S(1)}, u32[]{:S(2)}, u32[]{:S(2)}) %collective-permute-start.1) | collective-permute-done | bytes 202784 | tf_op jit(solution)/shard_map/ppermute | solution.py:22
  17.8 1.6 collective-permute-start.2
  19.4 1.3 collective-permute-start.3
  20.7 4.5 %collective-permute-done.3.b_in = f32[13,40,128]{2,1,0:T(8,128)S(1)} collective-permute-done((f32[13,40,128]{2,1,0:T(8,128)S(1)}, f32[13,40,128]{2,1,0:T(8,128)S(1)}, u32[]{:S(2)}, u32[]{:S(2)}) %collective-permute-start.3) | collective-permute-done | bytes 266272 | tf_op jit(solution)/shard_map/ppermute | solution.py:22
  25.2 8.6 %shard_map.79 = (f32[42,48,128]{2,1,0:T(8,128)S(1)}, f32[8,128]{1,0:T(8,128)S(1)}, f32[42,16,128]{2,1,0:T(8,128)S(1)}, f32[42,16,128]{2,1,0:T(8,128)S(1)}) custom-call(s32[3]{0:T(128)S(1)} %pad_add_fusion.info, f32[3,32,32,128]{3,2,1,0:T(8,128)S(1)} %copy-done, f32[12,128]{1,0:T(8,128)S(1)} %pad_maximum_fusion.pts, f32[4,128]{1,0:T(4,128)S(1)} %pad_maximum_fusion.1.sect, ...), custom_call_target="tpu_custom_call" | custom-call | flops 10000000 | bytes 4243468 | tf_op jit(solution)/shard_map/pallas_call | solution.py:48
  34.0 2.8 %collective-permute-start.5 = (f32[42,16,128]{2,1,0:T(8,128)S(1)}, f32[42,16,128]{2,1,0:T(8,128)S(1)}, u32[]{:S(2)}, u32[]{:S(2)}) collective-permute-start(f32[42,16,128]{2,1,0:T(8,128)S(1)} %get-tuple-element.38), channel_id=1, source_target_pairs={{0,7},{1,2},{2,1},{3,4},{4,3},{5,6},{6,5},{7,0},{8,15},{9,10},{10,... | collective-permute-start | bytes 1032200 | tf_op jit(solution)/shard_map/ppermute | solution.py:22
  36.8 3.3 %collective-permute-done.4.c_in = f32[42,16,128]{2,1,0:T(8,128)S(1)} collective-permute-done((f32[42,16,128]{2,1,0:T(8,128)S(1)}, f32[42,16,128]{2,1,0:T(8,128)S(1)}, u32[]{:S(2)}, u32[]{:S(2)}) %collective-permute-start.4) | collective-permute-done | bytes 344096 | tf_op jit(solution)/shard_map/ppermute | solution.py:22
  40.1 1.3 collective-permute-done.5.d_in
  42.2 4.8 %collective-permute-start.6 = (f32[11,48,128]{2,1,0:T(8,128)S(1)}, f32[11,48,128]{2,1,0:T(8,128)S(1)}, u32[]{:S(2)}, u32[]{:S(2)}) collective-permute-start(f32[11,48,128]{2,1,0:T(8,128)S(1)} %get-tuple-element.40), channel_id=1, source_target_pairs={{0,8},{1,9},{2,10},{3,11},{4,12},{5,13},{6,14},{7,15},{8,0},{9,1},... | collective-permute-start | bytes 811016 | tf_op jit(solution)/shard_map/ppermute | solution.py:22
  47.1 1.0 collective-permute-start.7
  48.2 5.0 %collective-permute-done.7.b_in = f32[11,48,128]{2,1,0:T(8,128)S(1)} collective-permute-done((f32[11,48,128]{2,1,0:T(8,128)S(1)}, f32[11,48,128]{2,1,0:T(8,128)S(1)}, u32[]{:S(2)}, u32[]{:S(2)}) %collective-permute-start.7) | collective-permute-done | bytes 270368 | tf_op jit(solution)/shard_map/ppermute | solution.py:22
  53.2 4.5 %shard_map.81 = (f32[44,48,128]{2,1,0:T(8,128)S(1)}, f32[44,48,128]{2,1,0:T(8,128)S(1)}, f32[9,16,128]{2,1,0:T(8,128)S(1)}) custom-call(s32[3]{0:T(128)S(1)} %pad_add_fusion.info, f32[42,48,128]{2,1,0:T(8,128)S(1)} %get-tuple-element.39.h, f32[11,48,128]{2,1,0:T(8,128)S(1)} %collective-permute-done.6.a_in, f32[11,48,128]{2,1,0:T(8,128)S(1)} %collective-permute-done.7.b_in, ...), custom_call_target="tpu_custom_call" | custom-call | flops 10000000 | bytes 3813388 | tf_op jit(solution)/shard_map/pallas_call | solution.py:48
  57.7 2.8 %collective-permute-start.9 = (f32[9,16,128]{2,1,0:T(8,128)S(1)}, f32[9,16,128]{2,1,0:T(8,128)S(1)}, u32[]{:S(2)}, u32[]{:S(2)}) collective-permute-start(f32[9,16,128]{2,1,0:T(8,128)S(1)} %get-tuple-element.43.own), channel_id=1, source_target_pairs={{0,7},{1,2},{2,1},{3,4},{4,3},{5,6},{6,5},{7,0},{8,15},{9,10},{10,... | collective-permute-start | bytes 221192 | tf_op jit(solution)/shard_map/ppermute | solution.py:22
  60.5 1.7 collective-permute-done.9.d_in.d1
  62.3 1.5 collective-permute-done.8.c_in.c1
  64.3 4.6 %collective-permute-start.10 = (f32[6,48,128]{2,1,0:T(8,128)S(1)}, f32[6,48,128]{2,1,0:T(8,128)S(1)}, u32[]{:S(2)}, u32[]{:S(2)}) collective-permute-start(f32[6,48,128]{2,1,0:T(8,128)S(1)} %get-tuple-element.44), channel_id=1, source_target_pairs={{0,8},{1,9},{2,10},{3,11},{4,12},{5,13},{6,14},{7,15},{8,0},{9,1},... | collective-permute-start | bytes 442376 | tf_op jit(solution)/shard_map/ppermute | solution.py:22
  68.9 1.0 collective-permute-done.10.a_in.a1
  69.9 3.6 %collective-permute-done.11.b_in.b1 = f32[6,48,128]{2,1,0:T(8,128)S(1)} collective-permute-done((f32[6,48,128]{2,1,0:T(8,128)S(1)}, f32[6,48,128]{2,1,0:T(8,128)S(1)}, u32[]{:S(2)}, u32[]{:S(2)}) %collective-permute-start.11) | collective-permute-done | bytes 147488 | tf_op jit(solution)/shard_map/ppermute | solution.py:22
  73.5 5.1 %shard_map.83 = (f32[36,48,128]{2,1,0:T(8,128)S(1)}, f32[36,48,128]{2,1,0:T(8,128)S(1)}, f32[16,24,128]{2,1,0:T(8,128)S(1)}, f32[16,24,128]{2,1,0:T(8,128)S(1)}, f32[2,128]{1,0:T(2,128)S(1)}) custom-call(s32[3]{0:T(128)S(1)} %pad_add_fusion.info, f32[9,16,128]{2,1,0:T(8,128)S(1)} %get-tuple-element.43.own, f32[9,16,128]{2,1,0:T(8,128)S(1)} %collective-permute-done.8.c_in.c1, ...), custom_call_target="tpu_custom_call" | custom-call | flops 10000000 | bytes 2679820 | tf_op jit(solution)/shard_map/pallas_call | solution.py:48
  78.7 26.4 %all_to_all.10 = f32[256,2,128]{2,1,0:T(2,128)S(1)} all-to-all(f32[256,2,128]{2,1,0:T(2,128)S(1)} %broadcast_in_dim.4), channel_id=1, replica_groups=mesh['gx'=32,'gy'=8] {'gx','gy'}, dimensions={0} | all-to-all | bytes 524288 | tf_op jit(solution)/shard_map/all_to_all | solution.py:730
  105.2 20.2 %shard_map.84 = (f32[44,48,128]{2,1,0:T(8,128)S(1)}, f32[8,16,128]{2,1,0:T(8,128)S(1)}) custom-call(s32[3]{0:T(128)S(1)} %pad_add_fusion.info, f32[32,16,128]{2,1,0:T(8,128)S(1)} %bitcast.8, f32[44,48,128]{2,1,0:T(8,128)S(1)} %get-tuple-element.47.b0, f32[44,48,128]{2,1,0:T(8,128)S(1)} %get-tuple-element.48.v0, f32[36,48,128]{2,1,0:T(8,128)S(1)} %get-tuple-element.49.b1, ...), custom_call_target="tpu_custom_call" | custom-call | flops 10000000 | bytes 5734412 | tf_op jit(solution)/shard_map/pallas_call | solution.py:48
  125.4 1.0 copy-done.4
  126.9 1.0 collective-permute-start.12
  127.8 3.3 %collective-permute-done.13.d_in = f32[9,16,128]{2,1,0:T(8,128)S(1)} collective-permute-done((f32[9,16,128]{2,1,0:T(8,128)S(1)}, f32[9,16,128]{2,1,0:T(8,128)S(1)}, u32[]{:S(2)}, u32[]{:S(2)}) %collective-permute-start.13) | collective-permute-done | bytes 73760 | tf_op jit(solution)/shard_map/ppermute | solution.py:22
  131.7 2.0 collective-permute-start.14
  133.7 1.0 collective-permute-done.14.a_in
  134.7 3.6 %collective-permute-done.15.b_in = f32[6,48,128]{2,1,0:T(8,128)S(1)} collective-permute-done((f32[6,48,128]{2,1,0:T(8,128)S(1)}, f32[6,48,128]{2,1,0:T(8,128)S(1)}, u32[]{:S(2)}, u32[]{:S(2)}) %collective-permute-start.15) | collective-permute-done | bytes 147488 | tf_op jit(solution)/shard_map/ppermute | solution.py:22
  138.2 5.1 %shard_map.86 = (f32[36,48,128]{2,1,0:T(8,128)S(1)}, f32[36,48,128]{2,1,0:T(8,128)S(1)}, f32[16,24,128]{2,1,0:T(8,128)S(1)}, f32[16,24,128]{2,1,0:T(8,128)S(1)}, f32[2,128]{1,0:T(2,128)S(1)}) custom-call(s32[3]{0:T(128)S(1)} %pad_add_fusion.info, f32[9,16,128]{2,1,0:T(8,128)S(1)} %concatenate.11.own, f32[9,16,128]{2,1,0:T(8,128)S(1)} %collective-permute-done.12.c_in, ...), custom_call_target="tpu_custom_call" | custom-call | flops 10000000 | bytes 2679820 | tf_op jit(solution)/shard_map/pallas_call | solution.py:48
  143.4 0.9 copy-done.10
  144.3 0.9 copy-done.12
  147.4 10.0 %all-to-all-start.1 = ((f32[256,2,128]{2,1,0:T(2,128)}), f32[256,2,128]{2,1,0:T(2,128)}, u32[]{:S(2)}, u32[]{:S(2)}) async-start(f32[256,2,128]{2,1,0:T(2,128)} %broadcast_in_dim.5), calls=%async_computation.1 | async-start | bytes 524288 | tf_op jit(solution)/shard_map/all_to_all | solution.py:730
  157.4 0.9 copy-done.7
  158.3 0.9 copy-done.9
  161.1 0.9 copy-done.19
  162.0 0.9 copy-done.21
  164.9 6.1 %shard_map.87.pushed = f32[3,32,32,128]{3,2,1,0:T(8,128)S(1)} custom-call(s32[3]{0:T(128)S(1)} %copy-done.29, f32[3,32,32,128]{3,2,1,0:T(8,128)S(1)} %copy-done.1, f32[12,128]{1,0:T(8,128)S(1)} %copy-done.23, f32[8,128]{1,0:T(8,128)S(1)} %copy-done.32, f32[99,4,128]{2,1,0:T(4,128)S(1)} %collective-permute-done.c_in, ...), custom_call_target="tpu_custom_call" | custom-call | flops 10000000 | bytes 4536332 | tf_op jit(solution)/shard_map/pallas_call | solution.py:48
  171.0 1.2 all-to-all-done.1
  172.2 1.2 copy-done.3
  173.5 1.2 copy-done.5
  174.7 1.2 copy-done.11
  175.9 1.2 copy-done.13
  177.0 0.9 copy-done.25
  178.0 0.9 copy-done.27
  179.5 17.8 %shard_map.88 = (f32[3,32,32,128]{3,2,1,0:T(8,128)}, f32[32,32,128]{2,1,0:T(8,128)}) custom-call(s32[3]{0:T(128)S(1)} %copy-done.30, f32[32,16,128]{2,1,0:T(8,128)} %bitcast.6.g, f32[44,48,128]{2,1,0:T(8,128)S(1)} %copy-done.3, f32[44,48,128]{2,1,0:T(8,128)S(1)} %copy-done.5, f32[36,48,128]{2,1,0:T(8,128)S(1)} %copy-done.11, f32[36,48,128]{2,1,0:T(8,128)S(1)} %copy-done.13, ...), custom_call_target="tpu_custom_call" | custom-call | flops 10000000 | bytes 8257548 | tf_op jit(solution)/shard_map/pallas_call | solution.py:48
  (79 shorter events, 11.5 us)
Async XLA Ops:
  2.7 22.5 %copy-start.22 = (f32[12,128]{1,0:T(8,128)}, f32[12,128]{1,0:T(8,128)S(1)}, u32[]{:S(2)}) copy-start(f32[12,128]{1,0:T(8,128)S(1)} %pad_maximum_fusion.pts) | copy-start | bytes 18436
  2.8 1.4 copy-start
  4.2 134.0 %copy-start.28 = (s32[3]{0:T(128)}, s32[3]{0:T(128)S(1)}, u32[]{:S(2)}) copy-start(s32[3]{0:T(128)S(1)} %pad_add_fusion.info) | copy-start | bytes 40
  4.2 16.5 %copy-start.33 = (f32[1,1,256]{2,1,0:T(1,128)S(1)}, f32[1,1,256]{2,1,0:T(1,128)}, u32[]{:S(2)}) copy-start(f32[1,1,256]{2,1,0:T(1,128)} %param.11) | copy-start | bytes 3076
  4.2 16.5 %copy-start.34 = (f32[1,1,256]{2,1,0:T(1,128)S(1)}, f32[1,1,256]{2,1,0:T(1,128)}, u32[]{:S(2)}) copy-start(f32[1,1,256]{2,1,0:T(1,128)} %param.10) | copy-start | bytes 3076
  5.5 7.2 %collective-permute-start = (f32[99,4,128]{2,1,0:T(4,128)S(1)}, f32[99,4,128]{2,1,0:T(4,128)S(1)}, u32[]{:S(2)}, u32[]{:S(2)}) collective-permute-start(f32[99,4,128]{2,1,0:T(4,128)S(1)} %get-tuple-element.32), channel_id=1, source_target_pairs={{0,1},{1,0},{2,3},{3,2},{4,5},{5,4},{6,7},{7,6},{8,9},{9,8},{10,11... | collective-permute-start | bytes 608264 | tf_op jit(solution)/shard_map/ppermute | solution.py:22
  8.1 9.1 %collective-permute-start.1 = (f32[99,4,128]{2,1,0:T(4,128)S(1)}, f32[99,4,128]{2,1,0:T(4,128)S(1)}, u32[]{:S(2)}, u32[]{:S(2)}) collective-permute-start(f32[99,4,128]{2,1,0:T(4,128)S(1)} %get-tuple-element.33), channel_id=1, source_target_pairs={{0,7},{1,2},{2,1},{3,4},{4,3},{5,6},{6,5},{7,0},{8,15},{9,10},{10,... | collective-permute-start | bytes 608264 | tf_op jit(solution)/shard_map/ppermute | solution.py:22
  17.8 2.9 %collective-permute-start.2 = (f32[13,40,128]{2,1,0:T(8,128)S(1)}, f32[13,40,128]{2,1,0:T(8,128)S(1)}, u32[]{:S(2)}, u32[]{:S(2)}) collective-permute-start(f32[13,40,128]{2,1,0:T(8,128)S(1)} %get-tuple-element.34), channel_id=1, source_target_pairs={{0,8},{1,9},{2,10},{3,11},{4,12},{5,13},{6,14},{7,15},{8,0},{9,1},... | collective-permute-start | bytes 798728 | tf_op jit(solution)/shard_map/ppermute | solution.py:22
  19.4 5.8 %collective-permute-start.3 = (f32[13,40,128]{2,1,0:T(8,128)S(1)}, f32[13,40,128]{2,1,0:T(8,128)S(1)}, u32[]{:S(2)}, u32[]{:S(2)}) collective-permute-start(f32[13,40,128]{2,1,0:T(8,128)S(1)} %get-tuple-element.35), channel_id=1, source_target_pairs={{0,248},{1,249},{2,250},{3,251},{4,252},{5,253},{6,254},{7,255},{8... | collective-permute-start | bytes 798728 | tf_op jit(solution)/shard_map/ppermute | solution.py:22
  20.7 13.2 %copy-start.6 = (f32[13,40,128]{2,1,0:T(8,128)}, f32[13,40,128]{2,1,0:T(8,128)S(1)}, u32[]{:S(2)}) copy-start(f32[13,40,128]{2,1,0:T(8,128)S(1)} %collective-permute-done.2.a_in) | copy-start | bytes 798724
  25.2 8.7 %copy-start.8 = (f32[13,40,128]{2,1,0:T(8,128)}, f32[13,40,128]{2,1,0:T(8,128)S(1)}, u32[]{:S(2)}) copy-start(f32[13,40,128]{2,1,0:T(8,128)S(1)} %collective-permute-done.3.b_in) | copy-start | bytes 798724
  33.9 23.8 %copy-start.31 = (f32[8,128]{1,0:T(8,128)}, f32[8,128]{1,0:T(8,128)S(1)}, u32[]{:S(2)}) copy-start(f32[8,128]{1,0:T(8,128)S(1)} %get-tuple-element.42.f) | copy-start | bytes 12292
  33.9 6.2 %collective-permute-start.4 = (f32[42,16,128]{2,1,0:T(8,128)S(1)}, f32[42,16,128]{2,1,0:T(8,128)S(1)}, u32[]{:S(2)}, u32[]{:S(2)}) collective-permute-start(f32[42,16,128]{2,1,0:T(8,128)S(1)} %get-tuple-element.37), channel_id=1, source_target_pairs={{0,1},{1,0},{2,3},{3,2},{4,5},{5,4},{6,7},{7,6},{8,9},{9,8},{10,11... | collective-permute-start | bytes 1032200 | tf_op jit(solution)/shard_map/ppermute | solution.py:22
  34.0 7.4 %collective-permute-start.5 = (f32[42,16,128]{2,1,0:T(8,128)S(1)}, f32[42,16,128]{2,1,0:T(8,128)S(1)}, u32[]{:S(2)}, u32[]{:S(2)}) collective-permute-start(f32[42,16,128]{2,1,0:T(8,128)S(1)} %get-tuple-element.38), channel_id=1, source_target_pairs={{0,7},{1,2},{2,1},{3,4},{4,3},{5,6},{6,5},{7,0},{8,15},{9,10},{10,... | collective-permute-start | bytes 1032200 | tf_op jit(solution)/shard_map/ppermute | solution.py:22
  42.2 6.0 %collective-permute-start.6 = (f32[11,48,128]{2,1,0:T(8,128)S(1)}, f32[11,48,128]{2,1,0:T(8,128)S(1)}, u32[]{:S(2)}, u32[]{:S(2)}) collective-permute-start(f32[11,48,128]{2,1,0:T(8,128)S(1)} %get-tuple-element.40), channel_id=1, source_target_pairs={{0,8},{1,9},{2,10},{3,11},{4,12},{5,13},{6,14},{7,15},{8,0},{9,1},... | collective-permute-start | bytes 811016 | tf_op jit(solution)/shard_map/ppermute | solution.py:22
  47.1 6.2 %collective-permute-start.7 = (f32[11,48,128]{2,1,0:T(8,128)S(1)}, f32[11,48,128]{2,1,0:T(8,128)S(1)}, u32[]{:S(2)}, u32[]{:S(2)}) collective-permute-start(f32[11,48,128]{2,1,0:T(8,128)S(1)} %get-tuple-element.41), channel_id=1, source_target_pairs={{0,248},{1,249},{2,250},{3,251},{4,252},{5,253},{6,254},{7,255},{8... | collective-permute-start | bytes 811016 | tf_op jit(solution)/shard_map/ppermute | solution.py:22
  57.7 67.6 %copy-start.2 = (f32[44,48,128]{2,1,0:T(8,128)}, f32[44,48,128]{2,1,0:T(8,128)S(1)}, u32[]{:S(2)}) copy-start(f32[44,48,128]{2,1,0:T(8,128)S(1)} %get-tuple-element.47.b0) | copy-start | bytes 3244036
  57.7 4.5 %collective-permute-start.9 = (f32[9,16,128]{2,1,0:T(8,128)S(1)}, f32[9,16,128]{2,1,0:T(8,128)S(1)}, u32[]{:S(2)}, u32[]{:S(2)}) collective-permute-start(f32[9,16,128]{2,1,0:T(8,128)S(1)} %get-tuple-element.43.own), channel_id=1, source_target_pairs={{0,7},{1,2},{2,1},{3,4},{4,3},{5,6},{6,5},{7,0},{8,15},{9,10},{10,... | collective-permute-start | bytes 221192 | tf_op jit(solution)/shard_map/ppermute | solution.py:22
  60.5 3.2 %collective-permute-start.8 = (f32[9,16,128]{2,1,0:T(8,128)S(1)}, f32[9,16,128]{2,1,0:T(8,128)S(1)}, u32[]{:S(2)}, u32[]{:S(2)}) collective-permute-start(f32[9,16,128]{2,1,0:T(8,128)S(1)} %get-tuple-element.43.own), channel_id=1, source_target_pairs={{0,1},{1,0},{2,3},{3,2},{4,5},{5,4},{6,7},{7,6},{8,9},{9,8},{10,11... | collective-permute-start | bytes 221192 | tf_op jit(solution)/shard_map/ppermute | solution.py:22
  62.2 63.1 %copy-start.14 = (f32[9,16,128]{2,1,0:T(8,128)}, f32[9,16,128]{2,1,0:T(8,128)S(1)}, u32[]{:S(2)}) copy-start(f32[9,16,128]{2,1,0:T(8,128)S(1)} %collective-permute-done.9.d_in.d1) | copy-start | bytes 221188
  63.7 41.4 %copy-start.16 = (f32[9,16,128]{2,1,0:T(8,128)}, f32[9,16,128]{2,1,0:T(8,128)S(1)}, u32[]{:S(2)}) copy-start(f32[9,16,128]{2,1,0:T(8,128)S(1)} %collective-permute-done.8.c_in.c1) | copy-start | bytes 221188
  64.3 5.6 %collective-permute-start.10 = (f32[6,48,128]{2,1,0:T(8,128)S(1)}, f32[6,48,128]{2,1,0:T(8,128)S(1)}, u32[]{:S(2)}, u32[]{:S(2)}) collective-permute-start(f32[6,48,128]{2,1,0:T(8,128)S(1)} %get-tuple-element.44), channel_id=1, source_target_pairs={{0,8},{1,9},{2,10},{3,11},{4,12},{5,13},{6,14},{7,15},{8,0},{9,1},... | collective-permute-start | bytes 442376 | tf_op jit(solution)/shard_map/ppermute | solution.py:22
  68.9 4.6 %collective-permute-start.11 = (f32[6,48,128]{2,1,0:T(8,128)S(1)}, f32[6,48,128]{2,1,0:T(8,128)S(1)}, u32[]{:S(2)}, u32[]{:S(2)}) collective-permute-start(f32[6,48,128]{2,1,0:T(8,128)S(1)} %get-tuple-element.45), channel_id=1, source_target_pairs={{0,248},{1,249},{2,250},{3,251},{4,252},{5,253},{6,254},{7,255},{8... | collective-permute-start | bytes 442376 | tf_op jit(solution)/shard_map/ppermute | solution.py:22
  69.9 55.4 %copy-start.18 = (f32[6,48,128]{2,1,0:T(8,128)}, f32[6,48,128]{2,1,0:T(8,128)S(1)}, u32[]{:S(2)}) copy-start(f32[6,48,128]{2,1,0:T(8,128)S(1)} %collective-permute-done.10.a_in.a1) | copy-start | bytes 442372
  73.5 31.7 %copy-start.20 = (f32[6,48,128]{2,1,0:T(8,128)}, f32[6,48,128]{2,1,0:T(8,128)S(1)}, u32[]{:S(2)}) copy-start(f32[6,48,128]{2,1,0:T(8,128)S(1)} %collective-permute-done.11.b_in.b1) | copy-start | bytes 442372
  125.4 1.0 copy-start.4
  126.4 30.9 %copy-start.1 = (f32[3,32,32,128]{3,2,1,0:T(8,128)S(1)}, f32[3,32,32,128]{3,2,1,0:T(8,128)}, u32[]{:S(2)}) copy-start(f32[3,32,32,128]{3,2,1,0:T(8,128)} %vel.7) | copy-start | bytes 4718596
  126.4 4.7 %collective-permute-start.13 = (f32[9,16,128]{2,1,0:T(8,128)S(1)}, f32[9,16,128]{2,1,0:T(8,128)S(1)}, u32[]{:S(2)}, u32[]{:S(2)}) collective-permute-start(f32[9,16,128]{2,1,0:T(8,128)S(1)} %concatenate.11.own), channel_id=1, source_target_pairs={{0,7},{1,2},{2,1},{3,4},{4,3},{5,6},{6,5},{7,0},{8,15},{9,10},{10,... | collective-permute-start | bytes 221192 | tf_op jit(solution)/shard_map/ppermute | solution.py:22
  126.9 4.2 %collective-permute-start.12 = (f32[9,16,128]{2,1,0:T(8,128)S(1)}, f32[9,16,128]{2,1,0:T(8,128)S(1)}, u32[]{:S(2)}, u32[]{:S(2)}) collective-permute-start(f32[9,16,128]{2,1,0:T(8,128)S(1)} %concatenate.11.own), channel_id=1, source_target_pairs={{0,1},{1,0},{2,3},{3,2},{4,5},{5,4},{6,7},{7,6},{8,9},{9,8},{10,11... | collective-permute-start | bytes 221192 | tf_op jit(solution)/shard_map/ppermute | solution.py:22
  131.7 3.0 %collective-permute-start.14 = (f32[6,48,128]{2,1,0:T(8,128)S(1)}, f32[6,48,128]{2,1,0:T(8,128)S(1)}, u32[]{:S(2)}, u32[]{:S(2)}) collective-permute-start(f32[6,48,128]{2,1,0:T(8,128)S(1)} %get-tuple-element.54), channel_id=1, source_target_pairs={{0,8},{1,9},{2,10},{3,11},{4,12},{5,13},{6,14},{7,15},{8,0},{9,1},... | collective-permute-start | bytes 442376 | tf_op jit(solution)/shard_map/ppermute | solution.py:22
  133.7 4.6 %collective-permute-start.15 = (f32[6,48,128]{2,1,0:T(8,128)S(1)}, f32[6,48,128]{2,1,0:T(8,128)S(1)}, u32[]{:S(2)}, u32[]{:S(2)}) collective-permute-start(f32[6,48,128]{2,1,0:T(8,128)S(1)} %get-tuple-element.55), channel_id=1, source_target_pairs={{0,248},{1,249},{2,250},{3,251},{4,252},{5,253},{6,254},{7,255},{8... | collective-permute-start | bytes 442376 | tf_op jit(solution)/shard_map/ppermute | solution.py:22
  143.4 0.9 copy-start.10
  144.3 0.9 copy-start.12
  145.2 0.7 copy-start.24
  147.4 24.8 %all-to-all-start.1 = ((f32[256,2,128]{2,1,0:T(2,128)}), f32[256,2,128]{2,1,0:T(2,128)}, u32[]{:S(2)}, u32[]{:S(2)}) async-start(f32[256,2,128]{2,1,0:T(2,128)} %broadcast_in_dim.5), calls=%async_computation.1 | async-start | bytes 524288 | tf_op jit(solution)/shard_map/all_to_all | solution.py:730
  157.4 1.0 copy-start.7
  158.3 1.0 copy-start.9
  159.3 0.9 copy-start.15
  160.2 0.9 copy-start.17
  161.1 0.9 copy-start.19
  162.0 0.9 copy-start.21
  162.9 0.7 copy-start.23
  172.2 1.2 copy-start.3
  173.5 1.2 copy-start.5
  174.7 1.2 copy-start.11
  175.9 1.2 copy-start.13
  177.0 0.9 copy-start.25
  178.0 0.9 copy-start.27
  (4 other events, 2.6 us)
where the time goes:
time: 198 us; the launch traced here: 197 us
  Pallas kernels  71.4 us (36%)
  starting transfers between devices  39.5 us (20%)
  waiting for transfers between devices  35.6 us (18%)
  blocking collectives  26.4 us (13%)
  local copies, waits for them, and re-layouts  21.3 us (11%)
    pallas_call x12, Pallas kernels, call(): pl.pallas_call(kernel, out_shape=[jax.ShapeDtypeStruct(s, F32) for s in o...  71.4 us
    ppermute x16, waiting for transfers between devices, swap(): return lax.ppermute(x, AXES, perm)  34.4 us
    ppermute x16, starting transfers between devices, swap(): return lax.ppermute(x, AXES, perm)  29.5 us
    all_to_all x1, blocking collectives, gather3(): lax.all_to_all(everyone, AXES, 0, 0, tiled=True).reshape(NGX, 16, 128)  26.4 us
    unnamed x70, local copies, waits for them, and re-layouts  20.5 us
    all_to_all x1, starting transfers between devices, gather3(): lax.all_to_all(everyone, AXES, 0, 0, tiled=True).reshape(NGX, 16, 128)  9.98 us
  transfers between devices with their start and end apart: 17, of which 14 were waited for; matrix products, arithmetic and copies ran while one was open for 0% of the time, Pallas kernels for 3%

commit v1 on v0

--- a/solution.py
+++ b/solution.py
@@ -14,7 +14,8 @@
 F32 = jnp.float32
 BF16 = jnp.bfloat16
 VMEM = pltpu.VMEM
-LIMIT = 40 * 1024 * 1024
+LIMIT = 24 * 1024 * 1024
+WHOLE = 63 * 1024 * 1024
 
 
 def swap(x, fx, fy):
@@ -42,23 +43,76 @@
     return swap(c, same, pair), swap(d, same, other(NGY))
 
 
-def call(kernel, out_shapes, scratch, *args, flops=10_000_000):
+class Late:
+    def __init__(self, copy, ref):
+        self.copy, self.ref, self.done = copy, ref, False
+
+    def get(self):
+        if not self.done:
+            self.copy.wait()
+            self.done = True
+        return self.ref
+
+
+def use(x):
+    return x.get() if isinstance(x, Late) else x
+
+
+class Early:
+    def __init__(self, copy, ref):
+        self.copy, self.ref, self.sent = copy, ref, False
+
+    def flush(self):
+        if not self.sent:
+            self.copy.start()
+            self.sent = True
+
+
+def call(kernel, out_shapes, scratch, *args, late=(), early=()):
     nbytes = sum(a.size * 4 for a in args) + sum(4 * functools.reduce(lambda x, y: x * y, s) for s in out_shapes)
-    specs = [pl.BlockSpec(memory_space=pltpu.SMEM)] + [pl.BlockSpec(memory_space=VMEM)] * (len(args) - 1)
+    n_in, n_out = len(args), len(out_shapes)
+
+    def body(*refs):
+        ins, outs = list(refs[:n_in]), list(refs[n_in : n_in + n_out])
+        rest = refs[n_in + n_out :]
+        own, rest = rest[: len(scratch)], rest[len(scratch) :]
+        if late or early:
+            bufs, sems = rest[:-1], rest[-1]
+        for n, at in enumerate(late):
+            copy = pltpu.make_async_copy(ins[at], bufs[n], sems.at[n])
+            copy.start()
+            ins[at] = Late(copy, bufs[n])
+        for n, at in enumerate(early):
+            k = len(late) + n
+            outs[at] = Early(pltpu.make_async_copy(bufs[k], outs[at], sems.at[k]), bufs[k])
+        kernel(*ins, *outs, *own)
+        for at in late:
+            use(ins[at])
+        for at in early:
+            outs[at].flush()
+        for at in early:
+            outs[at].copy.wait()
+
+    specs = [pl.BlockSpec(memory_space=pltpu.SMEM)] + [
+        pl.BlockSpec(memory_space=pltpu.HBM if n in late else VMEM) for n in range(1, n_in)
+    ]
+    extra = [VMEM(args[n].shape, args[n].dtype) for n in late] + [VMEM(out_shapes[n], F32) for n in early]
+    if extra:
+        extra.append(pltpu.SemaphoreType.DMA((len(extra),)))
     return pl.pallas_call(
-        kernel,
+        body,
         out_shape=[jax.ShapeDtypeStruct(s, F32) for s in out_shapes],
         in_specs=specs,
-        out_specs=[pl.BlockSpec(memory_space=VMEM)] * len(out_shapes),
-        scratch_shapes=scratch,
-        compiler_params=pltpu.CompilerParams(vmem_limit_bytes=LIMIT),
-        cost_estimate=pl.CostEstimate(flops=flops, bytes_accessed=nbytes, transcendentals=0),
+        out_specs=[pl.BlockSpec(memory_space=pltpu.HBM if n in early else VMEM) for n in range(n_out)],
+        scratch_shapes=list(scratch) + extra,
+        compiler_params=pltpu.CompilerParams(vmem_limit_bytes=WHOLE if late else LIMIT),
+        cost_estimate=pl.CostEstimate(flops=10_000_000, bytes_accessed=nbytes, transcendentals=0),
     )(*args)
 
 
 def rows(lo, hi, unroll, body):
     n = hi - lo
-    main = n // unroll
+    main = n // unroll if unroll < n else 0
     if main > 1:
 
         def step(t, c):
@@ -69,7 +123,7 @@
         lax.fori_loop(0, main, step, 0)
         lo = lo + main * unroll
     for i in range(lo, hi):
-        body(i, (i - lo) % unroll)
+        body(i, i - lo)
 
 
 def place(info):
@@ -121,7 +175,7 @@
     return okf((g >= 0) & (g < total))
 
 
-def double_sweep(dst, b, lo, hi, s, dom, start, size, ym=None, unroll=2):
+def double_sweep(dst, b, lo, hi, s, dom, start, size, ym=None, unroll=64):
     zm = z_masks(s)
 
     def body(i, u):
@@ -135,7 +189,7 @@
     rows(lo, hi, unroll, body)
 
 
-def sweep(dst, v_ref, b, lo, hi, s, dom, start, size, ym=None, unroll=2):
+def sweep(dst, v_ref, b, lo, hi, s, dom, start, size, ym=None, unroll=64):
     zm = z_masks(s)
 
     def body(i, u):
@@ -154,10 +208,10 @@
     return t + jnp.where((lane & s) == 0, pltpu.roll(t, 128 - s, 1), pltpu.roll(t, s, 1))
 
 
-def restrict_rows(emit, v_ref, b, tmp, klo, khi, base, s, keep, ym=None, unroll=2):
+def restrict_rows(emit, v_ref, b, tmp, klo, khi, base, s, keep, ym=None, unroll=64):
     zm = z_masks(s)
 
-    def body(k, u):
+    def first(k, u):
         i = base + 2 * k
         total = None
         for d in range(2):
@@ -165,19 +219,24 @@
             r = b[i + d] - 6.0 * v + neighbours(v_ref, i + d, v, s, zm, ym)
             total = r if total is None else total + r
         tmp[u, 0 : total.shape[0], :] = total
+
+    def second(k, u):
         both = tmp[u, pl.ds(0, keep, stride=2), :] + tmp[u, pl.ds(1, keep, stride=2), :]
         emit(k, u, z_pairs(both, s) * 0.5)
 
-    rows(klo, khi, unroll, body)
-
-
-def correct(dst, v_ref, e_ref, tmp, klo, khi, base, pieces, size, dom, start, total, get=None, unroll=2):
-    def body(k, u):
+    rows(klo, khi, unroll, first)
+    rows(klo, khi, unroll, second)
+
+
+def correct(dst, v_ref, e_ref, tmp, klo, khi, base, pieces, size, dom, start, total, get=None, unroll=64):
+    def first(k, u):
         e = e_ref[k] if get is None else get(k)
         for at, count, to in pieces:
             part = e[at : at + count]
             tmp[u, pl.ds(to, count, stride=2), :] = part
             tmp[u, pl.ds(to + 1, count, stride=2), :] = part
+
+    def second(k, u):
         wide = tmp[u, 0:size, :]
         for d in range(2):
             i = base + 2 * k + d
@@ -186,7 +245,8 @@
                 out = out * dom[...]
             dst[i] = out * x_in(start, i, total)
 
-    rows(klo, khi, unroll, body)
+    rows(klo, khi, unroll, first)
+    rows(klo, khi, unroll, second)
 
 
 def split3(x):
@@ -229,19 +289,25 @@
     return jnp.where(r < split, r, r - n).astype(F32)
 
 
-def pack_gy(info, vel, pts, c_out, d_out):
-    ix, iy, px, py = place(info)
+def pack_gy(info, vel, cells, offs, c_out, d_out, pts):
+    ix, iy, px, py = place(info)
+    cells, offs = use(cells), use(offs)
+    for n in range(3):
+        for h in range(2):
+            pts[2 * n + h : 2 * n + h + 1, :] = cells[n, 0, :, 128 * h : 128 * h + 128].astype(F32)
+            pts[6 + 2 * n + h : 7 + 2 * n + h, :] = offs[n, 0, :, 128 * h : 128 * h + 128]
+
+    vel = use(vel)
 
     def body(t, u):
         c = t // W
         x = t - c * W
-        top = vel[c, x, W - 4 : W, :]
-        bottom = vel[c, x, 0:4, :]
-        to_hi, to_lo = top, bottom
+        to_hi = vel[c, x, W - 4 : W, :]
+        to_lo = vel[c, x, 0:4, :]
         c_out[t] = jnp.where(py == 0, to_hi, to_lo)
         d_out[t] = jnp.where(py == 0, to_lo, to_hi)
 
-    rows(0, 3 * W, 4, body)
+    rows(0, 3 * W, 24, body)
     for k in range(3):
         c_out[3 * W + k] = pts[4 * k : 4 * k + 4, :]
         d_out[3 * W + k] = pts[4 * k : 4 * k + 4, :]
@@ -269,7 +335,11 @@
         out[12, 36:40, :] = jnp.zeros((4, 128), F32)
 
 
-def force_kernel(info, vel, pts, sect, c_in, d_in, a_in, b_in, g_out, f_out, c_out, d_out, wide, wxs, dxs, acc):
+def force_kernel(
+    info, vel, pts, drags, blades, c_in, d_in, a_in, b_in,
+    g_out, f_out, own_out, c_out, d_out, cg_out, dg_out, pts9,
+    wide, rv, vt, dom, tmp, tmp1,
+):
     ix, iy, px, py = place(info)
     ok_hi, ok_lo = okf(iy < NGY - 1), okf(iy > 0)
     okx_hi, okx_lo = okf(ix < NGX - 1), okf(ix > 0)
@@ -282,7 +352,7 @@
         wide[c, x + 4, W : W + 4, :] = hi * ok_hi
         wide[c, x + 4, W + 4 : W + 8, :] = lo * ok_lo
 
-    rows(0, 3 * W, 2, fill)
+    rows(0, 3 * W, 24, fill)
     for c in range(3):
         for k in range(4):
             e = c * 4 + k
@@ -302,25 +372,19 @@
     wz = taps(z, cz, oz, nz)
     wz_hi, wz_lo = split3(wz)
     wz3 = jnp.concatenate([wz_hi, wz_lo, wz_hi], axis=0)
-    wxs[0:40, :] = taps(row_coord(40, -4), cx, ox, nx)
+    wx40 = taps(row_coord(40, -4), cx, ox, nx)
     wy40 = taps(cyc_coord(40, 36), cy, oy, ny)
-    for c in range(3):
-        acc[c] = jnp.zeros((40, P_), F32)
-
-    def sample(t, carry):
+    acc = [None] * 3
+    for t in range(5):
         for c in range(3):
-            part = wide[c, pl.ds(t * 8, 8)].reshape(320, 128)
+            part = wide[c, t * 8 : t * 8 + 8].reshape(320, 128)
             hi, lo = split3(part)
             r = dot(jnp.concatenate([hi, hi, lo], axis=1), wz3).reshape(8, 40, P_)
-            s = acc[c]
             for k in range(8):
-                s = s + r[k] * wxs[pl.ds(t * 8 + k, 1), :]
-            acc[c] = s
-        return carry
-
-    lax.fori_loop(0, 5, sample, 0)
+                m = r[k] * wx40[t * 8 + k : t * 8 + k + 1, :]
+                acc[c] = m if acc[c] is None else acc[c] + m
     sampled = [jnp.sum(acc[c] * wy40, axis=0, keepdims=True) for c in range(3)]
-    drag, blade = vec(sect, 0), vec(sect, 2)
+    drag, blade = drags[0], blades[0]
     slot = lax.broadcasted_iota(jnp.int32, (1, P_), 1)
     live = okf(slot < info[2])
     speed = jnp.sqrt(sampled[0] * sampled[0] + sampled[1] * sampled[1] + sampled[2] * sampled[2] + blade * blade)
@@ -342,8 +406,6 @@
     wx, dx = axis_taps(row_coord(48, -5), cx, ox, nx, start_x, float(W * NGX))
     wy, dy = axis_taps(cyc_coord(48, 40), cy, oy, ny, start_y, float(W * NGY))
     wzz, dz = axis_taps(z, cz, oz, nz, 0.0, 128.0)
-    wxs[...] = wx
-    dxs[...] = dx
     r1_hi, r1_lo = split3(-0.5 * wzz.T)
     r2_hi, r2_lo = split3(-0.5 * dz.T)
     right = jnp.concatenate([r1_hi, r2_hi, r1_lo, r2_lo, r1_hi, r2_hi], axis=0)
@@ -351,42 +413,76 @@
     fx_wy = force[0] * wy
     fz_wy = force[2] * wy
 
-    def spread(t, carry):
+    dom[...] = y_domain(48, W, 8, iy * W, W * NGY)
+    zm = z_masks(1)
+    for x in range(W):
+        vx = wide[0, x + 5, 0:W, :] - wide[0, x + 3, 0:W, :]
+        vy = wide[1, x + 4]
+        vy = pltpu.roll(vy, 39, 0)[0:W] - pltpu.roll(vy, 1, 0)[0:W]
+        vz = wide[2, x + 4, 0:W, :]
+        vz = pltpu.roll(vz, 127, 1) * zm[1] - pltpu.roll(vz, 1, 1) * zm[0]
+        rv[x] = -0.5 * (vx + vy + vz)
+
+    for t in range(6):
         l1, l2 = [], []
         for k in range(7):
             i = t * 7 + k
-            row_w = wxs[pl.ds(i, 1), :]
-            row_d = dxs[pl.ds(i, 1), :]
+            row_w = wx[i : i + 1, :]
+            row_d = dx[i : i + 1, :]
             l1.append(row_d * fx_wy + row_w * fy_dy)
             l2.append(row_w * fz_wy)
         l1_hi, l1_lo = split3(jnp.concatenate(l1, axis=0))
         l2_hi, l2_lo = split3(jnp.concatenate(l2, axis=0))
         left = jnp.concatenate([l1_hi, l2_hi, l1_hi, l2_hi, l1_lo, l2_lo], axis=1)
-        g_out[pl.ds(t * 7, 7)] = dot(left, right).reshape(7, 48, 128)
-        return carry
-
-    lax.fori_loop(0, 6, spread, 0)
-
-    zm = z_masks(1)
-
-    def rhs(x, u):
-        vx = wide[0, x + 5, 0:W, :] - wide[0, x + 3, 0:W, :]
-        vy = wide[1, x + 4]
-        vy = pltpu.roll(vy, 39, 0)[0:W] - pltpu.roll(vy, 1, 0)[0:W]
-        vz = wide[2, x + 4, 0:W, :]
-        vz = pltpu.roll(vz, 127, 1) * zm[1] - pltpu.roll(vz, 1, 1) * zm[0]
-        g_out[x + 5, 0:W, :] = g_out[x + 5, 0:W, :] - 0.5 * (vx + vy + vz)
-
-    rows(0, W, 2, rhs)
-
-    def pack(i, u):
-        g = g_out[i]
-        to_hi = g[24:40]
-        to_lo = jnp.concatenate([g[40:48], g[0:8]], axis=0)
-        c_out[i] = jnp.where(py == 0, to_hi, to_lo)
-        d_out[i] = jnp.where(py == 0, to_lo, to_hi)
-
-    rows(0, 42, 2, pack)
+        r = dot(left, right).reshape(7, 48, 128)
+        for k in range(7):
+            i = t * 7 + k
+            share = r[k] * (dom[...] * x_in(ix * W - 5, i, W * NGX))
+            if 5 <= i < W + 5:
+                g_out[i + 4, 0:W, :] = share[0:W] + rv[i - 5]
+                g_out[i + 4, W:48, :] = share[W:48]
+            else:
+                g_out[i + 4] = share
+
+    zero = jnp.zeros((48, 128), F32)
+    for i in (0, 1, 2, 3, 46, 47, 48, 49):
+        g_out[i] = zero
+    vt[0] = zero
+    vt[49] = zero
+    double_sweep(vt, g_out, 1, 49, 1, dom, ix * W - 9, W * NGX)
+
+    def emit(k, u, r):
+        tmp1[k] = r
+
+    restrict_rows(emit, vt, g_out, tmp, 0, 24, 1, 1, 24)
+    even = (lanes((24, 128)) & 1) == 0
+    for k in range(12):
+        own = jnp.where(even, tmp1[2 * k], tmp1[2 * k + 1])
+        own_out[k] = own
+        to_hi = own[4:20]
+        to_lo = jnp.concatenate([own[20:24], own[0:12]], axis=0)
+        c_out[k] = jnp.where(py == 0, to_hi, to_lo)
+        d_out[k] = jnp.where(py == 0, to_lo, to_hi)
+    for out in (c_out, d_out):
+        out[12, 0:8, :] = f_out[...]
+        out[12, 8:16, :] = jnp.zeros((8, 128), F32)
+
+    for i in range(42):
+        to_hi = g_out[i + 4, 24:40, :]
+        to_lo = jnp.concatenate([g_out[i + 4, 40:48, :], g_out[i + 4, 0:8, :]], axis=0)
+        cg_out[i] = jnp.where(py == 0, to_hi, to_lo)
+        dg_out[i] = jnp.where(py == 0, to_lo, to_hi)
+    pts9[0, 0:12, :] = pts[...]
+    for k in range(3):
+        hi, lo = hi_lo(py, c_in[3 * W + k], d_in[3 * W + k])
+        pts9[1, 4 * k : 4 * k + 4, :] = hi
+        pts9[2, 4 * k : 4 * k + 4, :] = lo
+    hi, lo = hi_lo(px, a_in[12], b_in[12])
+    for m in range(3):
+        pts9[3 + m, 0:12, :] = hi[12 * m : 12 * m + 12]
+        pts9[6 + m, 0:12, :] = lo[12 * m : 12 * m + 12]
+    for k in range(9):
+        pts9[k, 12:16, :] = jnp.zeros((4, 128), F32)
 
 
 def merge_g(info, g, c_in, d_in, h_out, a_out, b_out):
@@ -396,13 +492,13 @@
     def body(i, u):
         hi, lo = hi_lo(py, c_in[i], d_in[i])
         hi, lo = hi * ok_hi, lo * ok_lo
-        v = g[i]
+        v = g[i + 4]
         h_out[i, 0:8, :] = v[0:8] + lo[8:16]
         h_out[i, 8:24, :] = v[8:24]
         h_out[i, 24:40, :] = v[24:40] + hi
         h_out[i, 40:48, :] = v[40:48] + lo[0:8]
 
-    rows(0, 42, 2, body)
+    rows(0, 42, 42, body)
     off_a = jnp.where(px == 0, 31, 0)
     off_b = 31 - off_a
 
@@ -410,7 +506,7 @@
         a_out[k] = h_out[off_a + k]
         b_out[k] = h_out[off_b + k]
 
-    rows(0, 11, 2, pack)
+    rows(0, 11, 11, pack)
 
 
 def emit_level1(c_out, tmp1, v2, b, tmp):
@@ -424,7 +520,7 @@
         c_out[k] = jnp.where((lane & 1) == 0, tmp1[2 * k], tmp1[2 * k + 1])
 
 
-def down0(info, h, a_in, b_in, f, b_out, v_out, c_out, dom, tmp, tmp1):
+def down0(info, h, a_in, b_in, b_out, dom):
     ix, iy, px, py = place(info)
     okx_hi, okx_lo = okf(ix < NGX - 1), okf(ix > 0)
     dom[...] = y_domain(48, W, 8, iy * W, W * NGY)
@@ -433,7 +529,7 @@
     def inner(i, u):
         b_out[i] = h[i - 1] * dom[...] * x_in(start, i, W * NGX)
 
-    rows(1, 43, 2, inner)
+    rows(1, 43, 42, inner)
     zero = jnp.zeros((48, 128), F32)
     b_out[0] = zero
     b_out[43] = zero
@@ -444,13 +540,60 @@
         j = k + 33
         b_out[j] = b_out[j] + hi * dom[...] * (okx_hi * x_in(start, j, W * NGX))
 
-    rows(0, 11, 1, rim)
-    v_out[0] = zero
-    v_out[43] = zero
-    double_sweep(v_out, b_out, 1, 43, 1, dom, start, W * NGX)
-    emit_level1(c_out, tmp1, v_out, b_out, tmp)
-    c_out[8, 0:8, :] = f[...]
-    c_out[8, 8:16, :] = jnp.zeros((8, 128), F32)
+    rows(0, 11, 11, rim)
+
+
+def merge1_gx(info, own, f, c_in, d_in, s_out, a_out, b_out):
+    ix, iy, px, py = place(info)
+    ok_hi, ok_lo = okf(iy < NGY - 1), okf(iy > 0)
+    for k in range(12):
+        hi, lo = hi_lo(py, c_in[k], d_in[k])
+        hi, lo = hi * ok_hi, lo * ok_lo
+        s_out[k, 0:4, :] = own[k, 0:4, :] + lo[12:16]
+        s_out[k, 4:12, :] = own[k, 4:12, :]
+        s_out[k, 12:20, :] = own[k, 12:20, :] + hi[0:8]
+        s_out[k, 20:28, :] = hi[8:16]
+        s_out[k, 28:36, :] = jnp.zeros((8, 128), F32)
+        s_out[k, 36:44, :] = lo[0:8]
+        s_out[k, 44:48, :] = own[k, 20:24, :] + lo[8:12]
+    off_a = jnp.where(px == 0, 5, 0)
+    off_b = 5 - off_a
+    hi, lo = hi_lo(py, c_in[12], d_in[12])
+    for out, off in ((a_out, off_a), (b_out, off_b)):
+        for k in range(7):
+            out[k] = s_out[off + k]
+        out[7, 0:8, :] = f[...]
+        out[7, 8:16, :] = jnp.zeros((8, 128), F32)
+        out[7, 16:32, :] = hi
+        out[7, 32:48, :] = lo
+
+
+def down1_shares(info, shares, f, c_in, d_in, a_in, b_in, pairs, packed, f9, s_b1, s_v1, s_b2, s_v2, dom1, dom2, tmp, tmp3):
+    ix, iy, px, py = place(info)
+    okx_hi, okx_lo = okf(ix < NGX - 1), okf(ix > 0)
+    dom1[...] = y_domain(48, 16, 16, iy * 16, W * NGY // 2)
+    start1, n1x = ix * 16 - 10, W * NGX // 2
+    for p in range(18):
+        total = None
+        if 3 <= p < 15:
+            total = shares[p - 3]
+        if p < 7:
+            part = hi_lo(px, a_in[p], b_in[p])[1] * okx_lo
+            total = part if total is None else total + part
+        if p >= 11:
+            part = hi_lo(px, a_in[p - 11], b_in[p - 11])[0] * okx_hi
+            total = part if total is None else total + part
+        pairs[p] = total * (dom1[...] * x_in(start1, 2 * p, n1x))
+    levels_down(info, pairs, s_b1, s_v1, s_b2, s_v2, dom1, dom2, tmp)
+    pack3(packed, s_b2, s_v2, tmp, tmp3)
+    fhi, flo = hi_lo(py, c_in[12, 0:8, :], d_in[12, 0:8, :])
+    f9[0] = f[...]
+    f9[1] = fhi
+    f9[2] = flo
+    hi, lo = hi_lo(px, a_in[7], b_in[7])
+    for m in range(3):
+        f9[3 + m] = hi[16 * m : 16 * m + 8]
+        f9[6 + m] = lo[16 * m : 16 * m + 8]
 
 
 def pack1_gx(info, own, c_in, d_in, a_out, b_out):
@@ -459,34 +602,40 @@
     off_a = jnp.where(px == 0, 3, 0)
     off_b = 3 - off_a
     for out, off in ((a_out, off_a), (b_out, off_b)):
-        for k in range(6):
-            e = off + k if k < 5 else 8
-            hi, lo = hi_lo(py, c_in[e], d_in[e])
-            out[k, 0:16, :] = own[e]
+        for k in range(5):
+            hi, lo = hi_lo(py, c_in[off + k], d_in[off + k])
+            out[k, 0:16, :] = own[off + k]
             out[k, 16:32, :] = hi * ok_hi
             out[k, 32:48, :] = lo * ok_lo
 
 
-def down1(info, own, c_in, d_in, a_in, b_in, b1, v1, b2, v2, packed, dom1, dom2, tmp, tmp3):
+def down1(info, own, c_in, d_in, a_in, b_in, pairs, packed, s_b1, s_v1, s_b2, s_v2, dom1, dom2, tmp, tmp3):
     ix, iy, px, py = place(info)
     ok_hi, ok_lo = okf(iy < NGY - 1), okf(iy > 0)
     okx_hi, okx_lo = okf(ix < NGX - 1), okf(ix > 0)
+    for k in range(8):
+        hi, lo = hi_lo(py, c_in[k], d_in[k])
+        pairs[5 + k, 0:16, :] = own[k]
+        pairs[5 + k, 16:32, :] = hi * ok_hi
+        pairs[5 + k, 32:48, :] = lo * ok_lo
+    for k in range(5):
+        hi, lo = hi_lo(px, a_in[k], b_in[k])
+        pairs[k] = lo * okx_lo
+        pairs[13 + k] = hi * okx_hi
+    levels_down(info, pairs, s_b1, s_v1, s_b2, s_v2, dom1, dom2, tmp)
+    pack3(packed, s_b2, s_v2, tmp, tmp3)
+
+
+def levels_down(info, pairs, b1, v1, b2, v2, dom1, dom2, tmp):
+    ix, iy, px, py = place(info)
     n1x, n1y = W * NGX // 2, W * NGY // 2
     dom1[...] = y_domain(48, 16, 16, iy * 16, n1y)
     dom2[...] = y_domain(24, 8, 8, iy * 8, n1y // 2)
     even = (lanes((48, 128)) & 1) == 0
-
-    def unpack(at, p):
-        b1[at] = jnp.where(even, p, pltpu.roll(p, 1, 1))
-        b1[at + 1] = jnp.where(even, pltpu.roll(p, 127, 1), p)
-
-    for k in range(8):
-        hi, lo = hi_lo(py, c_in[k], d_in[k])
-        unpack(10 + 2 * k, jnp.concatenate([own[k], hi * ok_hi, lo * ok_lo], axis=0))
-    for k in range(5):
-        hi, lo = hi_lo(px, a_in[k], b_in[k])
-        unpack(2 * k, lo * okx_lo)
-        unpack(26 + 2 * k, hi * okx_hi)
+    for k in range(18):
+        p = pairs[k]
+        b1[2 * k] = jnp.where(even, p, pltpu.roll(p, 1, 1))
+        b1[2 * k + 1] = jnp.where(even, pltpu.roll(p, 127, 1), p)
     zero1 = jnp.zeros((48, 128), F32)
     v1[0] = zero1
     v1[35] = zero1
@@ -503,6 +652,8 @@
     v2[15] = zero2
     double_sweep(v2, b2, 1, 15, 4, dom2, start2, n1x // 2)
 
+
+def pack3(packed, b2, v2, tmp, tmp3):
     def emit3(k, u, r):
         tmp3[k] = r
 
@@ -516,7 +667,7 @@
         packed[q : q + 1, :] = jnp.sum(s, axis=0, keepdims=True)
 
 
-def coarse_up(info, g, b1, v1, b2, v2, s):
+def coarse_up(info, g, pairs, s):
     ix, iy, px, py = place(info)
     n3x = NGX * 4
 
@@ -528,7 +679,7 @@
         s.px[pl.ds(pl.multiple_of(base, 8), 8), :] = g[at, pl.ds(0, 8, stride=2), :] * ok
         s.px[pl.ds(pl.multiple_of(base + 8, 8), 8), :] = g[at, pl.ds(1, 8, stride=2), :] * ok
 
-    rows(0, 15, 1, load)
+    rows(0, 15, 15, load)
     src = lax.broadcasted_iota(jnp.int32, (128, 1024), 0)
     dst = lax.broadcasted_iota(jnp.int32, (128, 1024), 1)
     pick = okf(src == ((dst & 127) >> 3) * 8 + (dst >> 7)).astype(BF16)
@@ -543,7 +694,7 @@
                 part = s.pu[pl.ds(pl.multiple_of(d * 16 + q * 8, 8), 8), j * 128 : (j + 1) * 128]
                 s.b3[d * 4 + 2 * q + (j >> 2), pl.ds(j & 3, 8, stride=4), :] = part
 
-    rows(0, 15, 1, place3)
+    rows(0, 15, 15, place3)
     e3, e4, e5 = y_edge(32), y_edge(16), y_edge(8)
     start3, start4, start5 = (ix - 7) * 4, (ix - 7) * 2, ix - 7
     z3, z4, z5 = jnp.zeros((32, 128), F32), jnp.zeros((16, 128), F32), jnp.zeros((8, 128), F32)
@@ -571,8 +722,7 @@
     correct(s.w3, s.v3, s.v4, s.tmp, 12, 18, 0, ((0, 16, 0),), 32, None, start3, n3x)
     sweep(s.v3, s.w3, s.b3, 26, 34, 8, None, start3, n3x, e3)
 
-    s.dom2[...] = y_domain(24, 8, 8, iy * 8, NGY * 8)
-    s.dom1[...] = y_domain(48, 16, 16, iy * 16, NGY * 16)
+    levels_down(info, use(pairs), s.b1, s.v1, s.b2, s.v2, s.dom1, s.dom2, s.tmp)
     turn = lax.rem(32 - 4 * iy, 32)
 
     def shifted(k):
@@ -580,10 +730,10 @@
 
     start2, start1 = ix * 8 - 4, ix * 16 - 10
     n2x, n1x = n3x * 2, n3x * 4
-    correct(s.w2, v2, None, s.tmp, 0, 8, 0, ((0, 8, 0), (28, 4, 16)), 24, s.dom2, start2, n2x, shifted)
-    sweep(s.e2, s.w2, b2, 2, 14, 4, s.dom2, start2, n2x)
-    correct(s.w1, v1, s.e2, s.tmp, 2, 14, 2, ((0, 24, 0),), 48, s.dom1, start1, n1x)
-    sweep(s.e1, s.w1, b1, 7, 29, 2, s.dom1, start1, n1x)
+    correct(s.w2, s.v2, None, s.tmp, 0, 8, 0, ((0, 8, 0), (28, 4, 16)), 24, s.dom2, start2, n2x, shifted)
+    sweep(s.e2, s.w2, s.b2, 2, 14, 4, s.dom2, start2, n2x)
+    correct(s.w1, s.v1, s.e2, s.tmp, 2, 14, 2, ((0, 24, 0),), 48, s.dom1, start1, n1x)
+    sweep(s.e1, s.w1, s.b1, 7, 29, 2, s.dom1, start1, n1x)
 
 
 class Bag:
@@ -611,7 +761,12 @@
     ("dom0", (48, 128)),
     ("dom1", (48, 128)),
     ("dom2", (24, 128)),
-    ("tmp", (4, 48, 128)),
+    ("b1", (36, 48, 128)),
+    ("v1", (36, 48, 128)),
+    ("b2", (16, 24, 128)),
+    ("v2", (16, 24, 128)),
+    ("v0", (44, 48, 128)),
+    ("tmp", (32, 48, 128)),
     ("tmp1", (16, 16, 128)),
 )
 COARSE_SCRATCH = [pltpu.VMEM(shape, F32) for name, shape in COARSE]
@@ -627,31 +782,39 @@
 PIECES0 = ((0, 20, 0), (44, 4, 40))
 
 
-def middle(info, g, b0, v0, b1, v1, b2, v2, v_out, c_out, *scratch):
+def middle(info, g, b0, pairs, v_late, c_out, *scratch):
     s = bag(scratch)
     ix, iy, px, py = place(info)
-    coarse_up(info, g, b1, v1, b2, v2, s)
+    coarse_up(info, g, pairs, s)
     s.dom0[...] = y_domain(48, W, 8, iy * W, W * NGY)
     start, size = ix * W - 6, W * NGX
-    correct(s.w0, v0, s.e1, s.tmp, 7, 29, -14, PIECES0, 48, s.dom0, start, size)
+    b0 = use(b0)
+    zero = jnp.zeros((48, 128), F32)
+    s.v0[0] = zero
+    s.v0[43] = zero
+    double_sweep(s.v0, b0, 1, 43, 1, s.dom0, start, size)
+    correct(s.w0, s.v0, s.e1, s.tmp, 7, 29, -14, PIECES0, 48, s.dom0, start, size)
     sweep(s.x0, s.w0, b0, 2, 42, 1, s.dom0, start, size)
     sweep(s.w0, s.x0, b0, 3, 41, 1, s.dom0, start, size)
+    v_out = v_late.ref
     sweep(v_out, s.w0, b0, 4, 40, 1, s.dom0, start, size)
-    zero = jnp.zeros((48, 128), F32)
     for i in (0, 1, 2, 3, 40, 41, 42, 43):
         v_out[i] = zero
+    v_late.flush()
     emit_level1(c_out, s.tmp1, v_out, b0, s.tmp)
 
 
-def final(info, g, b0, v0, b1, v1, b2, v2, pushed, vel_out, p_out, *scratch):
+def final(info, g, b0, v0, pairs, pushed, vel_out, p_out, *scratch):
     s = bag(scratch)
     ix, iy, px, py = place(info)
-    coarse_up(info, g, b1, v1, b2, v2, s)
+    coarse_up(info, g, pairs, s)
     s.dom0[...] = y_domain(48, W, 8, iy * W, W * NGY)
     start, size = ix * W - 6, W * NGX
+    b0, v0 = use(b0), use(v0)
     correct(s.w0, v0, s.e1, s.tmp, 9, 27, -14, PIECES0, 48, s.dom0, start, size)
     sweep(s.x0, s.w0, b0, 5, 39, 1, s.dom0, start, size)
     zm = z_masks(1)
+    pushed = use(pushed)
 
     def body(x, u):
         p = s.x0[x + 6]
@@ -664,41 +827,22 @@
         vel_out[1, x] = pushed[1, x] - 0.5 * gy
         vel_out[2, x] = pushed[2, x] - 0.5 * gz
 
-    rows(0, W, 2, body)
-
-
-def push_kernel(info, vel, pts, f, c_in, d_in, a_in, b_in, c1, d1, a1, b1, out, wxs, pbuf):
+    rows(0, W, 32, body)
+
+
+def push_kernel(info, vel, pts9, f9, out):
     ix, iy, px, py = place(info)
     ok = {-1: (okf(ix > 0), okf(iy > 0)), 0: (1.0, 1.0), 1: (okf(ix < NGX - 1), okf(iy < NGY - 1))}
     start_x = (ix * W).astype(F32)
     start_y = (iy * W).astype(F32)
-
-    def store(slot, points, forces):
-        pbuf[slot, 0:12, :] = points
-        pbuf[slot, 12:18, :] = forces
-
-    def cat3(ref):
-        return jnp.concatenate([ref[3 * W], ref[3 * W + 1], ref[3 * W + 2]], axis=0)
-
-    hi, lo = hi_lo(py, cat3(c_in), cat3(d_in))
-    fhi, flo = hi_lo(py, c1[8, 0:6, :], d1[8, 0:6, :])
-    store(0, pts[...], f[0:6, :])
-    store(1, hi, fhi)
-    store(2, lo, flo)
-    xhi, xlo = hi_lo(px, a_in[12], b_in[12])
-    ghi, glo = hi_lo(px, a1[5], b1[5])
-    for n, (q, fq) in enumerate(((xhi, ghi), (xlo, glo))):
-        for m in range(3):
-            store(3 + 3 * n + m, q[12 * m : 12 * m + 12], fq[16 * m : 16 * m + 6])
-
     order = ((0, 0), (0, 1), (0, -1), (1, 0), (1, 1), (1, -1), (-1, 0), (-1, 1), (-1, -1))
     for slot, (ox_, oy_) in enumerate(order):
-        q = pbuf.at[slot]
+        q, fq = pts9.at[slot], f9.at[slot]
         cx, cy, cz = vec(q, 0) - start_x, vec(q, 2) - start_y, vec(q, 4)
         ox, oy, oz = vec(q, 6), vec(q, 8), vec(q, 10)
         keep = ok[ox_][0] * ok[oy_][1]
-        force = [vec(q, 12 + 2 * c) * keep for c in range(3)]
-        wxs[...] = taps(row_coord(32, 0), cx, ox, tap_norm(ox))
+        force = [vec(fq, 2 * c) * keep for c in range(3)]
+        wx = taps(row_coord(32, 0), cx, ox, tap_norm(ox))
         y0, yn = {0: (0, 32), 1: (24, 8), -1: (0, 8)}[oy_]
         wy = taps(row_coord(yn, y0), cy, oy, tap_norm(oy))
         wz = taps(row_coord(128, 0), cz, oz, tap_norm(oz)).T
@@ -708,11 +852,11 @@
         x0, xn = {0: (0, 32), 1: (28, 4), -1: (0, 4)}[ox_]
         step = min(xn, 4 if oy_ == 0 else 16)
 
-        def spread(t, carry, x0=x0, step=step, fy=fy, right=right, y0=y0, yn=yn, slot=slot):
+        def spread(t, x0=x0, step=step, fy=fy, right=right, y0=y0, yn=yn, slot=slot, wx=wx):
             at = x0 + t * step
             left = []
             for k in range(step):
-                row = wxs[pl.ds(at + k, 1), :]
+                row = wx[at + k : at + k + 1, :]
                 left += [row * fy[c] for c in range(3)]
             hi, lo = split3(jnp.concatenate(left, axis=0))
             r = dot(jnp.concatenate([hi, hi, lo], axis=1), right).reshape(step, 3, yn, 128)
@@ -720,9 +864,9 @@
                 for c in range(3):
                     base = vel if slot == 0 else out
                     out[c, at + k, y0 : y0 + yn, :] = base[c, at + k, y0 : y0 + yn, :] + r[k, c]
-            return carry
-
-        lax.fori_loop(0, xn // step, spread, 0)
+
+        for t in range(xn // step):
+            spread(t)
 
 
 def gather3(packed):
@@ -730,55 +874,53 @@
     return lax.all_to_all(everyone, AXES, 0, 0, tiled=True).reshape(NGX, 16, 128)
 
 
-def level_one(info, own):
-    c1, d1 = swap_gy(own, own)
-    a1, b1 = call(pack1_gx, [(6, 48, 128)] * 2, [], info, own, c1, d1)
-    a1, b1 = swap_gx(a1, b1)
-    outs = call(
-        down1,
-        [(36, 48, 128), (36, 48, 128), (16, 24, 128), (16, 24, 128), (2, 128)],
-        [VMEM((48, 128), F32), VMEM((24, 128), F32), VMEM((4, 48, 128), F32), VMEM((4, 8, 128), F32)],
-        info, own, c1, d1, a1, b1,
-    )
-    return (c1, d1, a1, b1), outs[:4], gather3(outs[4])
+LEVELS12 = [(18, 48, 128), (2, 128)]
+DOWN1 = [
+    VMEM((36, 48, 128), F32), VMEM((36, 48, 128), F32), VMEM((16, 24, 128), F32), VMEM((16, 24, 128), F32),
+    VMEM((48, 128), F32), VMEM((24, 128), F32), VMEM((32, 48, 128), F32), VMEM((4, 8, 128), F32),
+]
 
 
 def per_device(velocity, point_cells, point_offsets, point_count, drag, blade_speed):
     info = jnp.stack([lax.axis_index("gx"), lax.axis_index("gy"), point_count.reshape(())]).astype(jnp.int32)
-    pts = jnp.concatenate([point_cells.astype(F32).reshape(6, 128), point_offsets.reshape(6, 128)], axis=0)
-    sect = jnp.concatenate([drag.reshape(2, 128), blade_speed.reshape(2, 128)], axis=0)
-
-    c0, d0 = call(pack_gy, [(99, 4, 128)] * 2, [], info, velocity, pts)
+
+    c0, d0, pts = call(
+        pack_gy, [(99, 4, 128)] * 2 + [(12, 128)], [], info, velocity, point_cells, point_offsets
+    )
     c0, d0 = swap_gy(c0, d0)
     a0, b0 = call(pack_gx, [(13, 40, 128)] * 2, [], info, velocity, pts, c0, d0)
     a0, b0 = swap_gx(a0, b0)
-    g, f, cg, dg = call(
+    g, f, own1, c1, d1, cg, dg, pts9 = call(
         force_kernel,
-        [(42, 48, 128), (8, 128), (42, 16, 128), (42, 16, 128)],
-        [VMEM((3, 40, 40, 128), F32), VMEM((48, P_), F32), VMEM((48, P_), F32), VMEM((3, 40, P_), F32)],
-        info, velocity, pts, sect, c0, d0, a0, b0,
+        [(50, 48, 128), (8, 128), (12, 24, 128), (13, 16, 128), (13, 16, 128), (42, 16, 128), (42, 16, 128), (9, 16, 128)],
+        [
+            VMEM((3, 40, 40, 128), F32), VMEM((W, W, 128), F32), VMEM((50, 48, 128), F32), VMEM((48, 128), F32),
+            VMEM((32, 48, 128), F32), VMEM((24, 24, 128), F32),
+        ],
+        info, velocity, pts, drag, blade_speed, c0, d0, a0, b0,
     )
+    c1, d1 = swap_gy(c1, d1)
+    shares, a1, b1 = call(merge1_gx, [(12, 48, 128), (8, 48, 128), (8, 48, 128)], [], info, own1, f, c1, d1)
+    a1, b1 = swap_gx(a1, b1)
+    pairs, packed, f9 = call(down1_shares, LEVELS12 + [(9, 8, 128)], DOWN1, info, shares, f, c1, d1, a1, b1)
+    packed, g, cg, dg = lax.optimization_barrier((packed, g, cg, dg))
+    gathered = gather3(packed)
     cg, dg = swap_gy(cg, dg)
     h, ag, bg = call(merge_g, [(42, 48, 128), (11, 48, 128), (11, 48, 128)], [], info, g, cg, dg)
     ag, bg = swap_gx(ag, bg)
-    rhs, v0, own1 = call(
-        down0,
-        [(44, 48, 128), (44, 48, 128), (9, 16, 128)],
-        [VMEM((48, 128), F32), VMEM((4, 48, 128), F32), VMEM((16, 16, 128), F32)],
-        info, h, ag, bg, f,
+    (rhs,) = call(down0, [(44, 48, 128)], [VMEM((48, 128), F32)], info, h, ag, bg)
+    v0, own1 = call(
+        middle, [(44, 48, 128), (8, 16, 128)], COARSE_SCRATCH, info, gathered, rhs, pairs, late=(2, 3), early=(0,)
     )
-    (c1, d1, a1, b1), levels, gathered = level_one(info, own1)
-    (pushed,) = call(
-        push_kernel,
-        [(3, W, W, 128)],
-        [VMEM((32, P_), F32), VMEM((9, 24, 128), F32)],
-        info, velocity, pts, f, c0, d0, a0, b0, c1, d1, a1, b1,
-    )
-    v0, own1 = call(middle, [(44, 48, 128), (8, 16, 128)], COARSE_SCRATCH, info, gathered, rhs, v0, *levels)
-    own1 = jnp.concatenate([own1, jnp.zeros((1, 16, 128), F32)], axis=0)
-    unused, levels, gathered = level_one(info, own1)
+    c1, d1 = swap_gy(own1, own1)
+    a1, b1 = call(pack1_gx, [(5, 48, 128)] * 2, [], info, own1, c1, d1)
+    a1, b1 = swap_gx(a1, b1)
+    pairs, packed = call(down1, LEVELS12, DOWN1, info, own1, c1, d1, a1, b1)
+    packed, pts9 = lax.optimization_barrier((packed, pts9))
+    gathered = gather3(packed)
+    (pushed,) = call(push_kernel, [(3, W, W, 128)], [], info, velocity, pts9, f9)
     vel_out, p_out = call(
-        final, [(3, W, W, 128), (W, W, 128)], COARSE_SCRATCH, info, gathered, rhs, v0, *levels, pushed
+        final, [(3, W, W, 128), (W, W, 128)], COARSE_SCRATCH, info, gathered, rhs, v0, pairs, pushed, late=(2, 3, 4, 5)
     )
     return vel_out, p_out
 

time: 198 us -> 144 us (0.73)
  Pallas kernels: 71.4 us -> 37.3 us
  blocking collectives: 26.4 us -> 0 us
  local copies, waits for them, and re-layouts: 21.3 us -> 11.7 us
  starting transfers between devices: 39.5 us -> 48.4 us
  waiting for transfers between devices: 35.6 us -> 44 us
    pallas_call x12, Pallas kernels: 71.4 us -> 37.3 us  [call(): pl.pallas_call(body, out_shape=[jax.ShapeDtypeStruct(s, F32) for s in out...]
    all_to_all x1 -> x0, blocking collectives: 26.4 us -> none  [gather3(): lax.all_to_all(everyone, AXES, 0, 0, tiled=True).reshape(NGX, 16, 128)]
    all_to_all x1 -> x2, starting transfers between devices: 9.98 us -> 21.6 us  [gather3(): lax.all_to_all(everyone, AXES, 0, 0, tiled=True).reshape(NGX, 16, 128)]
    all_to_all x1 -> x2, waiting for transfers between devices: 1.2 us -> 12.5 us  [gather3(): lax.all_to_all(everyone, AXES, 0, 0, tiled=True).reshape(NGX, 16, 128)]
    unnamed x70 -> x30, local copies, waits for them, and re-layouts: 20.5 us -> 10.1 us
    ppermute x16, waiting for transfers between devices: 34.4 us -> 31.6 us  [swap(): return lax.ppermute(x, AXES, perm)]
    ppermute x16, starting transfers between devices: 29.5 us -> 26.8 us  [swap(): return lax.ppermute(x, AXES, perm)]
  transfers between devices with their start and end apart: 17 -> 18, of which waited for: 14 -> 13; matrix products, arithmetic and copies ran while one was open for 0% -> 1% of each run, Pallas kernels for 3% -> 4%
where the time goes in v1:
time: 144 us; the launch traced here: 143 us
  starting transfers between devices  48.4 us (34%)
  waiting for transfers between devices  44 us (31%)
  Pallas kernels  37.3 us (26%)
  local copies, waits for them, and re-layouts  11.7 us (8%)
  between operations  1.65 us (1%)
    pallas_call x12, Pallas kernels, call(): pl.pallas_call(body, out_shape=[jax.ShapeDtypeStruct(s, F32) for s in out...  37.3 us
    ppermute x16, waiting for transfers between devices, swap(): return lax.ppermute(x, AXES, perm)  31.6 us
    ppermute x16, starting transfers between devices, swap(): return lax.ppermute(x, AXES, perm)  26.8 us
    all_to_all x2, starting transfers between devices, gather3(): lax.all_to_all(everyone, AXES, 0, 0, tiled=True).reshape(NGX, 16, 128)  21.6 us
    all_to_all x2, waiting for transfers between devices, gather3(): lax.all_to_all(everyone, AXES, 0, 0, tiled=True).reshape(NGX, 16, 128)  12.5 us
    unnamed x30, local copies, waits for them, and re-layouts  10.1 us
  transfers between devices with their start and end apart: 18, of which 13 were waited for; matrix products, arithmetic and copies ran while one was open for 1% of the time, Pallas kernels for 4%

profile of v1, /device:TPU:1, one launch (start us, length us, event | category | flops | bytes accessed | tf_op | source)
XLA Modules:
  0.0 143.2 jit_solution(9289173560647137441)
XLA Ops:
  1.4 1.4 copy-done
  2.8 0.7 copy-done.9
  3.5 0.7 copy-done.10
  4.1 1.2 shard_map.77
  5.3 2.6 %collective-permute-start = (f32[99,4,128]{2,1,0:T(4,128)S(1)}, f32[99,4,128]{2,1,0:T(4,128)S(1)}, u32[]{:S(2)}, u32[]{:S(2)}) collective-permute-start(f32[99,4,128]{2,1,0:T(4,128)S(1)} %get-tuple-element.37), channel_id=1, source_target_pairs={{0,1},{1,0},{2,3},{3,2},{4,5},{5,4},{6,7},{7,6},{8,9},{9,8},{10,11... | collective-permute-start | bytes 608264 | tf_op jit(solution)/shard_map/ppermute | solution.py:23
  7.9 4.7 %collective-permute-start.1 = (f32[99,4,128]{2,1,0:T(4,128)S(1)}, f32[99,4,128]{2,1,0:T(4,128)S(1)}, u32[]{:S(2)}, u32[]{:S(2)}) collective-permute-start(f32[99,4,128]{2,1,0:T(4,128)S(1)} %get-tuple-element.38), channel_id=1, source_target_pairs={{0,7},{1,2},{2,1},{3,4},{4,3},{5,6},{6,5},{7,0},{8,15},{9,10},{10,... | collective-permute-start | bytes 608264 | tf_op jit(solution)/shard_map/ppermute | solution.py:23
  12.5 4.4 %collective-permute-done.1.refs_4_.refs_6_ = f32[99,4,128]{2,1,0:T(4,128)S(1)} collective-permute-done((f32[99,4,128]{2,1,0:T(4,128)S(1)}, f32[99,4,128]{2,1,0:T(4,128)S(1)}, u32[]{:S(2)}, u32[]{:S(2)}) %collective-permute-start.1) | collective-permute-done | bytes 202784 | tf_op jit(solution)/shard_map/ppermute | solution.py:23
  17.6 1.6 %collective-permute-start.2 = (f32[13,40,128]{2,1,0:T(8,128)S(1)}, f32[13,40,128]{2,1,0:T(8,128)S(1)}, u32[]{:S(2)}, u32[]{:S(2)}) collective-permute-start(f32[13,40,128]{2,1,0:T(8,128)S(1)} %get-tuple-element.39), channel_id=1, source_target_pairs={{0,8},{1,9},{2,10},{3,11},{4,12},{5,13},{6,14},{7,15},{8,0},{9,1},... | collective-permute-start | bytes 798728 | tf_op jit(solution)/shard_map/ppermute | solution.py:23
  19.2 1.3 collective-permute-start.3
  20.5 4.6 %collective-permute-done.3.refs_8_ = f32[13,40,128]{2,1,0:T(8,128)S(1)} collective-permute-done((f32[13,40,128]{2,1,0:T(8,128)S(1)}, f32[13,40,128]{2,1,0:T(8,128)S(1)}, u32[]{:S(2)}, u32[]{:S(2)}) %collective-permute-start.3) | collective-permute-done | bytes 266272 | tf_op jit(solution)/shard_map/ppermute | solution.py:23
  25.0 6.0 %shard_map.79 = (f32[50,48,128]{2,1,0:T(8,128)S(1)}, f32[8,128]{1,0:T(8,128)S(1)}, f32[12,24,128]{2,1,0:T(8,128)S(1)}, f32[13,16,128]{2,1,0:T(8,128)S(1)}, f32[1...) custom-call(s32[3]{0:T(128)S(1)} %pad_add_fusion.refs_0_, ...), custom_call_target="tpu_custom_call" | custom-call | flops 10000000 | bytes 4874252 | tf_op jit(solution)/shard_map/pallas_call | solution.py:102
  31.1 2.8 %collective-permute-start.5 = (f32[13,16,128]{2,1,0:T(8,128)S(1)}, f32[13,16,128]{2,1,0:T(8,128)S(1)}, u32[]{:S(2)}, u32[]{:S(2)}) collective-permute-start(f32[13,16,128]{2,1,0:T(8,128)S(1)} %get-tuple-element.44), channel_id=1, source_target_pairs={{0,7},{1,2},{2,1},{3,4},{4,3},{5,6},{6,5},{7,0},{8,15},{9,10},{10,... | collective-permute-start | bytes 319496 | tf_op jit(solution)/shard_map/ppermute | solution.py:23
  33.9 0.8 collective-permute-done.4.refs_3_
  34.7 1.3 collective-permute-done.5.refs_4_
  36.0 0.6 shard_map.80
  36.6 4.8 %collective-permute-start.6 = (f32[8,48,128]{2,1,0:T(8,128)S(1)}, f32[8,48,128]{2,1,0:T(8,128)S(1)}, u32[]{:S(2)}, u32[]{:S(2)}) collective-permute-start(f32[8,48,128]{2,1,0:T(8,128)S(1)} %get-tuple-element.46), channel_id=1, source_target_pairs={{0,8},{1,9},{2,10},{3,11},{4,12},{5,13},{6,14},{7,15},{8,0},{9,1},... | collective-permute-start | bytes 589832 | tf_op jit(solution)/shard_map/ppermute | solution.py:23
  41.4 1.1 collective-permute-done.6.refs_5_
  42.5 4.0 %collective-permute-done.7.refs_6_ = f32[8,48,128]{2,1,0:T(8,128)S(1)} collective-permute-done((f32[8,48,128]{2,1,0:T(8,128)S(1)}, f32[8,48,128]{2,1,0:T(8,128)S(1)}, u32[]{:S(2)}, u32[]{:S(2)}) %collective-permute-start.7) | collective-permute-done | bytes 196640 | tf_op jit(solution)/shard_map/ppermute | solution.py:23
  46.5 2.0 %shard_map.81 = (f32[18,48,128]{2,1,0:T(8,128)S(1)}, f32[2,128]{1,0:T(2,128)S(1)}, f32[9,8,128]{2,1,0:T(8,128)S(1)}) custom-call(s32[3]{0:T(128)S(1)} %pad_add_fusion.refs_0_, f32[12,48,128]{2,1,0:T(8,128)S(1)} %get-tuple-element.45.refs_1_, f32[8,128]{1,0:T(8,128)S(1)} %get-tuple-element.42.refs_2_, f32[13,16,128]{2,1,0:T(8,128)S(1)} %collective-permute-done.4.refs_3_, ...), custom_call_target="tpu_custom_call" | custom-call | flops 10000000 | bytes 1385484 | tf_op jit(solution)/shard_map/pallas_call | solution.py:102
  48.6 0.8 copy-done.5
  49.8 2.7 %collective-permute-start.9 = (f32[42,16,128]{2,1,0:T(8,128)S(1)}, f32[42,16,128]{2,1,0:T(8,128)S(1)}, u32[]{:S(2)}, u32[]{:S(2)}) collective-permute-start(f32[42,16,128]{2,1,0:T(8,128)S(1)} %get-tuple-element.55), channel_id=1, source_target_pairs={{0,7},{1,2},{2,1},{3,4},{4,3},{5,6},{6,5},{7,0},{8,15},{9,10},{10,... | collective-permute-start | bytes 1032200 | tf_op jit(solution)/shard_map/ppermute | solution.py:23
  52.4 0.8 broadcast_in_dim.4
  53.2 10.9 %all-to-all-start = ((f32[256,2,128]{2,1,0:T(2,128)}), f32[256,2,128]{2,1,0:T(2,128)S(1)}, u32[]{:S(2)}, u32[]{:S(2)}) async-start(f32[256,2,128]{2,1,0:T(2,128)} %broadcast_in_dim.4), calls=%async_computation | async-start | bytes 524288 | tf_op jit(solution)/shard_map/all_to_all | solution.py:874
  64.1 0.7 shard_map.82
  64.8 2.2 %collective-permute-start.10 = (f32[11,48,128]{2,1,0:T(8,128)S(1)}, f32[11,48,128]{2,1,0:T(8,128)S(1)}, u32[]{:S(2)}, u32[]{:S(2)}) collective-permute-start(f32[11,48,128]{2,1,0:T(8,128)S(1)} %get-tuple-element.57), channel_id=1, source_target_pairs={{0,8},{1,9},{2,10},{3,11},{4,12},{5,13},{6,14},{7,15},{8,0},{9,1},... | collective-permute-start | bytes 811016 | tf_op jit(solution)/shard_map/ppermute | solution.py:23
  67.0 1.2 collective-permute-done.10.refs_2_
  68.2 6.5 %collective-permute-done.11.refs_3_ = f32[11,48,128]{2,1,0:T(8,128)S(1)} collective-permute-done((f32[11,48,128]{2,1,0:T(8,128)S(1)}, f32[11,48,128]{2,1,0:T(8,128)S(1)}, u32[]{:S(2)}, u32[]{:S(2)}) %collective-permute-start.11) | collective-permute-done | bytes 270368 | tf_op jit(solution)/shard_map/ppermute | solution.py:23
  74.7 0.7 shard_map.83.refs_2_
  75.4 1.0 copy-done.2
  76.4 3.2 %all-to-all-done = f32[256,2,128]{2,1,0:T(2,128)S(1)} async-done(((f32[256,2,128]{2,1,0:T(2,128)}), f32[256,2,128]{2,1,0:T(2,128)S(1)}, u32[]{:S(2)}, u32[]{:S(2)}) %all-to-all-start) | async-done | bytes 262176 | tf_op jit(solution)/shard_map/all_to_all | solution.py:874
  79.6 0.7 copy-done.14
  80.3 10.5 %shard_map.84 = (f32[44,48,128]{2,1,0:T(8,128)}, f32[8,16,128]{2,1,0:T(8,128)}) custom-call(s32[3]{0:T(128)} %copy-done.7, f32[32,16,128]{2,1,0:T(8,128)} %bitcast.7, f32[44,48,128]{2,1,0:T(8,128)} %copy-done.2, f32[18,48,128]{2,1,0:T(8,128)} %copy-done.5), custom_call_target="tpu_custom_call" | custom-call | flops 10000000 | bytes 2932748 | tf_op jit(solution)/shard_map/pallas_call | solution.py:102
  91.2 0.9 collective-permute-start.12
  92.0 3.4 %collective-permute-done.13.refs_3_ = f32[8,16,128]{2,1,0:T(8,128)S(1)} collective-permute-done((f32[8,16,128]{2,1,0:T(8,128)}, f32[8,16,128]{2,1,0:T(8,128)S(1)}, u32[]{:S(2)}, u32[]{:S(2)}) %collective-permute-start.13) | collective-permute-done | bytes 65568 | tf_op jit(solution)/shard_map/ppermute | solution.py:23
  95.5 0.8 copy-done.6
  96.9 2.4 %collective-permute-start.14 = (f32[5,48,128]{2,1,0:T(8,128)S(1)}, f32[5,48,128]{2,1,0:T(8,128)S(1)}, u32[]{:S(2)}, u32[]{:S(2)}) collective-permute-start(f32[5,48,128]{2,1,0:T(8,128)S(1)} %get-tuple-element.61), channel_id=1, source_target_pairs={{0,8},{1,9},{2,10},{3,11},{4,12},{5,13},{6,14},{7,15},{8,0},{9,1},... | collective-permute-start | bytes 368648 | tf_op jit(solution)/shard_map/ppermute | solution.py:23
  99.3 1.0 collective-permute-done.14.refs_4_
  100.3 3.3 %collective-permute-done.15.refs_5_ = f32[5,48,128]{2,1,0:T(8,128)S(1)} collective-permute-done((f32[5,48,128]{2,1,0:T(8,128)S(1)}, f32[5,48,128]{2,1,0:T(8,128)S(1)}, u32[]{:S(2)}, u32[]{:S(2)}) %collective-permute-start.15) | collective-permute-done | bytes 122912 | tf_op jit(solution)/shard_map/ppermute | solution.py:23
  103.6 2.0 %shard_map.86 = (f32[18,48,128]{2,1,0:T(8,128)S(1)}, f32[2,128]{1,0:T(2,128)S(1)}) custom-call(s32[3]{0:T(128)S(1)} %copy-done.8, f32[8,16,128]{2,1,0:T(8,128)S(1)} %copy-done.6, f32[8,16,128]{2,1,0:T(8,128)S(1)} %collective-permute-done.12.refs_2_, f32[8,16,128]{2,1,0:T(8,128)S(1)} %collective-permute-done.13.refs_3_, ...), custom_call_target="tpu_custom_call" | custom-call | flops 10000000 | bytes 885772 | tf_op jit(solution)/shard_map/pallas_call | solution.py:102
  105.6 0.8 copy-done.4
  106.4 0.8 broadcast_in_dim.5
  107.2 10.8 %all-to-all-start.1 = ((f32[256,2,128]{2,1,0:T(2,128)}), f32[256,2,128]{2,1,0:T(2,128)S(1)}, u32[]{:S(2)}, u32[]{:S(2)}) async-start(f32[256,2,128]{2,1,0:T(2,128)} %broadcast_in_dim.5), calls=%async_computation.1 | async-start | bytes 524288 | tf_op jit(solution)/shard_map/all_to_all | solution.py:874
  118.0 1.4 copy-done.1
  119.4 3.7 %shard_map.87.refs_5_ = f32[3,32,32,128]{3,2,1,0:T(8,128)S(1)} custom-call(s32[3]{0:T(128)S(1)} %copy-done.8, f32[3,32,32,128]{3,2,1,0:T(8,128)S(1)} %copy-done.1, f32[9,16,128]{2,1,0:T(8,128)S(1)} %get-tuple-element.68.refs_2_, f32[9,8,128]{2,1,0:T(8,128)S(1)} %get-tuple-element.69.refs_3_), custom_call_target="tpu_custom_call" | custom-call | flops 10000000 | bytes 3256332 | tf_op jit(solution)/shard_map/pallas_call | solution.py:102
  123.1 1.2 copy-done.3
  124.3 9.2 %all-to-all-done.1 = f32[256,2,128]{2,1,0:T(2,128)S(1)} async-done(((f32[256,2,128]{2,1,0:T(2,128)}), f32[256,2,128]{2,1,0:T(2,128)S(1)}, u32[]{:S(2)}, u32[]{:S(2)}) %all-to-all-start.1) | async-done | bytes 262176 | tf_op jit(solution)/shard_map/all_to_all | solution.py:874
  133.5 0.7 copy-done.13
  134.2 8.7 %shard_map.88 = (f32[3,32,32,128]{3,2,1,0:T(8,128)}, f32[32,32,128]{2,1,0:T(8,128)}) custom-call(s32[3]{0:T(128)} %copy-done.7, f32[32,16,128]{2,1,0:T(8,128)} %bitcast.6, f32[44,48,128]{2,1,0:T(8,128)} %copy-done.2, f32[44,48,128]{2,1,0:T(8,128)} %get-tuple-element.66.refs_3_, f32[18,48,128]{2,1,0:T(8,128)} %copy-done.4, f32[3,32,32,128]{3,2,1,0:T(8,128)} %copy-done.3), custom_call_target="tpu_custom_call" | custom-call | flops 10000000 | bytes 6537228 | tf_op jit(solution)/shard_map/pallas_call | solution.py:102
  (33 shorter events, 2.2 us)
Async XLA Ops:
  1.4 1.4 copy-start
  2.8 0.7 copy-start.9
  3.5 0.7 copy-start.10
  4.1 70.6 %copy-start.7 = (s32[3]{0:T(128)}, s32[3]{0:T(128)S(1)}, u32[]{:S(2)}) copy-start(s32[3]{0:T(128)S(1)} %pad_add_fusion.refs_0_) | copy-start | bytes 40
  4.1 20.9 %copy-start.11 = (f32[1,1,256]{2,1,0:T(1,128)S(1)}, f32[1,1,256]{2,1,0:T(1,128)}, u32[]{:S(2)}) copy-start(f32[1,1,256]{2,1,0:T(1,128)} %refs_3_.3) | copy-start | bytes 3076
  4.1 20.9 %copy-start.12 = (f32[1,1,256]{2,1,0:T(1,128)S(1)}, f32[1,1,256]{2,1,0:T(1,128)}, u32[]{:S(2)}) copy-start(f32[1,1,256]{2,1,0:T(1,128)} %refs_4_.1) | copy-start | bytes 3076
  5.3 7.2 %collective-permute-start = (f32[99,4,128]{2,1,0:T(4,128)S(1)}, f32[99,4,128]{2,1,0:T(4,128)S(1)}, u32[]{:S(2)}, u32[]{:S(2)}) collective-permute-start(f32[99,4,128]{2,1,0:T(4,128)S(1)} %get-tuple-element.37), channel_id=1, source_target_pairs={{0,1},{1,0},{2,3},{3,2},{4,5},{5,4},{6,7},{7,6},{8,9},{9,8},{10,11... | collective-permute-start | bytes 608264 | tf_op jit(solution)/shard_map/ppermute | solution.py:23
  7.9 9.1 %collective-permute-start.1 = (f32[99,4,128]{2,1,0:T(4,128)S(1)}, f32[99,4,128]{2,1,0:T(4,128)S(1)}, u32[]{:S(2)}, u32[]{:S(2)}) collective-permute-start(f32[99,4,128]{2,1,0:T(4,128)S(1)} %get-tuple-element.38), channel_id=1, source_target_pairs={{0,7},{1,2},{2,1},{3,4},{4,3},{5,6},{6,5},{7,0},{8,15},{9,10},{10,... | collective-permute-start | bytes 608264 | tf_op jit(solution)/shard_map/ppermute | solution.py:23
  17.6 2.9 %collective-permute-start.2 = (f32[13,40,128]{2,1,0:T(8,128)S(1)}, f32[13,40,128]{2,1,0:T(8,128)S(1)}, u32[]{:S(2)}, u32[]{:S(2)}) collective-permute-start(f32[13,40,128]{2,1,0:T(8,128)S(1)} %get-tuple-element.39), channel_id=1, source_target_pairs={{0,8},{1,9},{2,10},{3,11},{4,12},{5,13},{6,14},{7,15},{8,0},{9,1},... | collective-permute-start | bytes 798728 | tf_op jit(solution)/shard_map/ppermute | solution.py:23
  19.2 5.8 %collective-permute-start.3 = (f32[13,40,128]{2,1,0:T(8,128)S(1)}, f32[13,40,128]{2,1,0:T(8,128)S(1)}, u32[]{:S(2)}, u32[]{:S(2)}) collective-permute-start(f32[13,40,128]{2,1,0:T(8,128)S(1)} %get-tuple-element.40), channel_id=1, source_target_pairs={{0,248},{1,249},{2,250},{3,251},{4,252},{5,253},{6,254},{7,255},{8... | collective-permute-start | bytes 798728 | tf_op jit(solution)/shard_map/ppermute | solution.py:23
  31.0 3.6 %collective-permute-start.4 = (f32[13,16,128]{2,1,0:T(8,128)S(1)}, f32[13,16,128]{2,1,0:T(8,128)S(1)}, u32[]{:S(2)}, u32[]{:S(2)}) collective-permute-start(f32[13,16,128]{2,1,0:T(8,128)S(1)} %get-tuple-element.43), channel_id=1, source_target_pairs={{0,1},{1,0},{2,3},{3,2},{4,5},{5,4},{6,7},{7,6},{8,9},{9,8},{10,11... | collective-permute-start | bytes 319496 | tf_op jit(solution)/shard_map/ppermute | solution.py:23
  31.1 4.9 %collective-permute-start.5 = (f32[13,16,128]{2,1,0:T(8,128)S(1)}, f32[13,16,128]{2,1,0:T(8,128)S(1)}, u32[]{:S(2)}, u32[]{:S(2)}) collective-permute-start(f32[13,16,128]{2,1,0:T(8,128)S(1)} %get-tuple-element.44), channel_id=1, source_target_pairs={{0,7},{1,2},{2,1},{3,4},{4,3},{5,6},{6,5},{7,0},{8,15},{9,10},{10,... | collective-permute-start | bytes 319496 | tf_op jit(solution)/shard_map/ppermute | solution.py:23
  36.6 5.9 %collective-permute-start.6 = (f32[8,48,128]{2,1,0:T(8,128)S(1)}, f32[8,48,128]{2,1,0:T(8,128)S(1)}, u32[]{:S(2)}, u32[]{:S(2)}) collective-permute-start(f32[8,48,128]{2,1,0:T(8,128)S(1)} %get-tuple-element.46), channel_id=1, source_target_pairs={{0,8},{1,9},{2,10},{3,11},{4,12},{5,13},{6,14},{7,15},{8,0},{9,1},... | collective-permute-start | bytes 589832 | tf_op jit(solution)/shard_map/ppermute | solution.py:23
  41.4 5.1 %collective-permute-start.7 = (f32[8,48,128]{2,1,0:T(8,128)S(1)}, f32[8,48,128]{2,1,0:T(8,128)S(1)}, u32[]{:S(2)}, u32[]{:S(2)}) collective-permute-start(f32[8,48,128]{2,1,0:T(8,128)S(1)} %get-tuple-element.47), channel_id=1, source_target_pairs={{0,248},{1,249},{2,250},{3,251},{4,252},{5,253},{6,254},{7,255},{8... | collective-permute-start | bytes 589832 | tf_op jit(solution)/shard_map/ppermute | solution.py:23
  48.6 0.8 copy-start.5
  49.3 14.7 %collective-permute-start.8 = (f32[42,16,128]{2,1,0:T(8,128)S(1)}, f32[42,16,128]{2,1,0:T(8,128)S(1)}, u32[]{:S(2)}, u32[]{:S(2)}) collective-permute-start(f32[42,16,128]{2,1,0:T(8,128)S(1)} %get-tuple-element.54), channel_id=1, source_target_pairs={{0,1},{1,0},{2,3},{3,2},{4,5},{5,4},{6,7},{7,6},{8,9},{9,8},{10,11... | collective-permute-start | bytes 1032200 | tf_op jit(solution)/shard_map/ppermute | solution.py:23
  49.8 14.3 %collective-permute-start.9 = (f32[42,16,128]{2,1,0:T(8,128)S(1)}, f32[42,16,128]{2,1,0:T(8,128)S(1)}, u32[]{:S(2)}, u32[]{:S(2)}) collective-permute-start(f32[42,16,128]{2,1,0:T(8,128)S(1)} %get-tuple-element.55), channel_id=1, source_target_pairs={{0,7},{1,2},{2,1},{3,4},{4,3},{5,6},{6,5},{7,0},{8,15},{9,10},{10,... | collective-permute-start | bytes 1032200 | tf_op jit(solution)/shard_map/ppermute | solution.py:23
  53.2 26.4 %all-to-all-start = ((f32[256,2,128]{2,1,0:T(2,128)}), f32[256,2,128]{2,1,0:T(2,128)S(1)}, u32[]{:S(2)}, u32[]{:S(2)}) async-start(f32[256,2,128]{2,1,0:T(2,128)} %broadcast_in_dim.4), calls=%async_computation | async-start | bytes 524288 | tf_op jit(solution)/shard_map/all_to_all | solution.py:874
  64.8 3.4 %collective-permute-start.10 = (f32[11,48,128]{2,1,0:T(8,128)S(1)}, f32[11,48,128]{2,1,0:T(8,128)S(1)}, u32[]{:S(2)}, u32[]{:S(2)}) collective-permute-start(f32[11,48,128]{2,1,0:T(8,128)S(1)} %get-tuple-element.57), channel_id=1, source_target_pairs={{0,8},{1,9},{2,10},{3,11},{4,12},{5,13},{6,14},{7,15},{8,0},{9,1},... | collective-permute-start | bytes 811016 | tf_op jit(solution)/shard_map/ppermute | solution.py:23
  67.0 7.7 %collective-permute-start.11 = (f32[11,48,128]{2,1,0:T(8,128)S(1)}, f32[11,48,128]{2,1,0:T(8,128)S(1)}, u32[]{:S(2)}, u32[]{:S(2)}) collective-permute-start(f32[11,48,128]{2,1,0:T(8,128)S(1)} %get-tuple-element.58), channel_id=1, source_target_pairs={{0,248},{1,249},{2,250},{3,251},{4,252},{5,253},{6,254},{7,255},{8... | collective-permute-start | bytes 811016 | tf_op jit(solution)/shard_map/ppermute | solution.py:23
  75.4 1.0 copy-start.2
  76.4 19.0 %copy-start.8 = (s32[3]{0:T(128)S(1)}, s32[3]{0:T(128)}, u32[]{:S(2)}) copy-start(s32[3]{0:T(128)} %copy-done.7) | copy-start | bytes 40
  79.6 0.7 copy-start.14
  90.8 4.6 %collective-permute-start.13 = (f32[8,16,128]{2,1,0:T(8,128)}, f32[8,16,128]{2,1,0:T(8,128)S(1)}, u32[]{:S(2)}, u32[]{:S(2)}) collective-permute-start(f32[8,16,128]{2,1,0:T(8,128)} %get-tuple-element.60.refs_1_), channel_id=1, source_target_pairs={{0,7},{1,2},{2,1},{3,4},{4,3},{5,6},{6,5},{7,0},{8,15},{9,10},{10,... | collective-permute-start | bytes 196616 | tf_op jit(solution)/shard_map/ppermute | solution.py:23
  91.2 4.3 %collective-permute-start.12 = (f32[8,16,128]{2,1,0:T(8,128)}, f32[8,16,128]{2,1,0:T(8,128)S(1)}, u32[]{:S(2)}, u32[]{:S(2)}) collective-permute-start(f32[8,16,128]{2,1,0:T(8,128)} %get-tuple-element.60.refs_1_), channel_id=1, source_target_pairs={{0,1},{1,0},{2,3},{3,2},{4,5},{5,4},{6,7},{7,6},{8,9},{9,8},{10,11... | collective-permute-start | bytes 196616 | tf_op jit(solution)/shard_map/ppermute | solution.py:23
  95.5 0.8 copy-start.6
  96.9 3.4 %collective-permute-start.14 = (f32[5,48,128]{2,1,0:T(8,128)S(1)}, f32[5,48,128]{2,1,0:T(8,128)S(1)}, u32[]{:S(2)}, u32[]{:S(2)}) collective-permute-start(f32[5,48,128]{2,1,0:T(8,128)S(1)} %get-tuple-element.61), channel_id=1, source_target_pairs={{0,8},{1,9},{2,10},{3,11},{4,12},{5,13},{6,14},{7,15},{8,0},{9,1},... | collective-permute-start | bytes 368648 | tf_op jit(solution)/shard_map/ppermute | solution.py:23
  99.3 4.3 %collective-permute-start.15 = (f32[5,48,128]{2,1,0:T(8,128)S(1)}, f32[5,48,128]{2,1,0:T(8,128)S(1)}, u32[]{:S(2)}, u32[]{:S(2)}) collective-permute-start(f32[5,48,128]{2,1,0:T(8,128)S(1)} %get-tuple-element.62), channel_id=1, source_target_pairs={{0,248},{1,249},{2,250},{3,251},{4,252},{5,253},{6,254},{7,255},{8... | collective-permute-start | bytes 368648 | tf_op jit(solution)/shard_map/ppermute | solution.py:23
  105.6 0.8 copy-start.4
  107.2 26.4 %all-to-all-start.1 = ((f32[256,2,128]{2,1,0:T(2,128)}), f32[256,2,128]{2,1,0:T(2,128)S(1)}, u32[]{:S(2)}, u32[]{:S(2)}) async-start(f32[256,2,128]{2,1,0:T(2,128)} %broadcast_in_dim.5), calls=%async_computation.1 | async-start | bytes 524288 | tf_op jit(solution)/shard_map/all_to_all | solution.py:874
  118.0 1.4 copy-start.1
  123.1 1.2 copy-start.3
  133.5 0.7 copy-start.13

commit v2 on v1

--- a/solution.py
+++ b/solution.py
@@ -15,7 +15,7 @@
 BF16 = jnp.bfloat16
 VMEM = pltpu.VMEM
 LIMIT = 24 * 1024 * 1024
-WHOLE = 63 * 1024 * 1024
+WHOLE = 60 * 1024 * 1024
 
 
 def swap(x, fx, fy):
@@ -68,7 +68,7 @@
             self.sent = True
 
 
-def call(kernel, out_shapes, scratch, *args, late=(), early=()):
+def call(kernel, out_shapes, scratch, *args, late=(), early=(), direct=()):
     nbytes = sum(a.size * 4 for a in args) + sum(4 * functools.reduce(lambda x, y: x * y, s) for s in out_shapes)
     n_in, n_out = len(args), len(out_shapes)
 
@@ -103,7 +103,7 @@
         body,
         out_shape=[jax.ShapeDtypeStruct(s, F32) for s in out_shapes],
         in_specs=specs,
-        out_specs=[pl.BlockSpec(memory_space=pltpu.HBM if n in early else VMEM) for n in range(n_out)],
+        out_specs=[pl.BlockSpec(memory_space=pltpu.HBM if n in early or n in direct else VMEM) for n in range(n_out)],
         scratch_shapes=list(scratch) + extra,
         compiler_params=pltpu.CompilerParams(vmem_limit_bytes=WHOLE if late else LIMIT),
         cost_estimate=pl.CostEstimate(flops=10_000_000, bytes_accessed=nbytes, transcendentals=0),
@@ -289,31 +289,7 @@
     return jnp.where(r < split, r, r - n).astype(F32)
 
 
-def pack_gy(info, vel, cells, offs, c_out, d_out, pts):
-    ix, iy, px, py = place(info)
-    cells, offs = use(cells), use(offs)
-    for n in range(3):
-        for h in range(2):
-            pts[2 * n + h : 2 * n + h + 1, :] = cells[n, 0, :, 128 * h : 128 * h + 128].astype(F32)
-            pts[6 + 2 * n + h : 7 + 2 * n + h, :] = offs[n, 0, :, 128 * h : 128 * h + 128]
-
-    vel = use(vel)
-
-    def body(t, u):
-        c = t // W
-        x = t - c * W
-        to_hi = vel[c, x, W - 4 : W, :]
-        to_lo = vel[c, x, 0:4, :]
-        c_out[t] = jnp.where(py == 0, to_hi, to_lo)
-        d_out[t] = jnp.where(py == 0, to_lo, to_hi)
-
-    rows(0, 3 * W, 24, body)
-    for k in range(3):
-        c_out[3 * W + k] = pts[4 * k : 4 * k + 4, :]
-        d_out[3 * W + k] = pts[4 * k : 4 * k + 4, :]
-
-
-def pack_gx(info, vel, pts, c_in, d_in, a_out, b_out):
+def pack_gx(info, low, high, c_in, d_in, a_out, b_out):
     ix, iy, px, py = place(info)
     ok_hi, ok_lo = okf(iy < NGY - 1), okf(iy > 0)
     off_a = jnp.where(px == 0, W - 4, 0)
@@ -324,20 +300,70 @@
                 x = off + k
                 e = c * 4 + k
                 hi, lo = hi_lo(py, c_in[c * W + x], d_in[c * W + x])
-                out[e, 0:W, :] = vel[c, x]
+                out[e, 0:W, :] = jnp.where(off > 0, high[c, k], low[c, k])
                 out[e, W : W + 4, :] = hi * ok_hi
                 out[e, W + 4 : W + 8, :] = lo * ok_lo
-        out[12, 0:12, :] = pts[...]
-        for k in range(3):
-            hi, lo = hi_lo(py, c_in[3 * W + k], d_in[3 * W + k])
-            out[12, 12 + 4 * k : 16 + 4 * k, :] = hi
-            out[12, 24 + 4 * k : 28 + 4 * k, :] = lo
-        out[12, 36:40, :] = jnp.zeros((4, 128), F32)
+
+
+def points(info, cells, offs):
+    where = [cells[n, 0].astype(F32) for n in range(3)]
+    local = [where[0] - (info[0] * W).astype(F32), where[1] - (info[1] * W).astype(F32), where[2]]
+    off = [offs[n, 0] for n in range(3)]
+    return where, local, off, [tap_norm(o) for o in off]
+
+
+def sampled_lines(slabs, wx, first, wz3, acc):
+    for c in range(3):
+        n = slabs[c].shape[0]
+        hi, lo = split3(slabs[c].reshape(40 * n, 128))
+        r = dot(jnp.concatenate([hi, hi, lo], axis=1), wz3).reshape(n, 40, P_)
+        for k in range(n):
+            m = r[k] * wx[first + k : first + k + 1, :]
+            acc[c] = m if acc[c] is None else acc[c] + m
+
+
+def z_table(local, off, inv):
+    hi, lo = split3(taps(row_coord(128, 0), local[2], off[2], inv[2]))
+    return jnp.concatenate([hi, lo, hi], axis=0)
+
+
+def sample_kernel(info, vel, cells, offs, c_in, d_in, part, xt, yt, zt):
+    ix, iy, px, py = place(info)
+    ok_hi, ok_lo = okf(iy < NGY - 1), okf(iy > 0)
+    where, local, off, inv = points(info, cells, offs)
+    wz3 = z_table(local, off, inv)
+    wx = taps(row_coord(W, 0), local[0], off[0], inv[0])
+    acc = [None] * 3
+    for t in range(4):
+        slabs = []
+        for c in range(3):
+            lines = []
+            for x in range(t * 8, t * 8 + 8):
+                hi, lo = hi_lo(py, c_in[c * W + x], d_in[c * W + x])
+                lines.append(jnp.concatenate([vel[c, x], hi * ok_hi, lo * ok_lo], axis=0))
+            slabs.append(jnp.stack(lines))
+        sampled_lines(slabs, wx, t * 8, wz3, acc)
+    for c in range(3):
+        part[c] = acc[c]
+
+    def axis_taps(d, coord, start, size):
+        def at(shift):
+            q = coord + shift
+            ok = (q + start >= 0.0) & (q + start < size)
+            return taps(q, local[d], off[d], inv[d], ok)
+
+        return at(0.0), at(1.0) - at(-1.0)
+
+    xt[0], xt[1] = axis_taps(0, row_coord(48, -5), (ix * W).astype(F32), float(W * NGX))
+    yt[0], yt[1] = axis_taps(1, cyc_coord(48, 40), (iy * W).astype(F32), float(W * NGY))
+    wz, dz = axis_taps(2, row_coord(128, 0), 0.0, 128.0)
+    zt[0] = -0.5 * wz.T
+    zt[1] = -0.5 * dz.T
 
 
 def force_kernel(
-    info, vel, pts, drags, blades, c_in, d_in, a_in, b_in,
-    g_out, f_out, own_out, c_out, d_out, cg_out, dg_out, pts9,
+    info, vel, cells, offs, drags, blades, part, xt, yt, zt, c_in, d_in, a_in, b_in,
+    g_out, f_out, own_out, c_out, d_out,
     wide, rv, vt, dom, tmp, tmp1,
 ):
     ix, iy, px, py = place(info)
@@ -362,27 +388,17 @@
 
     start_x = (ix * W).astype(F32)
     start_y = (iy * W).astype(F32)
-    cx = vec(pts, 0) - start_x
-    cy = vec(pts, 2) - start_y
-    cz = vec(pts, 4)
-    ox, oy, oz = vec(pts, 6), vec(pts, 8), vec(pts, 10)
-    nx, ny, nz = tap_norm(ox), tap_norm(oy), tap_norm(oz)
+    place_of, local, off, inv = points(info, cells, offs)
+    (cx, cy, cz), (ox, oy, oz), (nx, ny, nz) = local, off, inv
     z = row_coord(128, 0)
 
-    wz = taps(z, cz, oz, nz)
-    wz_hi, wz_lo = split3(wz)
-    wz3 = jnp.concatenate([wz_hi, wz_lo, wz_hi], axis=0)
-    wx40 = taps(row_coord(40, -4), cx, ox, nx)
+    wz3 = z_table(local, off, inv)
+    rim = row_coord(8, 0)
+    wx8 = taps(jnp.where(rim < 4.0, rim - 4.0, rim + (W - 4.0)), cx, ox, nx)
     wy40 = taps(cyc_coord(40, 36), cy, oy, ny)
-    acc = [None] * 3
-    for t in range(5):
-        for c in range(3):
-            part = wide[c, t * 8 : t * 8 + 8].reshape(320, 128)
-            hi, lo = split3(part)
-            r = dot(jnp.concatenate([hi, hi, lo], axis=1), wz3).reshape(8, 40, P_)
-            for k in range(8):
-                m = r[k] * wx40[t * 8 + k : t * 8 + k + 1, :]
-                acc[c] = m if acc[c] is None else acc[c] + m
+    acc = [part[c] for c in range(3)]
+    slabs = [jnp.concatenate([wide[c, 0:4], wide[c, W + 4 : W + 8]], axis=0) for c in range(3)]
+    sampled_lines(slabs, wx8, 0, wz3, acc)
     sampled = [jnp.sum(acc[c] * wy40, axis=0, keepdims=True) for c in range(3)]
     drag, blade = drags[0], blades[0]
     slot = lax.broadcasted_iota(jnp.int32, (1, P_), 1)
@@ -390,25 +406,16 @@
     speed = jnp.sqrt(sampled[0] * sampled[0] + sampled[1] * sampled[1] + sampled[2] * sampled[2] + blade * blade)
     pull = -(drag * speed * live)
     force = [pull * s for s in sampled]
-    for c in range(3):
-        f_out[2 * c : 2 * c + 1, :] = force[c][:, 0:128]
-        f_out[2 * c + 1 : 2 * c + 2, :] = force[c][:, 128:256]
-    f_out[6:8, :] = jnp.zeros((2, 128), F32)
-
-    def axis_taps(coord, cell, off, inv, start, size):
-        def at(shift):
-            q = coord + shift
-            ok = (q + start >= 0.0) & (q + start < size)
-            return taps(q, cell, off, inv, ok)
-
-        return at(0.0), at(1.0) - at(-1.0)
-
-    wx, dx = axis_taps(row_coord(48, -5), cx, ox, nx, start_x, float(W * NGX))
-    wy, dy = axis_taps(cyc_coord(48, 40), cy, oy, ny, start_y, float(W * NGY))
-    wzz, dz = axis_taps(z, cz, oz, nz, 0.0, 128.0)
-    r1_hi, r1_lo = split3(-0.5 * wzz.T)
-    r2_hi, r2_lo = split3(-0.5 * dz.T)
-    right = jnp.concatenate([r1_hi, r2_hi, r1_lo, r2_lo, r1_hi, r2_hi], axis=0)
+    for n, q in enumerate(force + place_of + [ox, oy, oz]):
+        f_out[2 * n : 2 * n + 1, :] = q[:, 0:128]
+        f_out[2 * n + 1 : 2 * n + 2, :] = q[:, 128:256]
+    f_out[18:32, :] = jnp.zeros((14, 128), F32)
+
+    wx, dx, wy, dy = xt[0], xt[1], yt[0], yt[1]
+    r1_hi, r1_lo = split3(zt[0])
+    r2_hi, r2_lo = split3(zt[1])
+    right_hi = jnp.concatenate([r1_hi, r2_hi], axis=0)
+    right = jnp.concatenate([right_hi, jnp.concatenate([r1_lo, r2_lo], axis=0)], axis=1)
     fy_dy = force[1] * dy
     fx_wy = force[0] * wy
     fz_wy = force[2] * wy
@@ -433,8 +440,9 @@
             l2.append(row_w * fz_wy)
         l1_hi, l1_lo = split3(jnp.concatenate(l1, axis=0))
         l2_hi, l2_lo = split3(jnp.concatenate(l2, axis=0))
-        left = jnp.concatenate([l1_hi, l2_hi, l1_hi, l2_hi, l1_lo, l2_lo], axis=1)
-        r = dot(left, right).reshape(7, 48, 128)
+        both = dot(jnp.concatenate([l1_hi, l2_hi], axis=1), right)
+        rest = dot(jnp.concatenate([l1_lo, l2_lo], axis=1), right_hi)
+        r = (both[:, 0:128] + both[:, 128:256] + rest).reshape(7, 48, 128)
         for k in range(7):
             i = t * 7 + k
             share = r[k] * (dom[...] * x_in(ix * W - 5, i, W * NGX))
@@ -464,25 +472,17 @@
         c_out[k] = jnp.where(py == 0, to_hi, to_lo)
         d_out[k] = jnp.where(py == 0, to_lo, to_hi)
     for out in (c_out, d_out):
-        out[12, 0:8, :] = f_out[...]
-        out[12, 8:16, :] = jnp.zeros((8, 128), F32)
-
+        out[12] = f_out[0:16, :]
+        out[13] = f_out[16:32, :]
+
+
+def pack_g(info, g, cg_out, dg_out):
+    ix, iy, px, py = place(info)
     for i in range(42):
-        to_hi = g_out[i + 4, 24:40, :]
-        to_lo = jnp.concatenate([g_out[i + 4, 40:48, :], g_out[i + 4, 0:8, :]], axis=0)
+        to_hi = g[i + 4, 24:40, :]
+        to_lo = jnp.concatenate([g[i + 4, 40:48, :], g[i + 4, 0:8, :]], axis=0)
         cg_out[i] = jnp.where(py == 0, to_hi, to_lo)
         dg_out[i] = jnp.where(py == 0, to_lo, to_hi)
-    pts9[0, 0:12, :] = pts[...]
-    for k in range(3):
-        hi, lo = hi_lo(py, c_in[3 * W + k], d_in[3 * W + k])
-        pts9[1, 4 * k : 4 * k + 4, :] = hi
-        pts9[2, 4 * k : 4 * k + 4, :] = lo
-    hi, lo = hi_lo(px, a_in[12], b_in[12])
-    for m in range(3):
-        pts9[3 + m, 0:12, :] = hi[12 * m : 12 * m + 12]
-        pts9[6 + m, 0:12, :] = lo[12 * m : 12 * m + 12]
-    for k in range(9):
-        pts9[k, 12:16, :] = jnp.zeros((4, 128), F32)
 
 
 def merge_g(info, g, c_in, d_in, h_out, a_out, b_out):
@@ -509,7 +509,7 @@
     rows(0, 11, 11, pack)
 
 
-def emit_level1(c_out, tmp1, v2, b, tmp):
+def emit_level1(own_out, c_out, d_out, py, tmp1, v2, b, tmp):
     lane = lanes((16, 128))
 
     def emit(k, u, r):
@@ -517,7 +517,10 @@
 
     restrict_rows(emit, v2, b, tmp, 0, 16, 6, 1, 16)
     for k in range(8):
-        c_out[k] = jnp.where((lane & 1) == 0, tmp1[2 * k], tmp1[2 * k + 1])
+        own = jnp.where((lane & 1) == 0, tmp1[2 * k], tmp1[2 * k + 1])
+        own_out[k] = own
+        c_out[k] = jnp.where(py == 0, own[8:16], own[0:8])
+        d_out[k] = jnp.where(py == 0, own[0:8], own[8:16])
 
 
 def down0(info, h, a_in, b_in, b_out, dom):
@@ -558,14 +561,18 @@
         s_out[k, 44:48, :] = own[k, 20:24, :] + lo[8:12]
     off_a = jnp.where(px == 0, 5, 0)
     off_b = 5 - off_a
-    hi, lo = hi_lo(py, c_in[12], d_in[12])
     for out, off in ((a_out, off_a), (b_out, off_b)):
         for k in range(7):
-            out[k] = s_out[off + k]
-        out[7, 0:8, :] = f[...]
-        out[7, 8:16, :] = jnp.zeros((8, 128), F32)
-        out[7, 16:32, :] = hi
-        out[7, 32:48, :] = lo
+            out[k, 0:28, :] = s_out[off + k, 0:28, :]
+            out[k, 28:40, :] = s_out[off + k, 36:48, :]
+        for n in range(2):
+            hi, lo = hi_lo(py, c_in[12 + n], d_in[12 + n])
+            out[7 + n, 0:16, :] = f[16 * n : 16 * n + 16, :]
+            out[7 + n, 16:32, :] = hi
+            out[9, 16 * n : 16 * n + 16, :] = lo
+        out[7, 32:40, :] = jnp.zeros((8, 128), F32)
+        out[8, 32:40, :] = jnp.zeros((8, 128), F32)
+        out[9, 32:40, :] = jnp.zeros((8, 128), F32)
 
 
 def down1_shares(info, shares, f, c_in, d_in, a_in, b_in, pairs, packed, f9, s_b1, s_v1, s_b2, s_v2, dom1, dom2, tmp, tmp3):
@@ -573,55 +580,73 @@
     okx_hi, okx_lo = okf(ix < NGX - 1), okf(ix > 0)
     dom1[...] = y_domain(48, 16, 16, iy * 16, W * NGY // 2)
     start1, n1x = ix * 16 - 10, W * NGX // 2
+    gap = jnp.zeros((8, 128), F32)
+
+    def wide_y(v):
+        return jnp.concatenate([v[0:28], gap, v[28:40]], axis=0)
+
     for p in range(18):
         total = None
         if 3 <= p < 15:
             total = shares[p - 3]
         if p < 7:
-            part = hi_lo(px, a_in[p], b_in[p])[1] * okx_lo
+            part = wide_y(hi_lo(px, a_in[p], b_in[p])[1] * okx_lo)
             total = part if total is None else total + part
         if p >= 11:
-            part = hi_lo(px, a_in[p - 11], b_in[p - 11])[0] * okx_hi
+            part = wide_y(hi_lo(px, a_in[p - 11], b_in[p - 11])[0] * okx_hi)
             total = part if total is None else total + part
         pairs[p] = total * (dom1[...] * x_in(start1, 2 * p, n1x))
     levels_down(info, pairs, s_b1, s_v1, s_b2, s_v2, dom1, dom2, tmp)
     pack3(packed, s_b2, s_v2, tmp, tmp3)
-    fhi, flo = hi_lo(py, c_in[12, 0:8, :], d_in[12, 0:8, :])
-    f9[0] = f[...]
-    f9[1] = fhi
-    f9[2] = flo
-    hi, lo = hi_lo(px, a_in[7], b_in[7])
-    for m in range(3):
-        f9[3 + m] = hi[16 * m : 16 * m + 8]
-        f9[6 + m] = lo[16 * m : 16 * m + 8]
+    for n in range(2):
+        rows16 = slice(16 * n, 16 * n + 16)
+        f9[0, rows16, :] = f[rows16, :]
+        hi, lo = hi_lo(py, c_in[12 + n], d_in[12 + n])
+        f9[1, rows16, :] = hi
+        f9[2, rows16, :] = lo
+        hi, lo = hi_lo(px, a_in[7 + n], b_in[7 + n])
+        for m in range(2):
+            f9[3 + m, rows16, :] = hi[16 * m : 16 * m + 16]
+            f9[6 + m, rows16, :] = lo[16 * m : 16 * m + 16]
+    hi, lo = hi_lo(px, a_in[9], b_in[9])
+    f9[5] = hi[0:32]
+    f9[8] = lo[0:32]
 
 
 def pack1_gx(info, own, c_in, d_in, a_out, b_out):
     ix, iy, px, py = place(info)
     ok_hi, ok_lo = okf(iy < NGY - 1), okf(iy > 0)
-    off_a = jnp.where(px == 0, 3, 0)
-    off_b = 3 - off_a
+    off_a = jnp.where(px == 0, 4, 0)
+    off_b = 4 - off_a
     for out, off in ((a_out, off_a), (b_out, off_b)):
-        for k in range(5):
+        for k in range(4):
             hi, lo = hi_lo(py, c_in[off + k], d_in[off + k])
             out[k, 0:16, :] = own[off + k]
-            out[k, 16:32, :] = hi * ok_hi
-            out[k, 32:48, :] = lo * ok_lo
+            out[k, 16:24, :] = hi * ok_hi
+            out[k, 24:32, :] = lo * ok_lo
 
 
 def down1(info, own, c_in, d_in, a_in, b_in, pairs, packed, s_b1, s_v1, s_b2, s_v2, dom1, dom2, tmp, tmp3):
     ix, iy, px, py = place(info)
     ok_hi, ok_lo = okf(iy < NGY - 1), okf(iy > 0)
     okx_hi, okx_lo = okf(ix < NGX - 1), okf(ix > 0)
+    gap = jnp.zeros((16, 128), F32)
+    for k in range(18):
+        pairs[k, 24:40, :] = gap
+    zero = jnp.zeros((48, 128), F32)
+    pairs[0] = zero
+    pairs[17] = zero
     for k in range(8):
         hi, lo = hi_lo(py, c_in[k], d_in[k])
         pairs[5 + k, 0:16, :] = own[k]
-        pairs[5 + k, 16:32, :] = hi * ok_hi
-        pairs[5 + k, 32:48, :] = lo * ok_lo
-    for k in range(5):
+        pairs[5 + k, 16:24, :] = hi * ok_hi
+        pairs[5 + k, 40:48, :] = lo * ok_lo
+    for k in range(4):
         hi, lo = hi_lo(px, a_in[k], b_in[k])
-        pairs[k] = lo * okx_lo
-        pairs[13 + k] = hi * okx_hi
+        pairs[1 + k, 0:24, :] = lo[0:24] * okx_lo
+        pairs[1 + k, 40:48, :] = lo[24:32] * okx_lo
+        pairs[13 + k, 0:24, :] = hi[0:24] * okx_hi
+        pairs[13 + k, 40:48, :] = hi[24:32] * okx_hi
     levels_down(info, pairs, s_b1, s_v1, s_b2, s_v2, dom1, dom2, tmp)
     pack3(packed, s_b2, s_v2, tmp, tmp3)
 
@@ -664,10 +689,18 @@
     second = okf((lane == row + 4) & (row < 4))
     for q in range(2):
         s = tmp3[2 * q] * first + tmp3[2 * q + 1] * second
-        packed[q : q + 1, :] = jnp.sum(s, axis=0, keepdims=True)
-
-
-def coarse_up(info, g, pairs, s):
+        tmp3[4 + q, 0:1, :] = jnp.sum(s, axis=0, keepdims=True)
+    both = jnp.concatenate([tmp3[4, 0:1, :], tmp3[5, 0:1, :]], axis=0)
+    packed[...] = jnp.broadcast_to(both[None], packed.shape)
+
+
+def again(info, pairs, v0, b1, v1, b2, v2, v_out, dom1, dom2, tmp):
+    for i in range(44):
+        v_out[i] = v0[i]
+    levels_down(info, pairs, b1, v1, b2, v2, dom1, dom2, tmp)
+
+
+def coarse_up(info, g, pairs, s, ready=None):
     ix, iy, px, py = place(info)
     n3x = NGX * 4
 
@@ -722,7 +755,12 @@
     correct(s.w3, s.v3, s.v4, s.tmp, 12, 18, 0, ((0, 16, 0),), 32, None, start3, n3x)
     sweep(s.v3, s.w3, s.b3, 26, 34, 8, None, start3, n3x, e3)
 
-    levels_down(info, use(pairs), s.b1, s.v1, s.b2, s.v2, s.dom1, s.dom2, s.tmp)
+    if ready is None:
+        levels_down(info, use(pairs), s.b1, s.v1, s.b2, s.v2, s.dom1, s.dom2, s.tmp)
+    else:
+        s.b1, s.v1, s.b2, s.v2 = [use(r) for r in ready]
+        s.dom1[...] = y_domain(48, 16, 16, iy * 16, NGY * 16)
+        s.dom2[...] = y_domain(24, 8, 8, iy * 8, NGY * 8)
     turn = lax.rem(32 - 4 * iy, 32)
 
     def shifted(k):
@@ -772,6 +810,9 @@
 COARSE_SCRATCH = [pltpu.VMEM(shape, F32) for name, shape in COARSE]
 
 
+OUT_SCRATCH = [pltpu.VMEM((3, W, W, 128), F32), pltpu.VMEM((W, W, 128), F32), pltpu.SemaphoreType.DMA((8,))]
+
+
 def bag(refs):
     s = Bag()
     for (name, shape), ref in zip(COARSE, refs):
@@ -782,7 +823,7 @@
 PIECES0 = ((0, 20, 0), (44, 4, 40))
 
 
-def middle(info, g, b0, pairs, v_late, c_out, *scratch):
+def middle(info, g, b0, pairs, v_out, own_out, c_out, d_out, *scratch):
     s = bag(scratch)
     ix, iy, px, py = place(info)
     coarse_up(info, g, pairs, s)
@@ -796,18 +837,16 @@
     correct(s.w0, s.v0, s.e1, s.tmp, 7, 29, -14, PIECES0, 48, s.dom0, start, size)
     sweep(s.x0, s.w0, b0, 2, 42, 1, s.dom0, start, size)
     sweep(s.w0, s.x0, b0, 3, 41, 1, s.dom0, start, size)
-    v_out = v_late.ref
     sweep(v_out, s.w0, b0, 4, 40, 1, s.dom0, start, size)
     for i in (0, 1, 2, 3, 40, 41, 42, 43):
         v_out[i] = zero
-    v_late.flush()
-    emit_level1(c_out, s.tmp1, v_out, b0, s.tmp)
-
-
-def final(info, g, b0, v0, pairs, pushed, vel_out, p_out, *scratch):
+    emit_level1(own_out, c_out, d_out, py, s.tmp1, v_out, b0, s.tmp)
+
+
+def final(info, g, b0, v0, b1, v1, b2, v2, pushed, vel_out, p_out, vel_buf, p_buf, sems, *scratch):
     s = bag(scratch)
     ix, iy, px, py = place(info)
-    coarse_up(info, g, pairs, s)
+    coarse_up(info, g, None, s, (b1, v1, b2, v2))
     s.dom0[...] = y_domain(48, W, 8, iy * W, W * NGY)
     start, size = ix * W - 6, W * NGX
     b0, v0 = use(b0), use(v0)
@@ -815,33 +854,39 @@
     sweep(s.x0, s.w0, b0, 5, 39, 1, s.dom0, start, size)
     zm = z_masks(1)
     pushed = use(pushed)
-
-    def body(x, u):
-        p = s.x0[x + 6]
-        own = p[0:W]
-        p_out[x] = own
-        gx = s.x0[x + 7, 0:W, :] - s.x0[x + 5, 0:W, :]
-        gy = pltpu.roll(p, 47, 0)[0:W] - pltpu.roll(p, 1, 0)[0:W]
-        gz = pltpu.roll(own, 127, 1) * zm[1] - pltpu.roll(own, 1, 1) * zm[0]
-        vel_out[0, x] = pushed[0, x] - 0.5 * gx
-        vel_out[1, x] = pushed[1, x] - 0.5 * gy
-        vel_out[2, x] = pushed[2, x] - 0.5 * gz
-
-    rows(0, W, 32, body)
-
-
-def push_kernel(info, vel, pts9, f9, out):
+    copies = []
+    for t in range(4):
+        for x in range(8 * t, 8 * t + 8):
+            p = s.x0[x + 6]
+            own = p[0:W]
+            p_buf[x] = own
+            gx = s.x0[x + 7, 0:W, :] - s.x0[x + 5, 0:W, :]
+            gy = pltpu.roll(p, 47, 0)[0:W] - pltpu.roll(p, 1, 0)[0:W]
+            gz = pltpu.roll(own, 127, 1) * zm[1] - pltpu.roll(own, 1, 1) * zm[0]
+            vel_buf[0, x] = pushed[0, x] - 0.5 * gx
+            vel_buf[1, x] = pushed[1, x] - 0.5 * gy
+            vel_buf[2, x] = pushed[2, x] - 0.5 * gz
+        part = pl.ds(8 * t, 8)
+        copies.append(pltpu.make_async_copy(vel_buf.at[:, part], vel_out.at[:, part], sems.at[2 * t]))
+        copies.append(pltpu.make_async_copy(p_buf.at[part], p_out.at[part], sems.at[2 * t + 1]))
+        copies[-2].start()
+        copies[-1].start()
+    for copy in copies:
+        copy.wait()
+
+
+def push_kernel(info, vel, f9, out):
     ix, iy, px, py = place(info)
     ok = {-1: (okf(ix > 0), okf(iy > 0)), 0: (1.0, 1.0), 1: (okf(ix < NGX - 1), okf(iy < NGY - 1))}
     start_x = (ix * W).astype(F32)
     start_y = (iy * W).astype(F32)
     order = ((0, 0), (0, 1), (0, -1), (1, 0), (1, 1), (1, -1), (-1, 0), (-1, 1), (-1, -1))
     for slot, (ox_, oy_) in enumerate(order):
-        q, fq = pts9.at[slot], f9.at[slot]
-        cx, cy, cz = vec(q, 0) - start_x, vec(q, 2) - start_y, vec(q, 4)
-        ox, oy, oz = vec(q, 6), vec(q, 8), vec(q, 10)
+        q = f9.at[slot]
+        cx, cy, cz = vec(q, 6) - start_x, vec(q, 8) - start_y, vec(q, 10)
+        ox, oy, oz = vec(q, 12), vec(q, 14), vec(q, 16)
         keep = ok[ox_][0] * ok[oy_][1]
-        force = [vec(fq, 2 * c) * keep for c in range(3)]
+        force = [vec(q, 2 * c) * keep for c in range(3)]
         wx = taps(row_coord(32, 0), cx, ox, tap_norm(ox))
         y0, yn = {0: (0, 32), 1: (24, 8), -1: (0, 8)}[oy_]
         wy = taps(row_coord(yn, y0), cy, oy, tap_norm(oy))
@@ -870,57 +915,64 @@
 
 
 def gather3(packed):
-    everyone = jnp.broadcast_to(packed[None], (NGX * NGY, 2, 128))
-    return lax.all_to_all(everyone, AXES, 0, 0, tiled=True).reshape(NGX, 16, 128)
-
-
-LEVELS12 = [(18, 48, 128), (2, 128)]
+    return lax.all_to_all(packed, AXES, 0, 0, tiled=True).reshape(NGX, 16, 128)
+
+
+LEVELS12 = [(18, 48, 128), (NGX * NGY, 2, 128)]
 DOWN1 = [
     VMEM((36, 48, 128), F32), VMEM((36, 48, 128), F32), VMEM((16, 24, 128), F32), VMEM((16, 24, 128), F32),
-    VMEM((48, 128), F32), VMEM((24, 128), F32), VMEM((32, 48, 128), F32), VMEM((4, 8, 128), F32),
+    VMEM((48, 128), F32), VMEM((24, 128), F32), VMEM((32, 48, 128), F32), VMEM((6, 8, 128), F32),
 ]
 
 
 def per_device(velocity, point_cells, point_offsets, point_count, drag, blade_speed):
     info = jnp.stack([lax.axis_index("gx"), lax.axis_index("gy"), point_count.reshape(())]).astype(jnp.int32)
 
-    c0, d0, pts = call(
-        pack_gy, [(99, 4, 128)] * 2 + [(12, 128)], [], info, velocity, point_cells, point_offsets
+    py = lax.axis_index("gy") % 2
+    top, bottom = velocity[:, :, W - 4 :, :].reshape(3 * W, 4, 128), velocity[:, :, :4, :].reshape(3 * W, 4, 128)
+    c0, d0 = swap_gy(jnp.where(py == 0, top, bottom), jnp.where(py == 0, bottom, top))
+    a0, b0 = call(pack_gx, [(12, 40, 128)] * 2, [], info, velocity[:, :4], velocity[:, W - 4 :], c0, d0)
+    a0, b0 = swap_gx(a0, b0)
+    part, xt, yt, zt = call(
+        sample_kernel, [(3, 40, P_), (2, 48, P_), (2, 48, P_), (2, P_, 128)], [], info, velocity, point_cells, point_offsets, c0, d0
     )
-    c0, d0 = swap_gy(c0, d0)
-    a0, b0 = call(pack_gx, [(13, 40, 128)] * 2, [], info, velocity, pts, c0, d0)
-    a0, b0 = swap_gx(a0, b0)
-    g, f, own1, c1, d1, cg, dg, pts9 = call(
+    g, f, own1, c1, d1 = call(
         force_kernel,
-        [(50, 48, 128), (8, 128), (12, 24, 128), (13, 16, 128), (13, 16, 128), (42, 16, 128), (42, 16, 128), (9, 16, 128)],
+        [(50, 48, 128), (32, 128), (12, 24, 128), (14, 16, 128), (14, 16, 128)],
         [
             VMEM((3, 40, 40, 128), F32), VMEM((W, W, 128), F32), VMEM((50, 48, 128), F32), VMEM((48, 128), F32),
             VMEM((32, 48, 128), F32), VMEM((24, 24, 128), F32),
         ],
-        info, velocity, pts, drag, blade_speed, c0, d0, a0, b0,
+        info, velocity, point_cells, point_offsets, drag, blade_speed, part, xt, yt, zt, c0, d0, a0, b0,
     )
     c1, d1 = swap_gy(c1, d1)
-    shares, a1, b1 = call(merge1_gx, [(12, 48, 128), (8, 48, 128), (8, 48, 128)], [], info, own1, f, c1, d1)
+    shares, a1, b1 = call(merge1_gx, [(12, 48, 128), (10, 40, 128), (10, 40, 128)], [], info, own1, f, c1, d1)
     a1, b1 = swap_gx(a1, b1)
-    pairs, packed, f9 = call(down1_shares, LEVELS12 + [(9, 8, 128)], DOWN1, info, shares, f, c1, d1, a1, b1)
-    packed, g, cg, dg = lax.optimization_barrier((packed, g, cg, dg))
+    pairs, packed, f9 = call(down1_shares, LEVELS12 + [(9, 32, 128)], DOWN1, info, shares, f, c1, d1, a1, b1)
+    cg, dg = call(pack_g, [(42, 16, 128)] * 2, [], info, g)
+    packed, g, cg, dg, f9 = lax.optimization_barrier((packed, g, cg, dg, f9))
     gathered = gather3(packed)
     cg, dg = swap_gy(cg, dg)
     h, ag, bg = call(merge_g, [(42, 48, 128), (11, 48, 128), (11, 48, 128)], [], info, g, cg, dg)
     ag, bg = swap_gx(ag, bg)
     (rhs,) = call(down0, [(44, 48, 128)], [VMEM((48, 128), F32)], info, h, ag, bg)
-    v0, own1 = call(
-        middle, [(44, 48, 128), (8, 16, 128)], COARSE_SCRATCH, info, gathered, rhs, pairs, late=(2, 3), early=(0,)
+    v0, own1, c1, d1 = call(
+        middle, [(44, 48, 128), (8, 16, 128), (8, 8, 128), (8, 8, 128)], COARSE_SCRATCH, info, gathered, rhs, pairs
     )
-    c1, d1 = swap_gy(own1, own1)
-    a1, b1 = call(pack1_gx, [(5, 48, 128)] * 2, [], info, own1, c1, d1)
+    c1, d1 = swap_gy(c1, d1)
+    a1, b1 = call(pack1_gx, [(4, 32, 128)] * 2, [], info, own1, c1, d1)
     a1, b1 = swap_gx(a1, b1)
     pairs, packed = call(down1, LEVELS12, DOWN1, info, own1, c1, d1, a1, b1)
-    packed, pts9 = lax.optimization_barrier((packed, pts9))
+    packed, pairs, v0 = lax.optimization_barrier((packed, pairs, v0))
     gathered = gather3(packed)
-    (pushed,) = call(push_kernel, [(3, W, W, 128)], [], info, velocity, pts9, f9)
+    *levels, v0 = call(
+        again, [(36, 48, 128), (36, 48, 128), (16, 24, 128), (16, 24, 128), (44, 48, 128)],
+        [VMEM((48, 128), F32), VMEM((24, 128), F32), VMEM((32, 48, 128), F32)], info, pairs, v0,
+    )
+    (pushed,) = call(push_kernel, [(3, W, W, 128)], [], info, velocity, f9)
     vel_out, p_out = call(
-        final, [(3, W, W, 128), (W, W, 128)], COARSE_SCRATCH, info, gathered, rhs, v0, pairs, pushed, late=(2, 3, 4, 5)
+        final, [(3, W, W, 128), (W, W, 128)], OUT_SCRATCH + COARSE_SCRATCH, info, gathered, rhs, v0, *levels, pushed,
+        late=(2, 3, 4, 5, 6, 7, 8), direct=(0, 1),
     )
     return vel_out, p_out
 

time: 144 us -> 132 us (0.917)
  waiting for transfers between devices: 44 us -> 33.4 us
    ppermute x16, waiting for transfers between devices: 31.6 us -> 26 us  [swap(): return lax.ppermute(x, AXES, perm)]
    all_to_all x2, waiting for transfers between devices: 12.5 us -> 7.39 us  [gather3(): return lax.all_to_all(packed, AXES, 0, 0, tiled=True).reshape(NGX, 16, 128)]
    broadcast_in_dim x2 -> x0, local copies, waits for them, and re-layouts: 1.54 us -> none  [gather3(): everyone = jnp.broadcast_to(packed[None], (NGX * NGY, 2, 128))]
    unnamed x30 -> x38, local copies, waits for them, and re-layouts: 10.1 us -> 9.32 us
    pallas_call x12 -> x14, Pallas kernels: 37.3 us -> 37.3 us  [call(): pl.pallas_call(body, out_shape=[jax.ShapeDtypeStruct(s, F32) for s in out...]
  transfers between devices with their start and end apart: 18 -> 18, of which waited for: 13 -> 13; matrix products, arithmetic and copies ran while one was open for 1% -> 1% of each run, Pallas kernels for 4% -> 8%
where the time goes in v2:
time: 132 us
  starting transfers between devices  47.3 us (36%)
  Pallas kernels  37.3 us (28%)
  waiting for transfers between devices  33.4 us (25%)
  local copies, waits for them, and re-layouts  10.4 us (8%)
  between operations  1.73 us (1%)
  other arithmetic  1.38 us (1%)
    pallas_call x14, Pallas kernels, call(): pl.pallas_call(body, out_shape=[jax.ShapeDtypeStruct(s, F32) for s in out...  37.3 us
    ppermute x16, starting transfers between devices, swap(): return lax.ppermute(x, AXES, perm)  26.2 us
    ppermute x16, waiting for transfers between devices, swap(): return lax.ppermute(x, AXES, perm)  26 us
    all_to_all x2, starting transfers between devices, gather3(): return lax.all_to_all(packed, AXES, 0, 0, tiled=True).reshape(NGX, 16, 128)  21.2 us
    unnamed x38, local copies, waits for them, and re-layouts  9.32 us
    all_to_all x2, waiting for transfers between devices, gather3(): return lax.all_to_all(packed, AXES, 0, 0, tiled=True).reshape(NGX, 16, 128)  7.39 us
  transfers between devices with their start and end apart: 18, of which 13 were waited for; matrix products, arithmetic and copies ran while one was open for 1% of the time, Pallas kernels for 8%

profile of v2, /device:TPU:1, one launch (start us, length us, event | category | flops | bytes accessed | tf_op | source)
XLA Modules:
  0.0 131.5 jit_solution(16990015844040521335)
XLA Ops:
  0.7 1.3 slice_select_fusion
  2.0 2.6 %collective-permute-start = (f32[96,4,128]{2,1,0:T(4,128)S(1)}, f32[96,4,128]{2,1,0:T(4,128)S(1)}, u32[]{:S(2)}, u32[]{:S(2)}) collective-permute-start(f32[96,4,128]{2,1,0:T(4,128)S(1)} %bitcast.11), channel_id=1, source_target_pairs={{0,1},{1,0},{2,3},{3,2},{4,5},{5,4},{6,7},{7,6},{8,9},{9,8},{10,11... | collective-permute-start | bytes 589832 | tf_op jit(solution)/shard_map/ppermute | solution.py:23
  4.5 4.7 %collective-permute-start.1 = (f32[96,4,128]{2,1,0:T(4,128)S(1)}, f32[96,4,128]{2,1,0:T(4,128)S(1)}, u32[]{:S(2)}, u32[]{:S(2)}) collective-permute-start(f32[96,4,128]{2,1,0:T(4,128)S(1)} %bitcast.10), channel_id=1, source_target_pairs={{0,7},{1,2},{2,1},{3,4},{4,3},{5,6},{6,5},{7,0},{8,15},{9,10},{10,... | collective-permute-start | bytes 589832 | tf_op jit(solution)/shard_map/ppermute | solution.py:23
  9.9 1.1 fusion
  11.0 2.5 %collective-permute-done.1.refs_5_.refs_4_.refs_11_ = f32[96,4,128]{2,1,0:T(4,128)S(1)} collective-permute-done((f32[96,4,128]{2,1,0:T(4,128)S(1)}, f32[96,4,128]{2,1,0:T(4,128)S(1)}, u32[]{:S(2)}, u32[]{:S(2)}) %collective-permute-start.1) | collective-permute-done | bytes 196640 | tf_op jit(solution)/shard_map/ppermute | solution.py:23
  14.1 1.6 %collective-permute-start.2 = (f32[12,40,128]{2,1,0:T(8,128)S(1)}, f32[12,40,128]{2,1,0:T(8,128)S(1)}, u32[]{:S(2)}, u32[]{:S(2)}) collective-permute-start(f32[12,40,128]{2,1,0:T(8,128)S(1)} %get-tuple-element.49), channel_id=1, source_target_pairs={{0,8},{1,9},{2,10},{3,11},{4,12},{5,13},{6,14},{7,15},{8,0},{9,1},... | collective-permute-start | bytes 737288 | tf_op jit(solution)/shard_map/ppermute | solution.py:23
  15.7 1.3 collective-permute-start.3
  17.0 2.0 %shard_map.77 = (f32[3,40,256]{2,1,0:T(8,128)S(1)}, f32[2,48,256]{2,1,0:T(8,128)S(1)}, f32[2,48,256]{2,1,0:T(8,128)S(1)}, f32[2,256,128]{2,1,0:T(8,128)S(1)}) custom-call(s32[3]{0:T(128)S(1)} %pad_add_fusion.refs_0_, f32[3,32,32,128]{3,2,1,0:T(8,128)S(1)} %copy-done, s32[3,1,1,256]{3,2,1,0:T(1,128)S(1)} %copy-done.14, f32[3,1,1,256]{3,2,1,0:T(1,128)S(1)} %copy-done.15, ...), custom_call_target="tpu_custom_call" | custom-call | flops 10000000 | bytes 2553868 | tf_op jit(solution)/shard_map/pallas_call | solution.py:102
  19.1 2.3 %collective-permute-done.3.refs_13_ = f32[12,40,128]{2,1,0:T(8,128)S(1)} collective-permute-done((f32[12,40,128]{2,1,0:T(8,128)S(1)}, f32[12,40,128]{2,1,0:T(8,128)S(1)}, u32[]{:S(2)}, u32[]{:S(2)}) %collective-permute-start.3) | collective-permute-done | bytes 245792 | tf_op jit(solution)/shard_map/ppermute | solution.py:23
  21.4 4.6 %shard_map.79 = (f32[50,48,128]{2,1,0:T(8,128)S(1)}, f32[32,128]{1,0:T(8,128)S(1)}, f32[12,24,128]{2,1,0:T(8,128)S(1)}, f32[14,16,128]{2,1,0:T(8,128)S(1)}, f32[14,16,128]{2,1,0:T(8,128)S(1)}) custom-call(s32[3]{0:T(128)S(1)} %pad_add_fusion.refs_0_, f32[3,32,32,128]{3,2,1,0:T(8,128)S(1)} %copy-done, s32[3,1,1,256]{3,2,1,0:T(1,128)S(1)} %copy-done.14, ...), custom_call_target="tpu_custom_call" | custom-call | flops 10000000 | bytes 4669452 | tf_op jit(solution)/shard_map/pallas_call | solution.py:102
  26.1 2.8 %collective-permute-start.5 = (f32[14,16,128]{2,1,0:T(8,128)S(1)}, f32[14,16,128]{2,1,0:T(8,128)S(1)}, u32[]{:S(2)}, u32[]{:S(2)}) collective-permute-start(f32[14,16,128]{2,1,0:T(8,128)S(1)} %get-tuple-element.54), channel_id=1, source_target_pairs={{0,7},{1,2},{2,1},{3,4},{4,3},{5,6},{6,5},{7,0},{8,15},{9,10},{10,... | collective-permute-start | bytes 344072 | tf_op jit(solution)/shard_map/ppermute | solution.py:23
  28.9 0.9 collective-permute-done.4.refs_3_
  29.8 1.3 collective-permute-done.5.refs_4_
  31.7 4.8 %collective-permute-start.6 = (f32[10,40,128]{2,1,0:T(8,128)S(1)}, f32[10,40,128]{2,1,0:T(8,128)S(1)}, u32[]{:S(2)}, u32[]{:S(2)}) collective-permute-start(f32[10,40,128]{2,1,0:T(8,128)S(1)} %get-tuple-element.56), channel_id=1, source_target_pairs={{0,8},{1,9},{2,10},{3,11},{4,12},{5,13},{6,14},{7,15},{8,0},{9,1},... | collective-permute-start | bytes 614408 | tf_op jit(solution)/shard_map/ppermute | solution.py:23
  36.5 1.4 %shard_map.82 = (f32[42,16,128]{2,1,0:T(8,128)}, f32[42,16,128]{2,1,0:T(8,128)}) custom-call(s32[3]{0:T(128)S(1)} %pad_add_fusion.refs_0_, f32[50,48,128]{2,1,0:T(8,128)S(1)} %get-tuple-element.64.refs_1_), custom_call_target="tpu_custom_call" | custom-call | flops 10000000 | bytes 1916940 | tf_op jit(solution)/shard_map/pallas_call | solution.py:102
  38.0 3.7 %collective-permute-done.7.refs_6_ = f32[10,40,128]{2,1,0:T(8,128)S(1)} collective-permute-done((f32[10,40,128]{2,1,0:T(8,128)S(1)}, f32[10,40,128]{2,1,0:T(8,128)S(1)}, u32[]{:S(2)}, u32[]{:S(2)}) %collective-permute-start.7) | collective-permute-done | bytes 204832 | tf_op jit(solution)/shard_map/ppermute | solution.py:23
  41.7 2.1 %shard_map.81 = (f32[18,48,128]{2,1,0:T(8,128)S(1)}, f32[256,2,128]{2,1,0:T(2,128)S(1)}, f32[9,32,128]{2,1,0:T(8,128)S(1)}) custom-call(s32[3]{0:T(128)S(1)} %pad_add_fusion.refs_0_, f32[12,48,128]{2,1,0:T(8,128)S(1)} %get-tuple-element.55.refs_1_, f32[32,128]{1,0:T(8,128)S(1)} %get-tuple-element.52.refs_2_, ...), custom_call_target="tpu_custom_call" | custom-call | flops 10000000 | bytes 1802252 | tf_op jit(solution)/shard_map/pallas_call | solution.py:102
  43.8 0.7 copy-done.8
  45.6 2.7 %collective-permute-start.9 = (f32[42,16,128]{2,1,0:T(8,128)}, f32[42,16,128]{2,1,0:T(8,128)}, u32[]{:S(2)}, u32[]{:S(2)}) collective-permute-start(f32[42,16,128]{2,1,0:T(8,128)} %get-tuple-element.66), channel_id=1, source_target_pairs={{0,7},{1,2},{2,1},{3,4},{4,3},{5,6},{6,5},{7,0},{8,15},{9,10},{10,... | collective-permute-start | bytes 1032200 | tf_op jit(solution)/shard_map/ppermute | solution.py:23
  48.2 10.9 %all-to-all-start = ((f32[256,2,128]{2,1,0:T(2,128)}), f32[256,2,128]{2,1,0:T(2,128)S(1)}, u32[]{:S(2)}, u32[]{:S(2)}) async-start(f32[256,2,128]{2,1,0:T(2,128)} %copy-done.8), calls=%async_computation | async-start | bytes 524288 | tf_op jit(solution)/shard_map/all_to_all | solution.py:918
  59.1 1.2 shard_map.83
  60.4 2.2 %collective-permute-start.10 = (f32[11,48,128]{2,1,0:T(8,128)S(1)}, f32[11,48,128]{2,1,0:T(8,128)S(1)}, u32[]{:S(2)}, u32[]{:S(2)}) collective-permute-start(f32[11,48,128]{2,1,0:T(8,128)S(1)} %get-tuple-element.68), channel_id=1, source_target_pairs={{0,8},{1,9},{2,10},{3,11},{4,12},{5,13},{6,14},{7,15},{8,0},{9,1},... | collective-permute-start | bytes 811016 | tf_op jit(solution)/shard_map/ppermute | solution.py:23
  62.6 1.2 collective-permute-done.10.refs_2_
  63.8 6.5 %collective-permute-done.11.refs_3_ = f32[11,48,128]{2,1,0:T(8,128)S(1)} collective-permute-done((f32[11,48,128]{2,1,0:T(8,128)S(1)}, f32[11,48,128]{2,1,0:T(8,128)S(1)}, u32[]{:S(2)}, u32[]{:S(2)}) %collective-permute-start.11) | collective-permute-done | bytes 270368 | tf_op jit(solution)/shard_map/ppermute | solution.py:23
  70.2 0.7 shard_map.84.refs_2_
  71.0 3.7 %all-to-all-done = f32[256,2,128]{2,1,0:T(2,128)S(1)} async-done(((f32[256,2,128]{2,1,0:T(2,128)}), f32[256,2,128]{2,1,0:T(2,128)S(1)}, u32[]{:S(2)}, u32[]{:S(2)}) %all-to-all-start) | async-done | bytes 262176 | tf_op jit(solution)/shard_map/all_to_all | solution.py:918
  74.7 7.3 %shard_map.85 = (f32[44,48,128]{2,1,0:T(8,128)S(1)}, f32[8,16,128]{2,1,0:T(8,128)S(1)}, f32[8,8,128]{2,1,0:T(8,128)S(1)}, f32[8,8,128]{2,1,0:T(8,128)S(1)}) custom-call(s32[3]{0:T(128)S(1)} %pad_add_fusion.refs_0_, f32[32,16,128]{2,1,0:T(8,128)S(1)} %bitcast.8, f32[44,48,128]{2,1,0:T(8,128)S(1)} %shard_map.84.refs_2_, ...), custom_call_target="tpu_custom_call" | custom-call | flops 10000000 | bytes 2998284 | tf_op jit(solution)/shard_map/pallas_call | solution.py:102
  82.0 1.0 copy-done.4
  83.0 0.7 collective-permute-start.12
  83.7 2.0 %collective-permute-done.12.refs_2_ = f32[8,8,128]{2,1,0:T(8,128)S(1)} collective-permute-done((f32[8,8,128]{2,1,0:T(8,128)S(1)}, f32[8,8,128]{2,1,0:T(8,128)S(1)}, u32[]{:S(2)}, u32[]{:S(2)}) %collective-permute-start.12) | collective-permute-done | bytes 32800 | tf_op jit(solution)/shard_map/ppermute | solution.py:23
  85.8 1.9 %collective-permute-done.13.refs_3_ = f32[8,8,128]{2,1,0:T(8,128)S(1)} collective-permute-done((f32[8,8,128]{2,1,0:T(8,128)S(1)}, f32[8,8,128]{2,1,0:T(8,128)S(1)}, u32[]{:S(2)}, u32[]{:S(2)}) %collective-permute-start.13) | collective-permute-done | bytes 32800 | tf_op jit(solution)/shard_map/ppermute | solution.py:23
  88.3 2.3 %collective-permute-start.14 = (f32[4,32,128]{2,1,0:T(8,128)S(1)}, f32[4,32,128]{2,1,0:T(8,128)S(1)}, u32[]{:S(2)}, u32[]{:S(2)}) collective-permute-start(f32[4,32,128]{2,1,0:T(8,128)S(1)} %get-tuple-element.74), channel_id=1, source_target_pairs={{0,8},{1,9},{2,10},{3,11},{4,12},{5,13},{6,14},{7,15},{8,0},{9,1},... | collective-permute-start | bytes 196616 | tf_op jit(solution)/shard_map/ppermute | solution.py:23
  90.5 0.9 collective-permute-done.14.refs_4_
  91.4 2.8 %collective-permute-done.15.refs_5_ = f32[4,32,128]{2,1,0:T(8,128)S(1)} collective-permute-done((f32[4,32,128]{2,1,0:T(8,128)S(1)}, f32[4,32,128]{2,1,0:T(8,128)S(1)}, u32[]{:S(2)}, u32[]{:S(2)}) %collective-permute-start.15) | collective-permute-done | bytes 65568 | tf_op jit(solution)/shard_map/ppermute | solution.py:23
  94.2 2.6 %shard_map.87 = (f32[18,48,128]{2,1,0:T(8,128)S(1)}, f32[256,2,128]{2,1,0:T(2,128)}) custom-call(s32[3]{0:T(128)S(1)} %pad_add_fusion.refs_0_, f32[8,16,128]{2,1,0:T(8,128)S(1)} %get-tuple-element.71.refs_1_, f32[8,8,128]{2,1,0:T(8,128)S(1)} %collective-permute-done.12.refs_2_, f32[8,8,128]{2,1,0:T(8,128)S(1)} %collective-permute-done.13.refs_3_, ...), custom_call_target="tpu_custom_call" | custom-call | flops 10000000 | bytes 966668 | tf_op jit(solution)/shard_map/pallas_call | solution.py:102
  96.9 10.3 %all-to-all-start.1 = ((f32[256,2,128]{2,1,0:T(2,128)}), f32[256,2,128]{2,1,0:T(2,128)S(1)}, u32[]{:S(2)}, u32[]{:S(2)}) async-start(f32[256,2,128]{2,1,0:T(2,128)} %get-tuple-element.79), calls=%async_computation.1 | async-start | bytes 524288 | tf_op jit(solution)/shard_map/all_to_all | solution.py:918
  107.2 0.9 copy-done.12
  108.1 3.7 %shard_map.89.refs_8_ = f32[3,32,32,128]{3,2,1,0:T(8,128)S(1)} custom-call(s32[3]{0:T(128)S(1)} %pad_add_fusion.refs_0_, f32[3,32,32,128]{3,2,1,0:T(8,128)S(1)} %copy-done, f32[9,32,128]{2,1,0:T(8,128)S(1)} %copy-done.12), custom_call_target="tpu_custom_call" | custom-call | flops 10000000 | bytes 3293196 | tf_op jit(solution)/shard_map/pallas_call | solution.py:102
  111.8 1.2 copy-done.2
  113.0 1.9 %shard_map.88 = (f32[36,48,128]{2,1,0:T(8,128)S(1)}, f32[36,48,128]{2,1,0:T(8,128)S(1)}, f32[16,24,128]{2,1,0:T(8,128)S(1)}, f32[16,24,128]{2,1,0:T(8,128)S(1)}, f32[44,48,128]{2,1,0:T(8,128)S(1)}) custom-call(s32[3]{0:T(128)S(1)} %pad_add_fusion.refs_0_, f32[18,48,128]{2,1,0:T(8,128)S(1)} %get-tuple-element.80.refs_1_, f32[44,48,128]{2,1,0:T(8,128)S(1)} %copy-done.5), custom_call_target="tpu_custom_call" | custom-call | flops 10000000 | bytes 4767756 | tf_op jit(solution)/shard_map/pallas_call | solution.py:102
  114.9 1.0 copy-done.3
  115.9 0.9 copy-done.6
  116.8 0.9 copy-done.7
  117.7 0.7 copy-done.9
  118.4 0.7 copy-done.10
  119.1 3.7 %all-to-all-done.1 = f32[256,2,128]{2,1,0:T(2,128)S(1)} async-done(((f32[256,2,128]{2,1,0:T(2,128)}), f32[256,2,128]{2,1,0:T(2,128)S(1)}, u32[]{:S(2)}, u32[]{:S(2)}) %all-to-all-start.1) | async-done | bytes 262176 | tf_op jit(solution)/shard_map/all_to_all | solution.py:918
  122.8 0.7 copy-done.18
  123.5 7.9 %shard_map.90 = (f32[3,32,32,128]{3,2,1,0:T(8,128)}, f32[32,32,128]{2,1,0:T(8,128)}) custom-call(s32[3]{0:T(128)} %copy-done.13, f32[32,16,128]{2,1,0:T(8,128)} %bitcast.9, f32[44,48,128]{2,1,0:T(8,128)} %copy-done.1, f32[44,48,128]{2,1,0:T(8,128)} %copy-done.3, f32[36,48,128]{2,1,0:T(8,128)} %copy-done.6, f32[36,48,128]{2,1,0:T(8,128)} %copy-done.7, ...), custom_call_target="tpu_custom_call" | custom-call | flops 10000000 | bytes 8257548 | tf_op jit(solution)/shard_map/pallas_call | solution.py:102
  (43 shorter events, 3.1 us)
Async XLA Ops:
  0.6 16.4 %copy-start = (f32[3,32,32,128]{3,2,1,0:T(8,128)S(1)}, f32[3,32,32,128]{3,2,1,0:T(8,128)}, u32[]{:S(2)}) copy-start(f32[3,32,32,128]{3,2,1,0:T(8,128)} %refs_1_.5) | copy-start | bytes 4718596
  0.6 16.4 %copy-start.15 = (f32[3,1,1,256]{3,2,1,0:T(1,128)S(1)}, f32[3,1,1,256]{3,2,1,0:T(1,128)}, u32[]{:S(2)}) copy-start(f32[3,1,1,256]{3,2,1,0:T(1,128)} %refs_3_.3) | copy-start | bytes 9220
  0.7 16.4 %copy-start.14 = (s32[3,1,1,256]{3,2,1,0:T(1,128)S(1)}, s32[3,1,1,256]{3,2,1,0:T(1,128)}, u32[]{:S(2)}) copy-start(s32[3,1,1,256]{3,2,1,0:T(1,128)} %refs_2_.3) | copy-start | bytes 9220
  2.0 9.0 %collective-permute-start = (f32[96,4,128]{2,1,0:T(4,128)S(1)}, f32[96,4,128]{2,1,0:T(4,128)S(1)}, u32[]{:S(2)}, u32[]{:S(2)}) collective-permute-start(f32[96,4,128]{2,1,0:T(4,128)S(1)} %bitcast.11), channel_id=1, source_target_pairs={{0,1},{1,0},{2,3},{3,2},{4,5},{5,4},{6,7},{7,6},{8,9},{9,8},{10,11... | collective-permute-start | bytes 589832 | tf_op jit(solution)/shard_map/ppermute | solution.py:23
  4.5 9.0 %collective-permute-start.1 = (f32[96,4,128]{2,1,0:T(4,128)S(1)}, f32[96,4,128]{2,1,0:T(4,128)S(1)}, u32[]{:S(2)}, u32[]{:S(2)}) collective-permute-start(f32[96,4,128]{2,1,0:T(4,128)S(1)} %bitcast.10), channel_id=1, source_target_pairs={{0,7},{1,2},{2,1},{3,4},{4,3},{5,6},{6,5},{7,0},{8,15},{9,10},{10,... | collective-permute-start | bytes 589832 | tf_op jit(solution)/shard_map/ppermute | solution.py:23
  9.9 101.9 %copy-start.13 = (s32[3]{0:T(128)}, s32[3]{0:T(128)S(1)}, u32[]{:S(2)}) copy-start(s32[3]{0:T(128)S(1)} %pad_add_fusion.refs_0_) | copy-start | bytes 40
  11.0 10.4 %copy-start.16 = (f32[1,1,256]{2,1,0:T(1,128)S(1)}, f32[1,1,256]{2,1,0:T(1,128)}, u32[]{:S(2)}) copy-start(f32[1,1,256]{2,1,0:T(1,128)} %refs_4_.1) | copy-start | bytes 3076
  11.0 10.4 %copy-start.17 = (f32[1,1,256]{2,1,0:T(1,128)S(1)}, f32[1,1,256]{2,1,0:T(1,128)}, u32[]{:S(2)}) copy-start(f32[1,1,256]{2,1,0:T(1,128)} %refs_5_.1) | copy-start | bytes 3076
  14.1 5.0 %collective-permute-start.2 = (f32[12,40,128]{2,1,0:T(8,128)S(1)}, f32[12,40,128]{2,1,0:T(8,128)S(1)}, u32[]{:S(2)}, u32[]{:S(2)}) collective-permute-start(f32[12,40,128]{2,1,0:T(8,128)S(1)} %get-tuple-element.49), channel_id=1, source_target_pairs={{0,8},{1,9},{2,10},{3,11},{4,12},{5,13},{6,14},{7,15},{8,0},{9,1},... | collective-permute-start | bytes 737288 | tf_op jit(solution)/shard_map/ppermute | solution.py:23
  15.7 5.6 %collective-permute-start.3 = (f32[12,40,128]{2,1,0:T(8,128)S(1)}, f32[12,40,128]{2,1,0:T(8,128)S(1)}, u32[]{:S(2)}, u32[]{:S(2)}) collective-permute-start(f32[12,40,128]{2,1,0:T(8,128)S(1)} %get-tuple-element.50), channel_id=1, source_target_pairs={{0,248},{1,249},{2,250},{3,251},{4,252},{5,253},{6,254},{7,255},{8... | collective-permute-start | bytes 737288 | tf_op jit(solution)/shard_map/ppermute | solution.py:23
  26.0 3.7 %collective-permute-start.4 = (f32[14,16,128]{2,1,0:T(8,128)S(1)}, f32[14,16,128]{2,1,0:T(8,128)S(1)}, u32[]{:S(2)}, u32[]{:S(2)}) collective-permute-start(f32[14,16,128]{2,1,0:T(8,128)S(1)} %get-tuple-element.53), channel_id=1, source_target_pairs={{0,1},{1,0},{2,3},{3,2},{4,5},{5,4},{6,7},{7,6},{8,9},{9,8},{10,11... | collective-permute-start | bytes 344072 | tf_op jit(solution)/shard_map/ppermute | solution.py:23
  26.1 4.9 %collective-permute-start.5 = (f32[14,16,128]{2,1,0:T(8,128)S(1)}, f32[14,16,128]{2,1,0:T(8,128)S(1)}, u32[]{:S(2)}, u32[]{:S(2)}) collective-permute-start(f32[14,16,128]{2,1,0:T(8,128)S(1)} %get-tuple-element.54), channel_id=1, source_target_pairs={{0,7},{1,2},{2,1},{3,4},{4,3},{5,6},{6,5},{7,0},{8,15},{9,10},{10,... | collective-permute-start | bytes 344072 | tf_op jit(solution)/shard_map/ppermute | solution.py:23
  31.7 6.3 %collective-permute-start.6 = (f32[10,40,128]{2,1,0:T(8,128)S(1)}, f32[10,40,128]{2,1,0:T(8,128)S(1)}, u32[]{:S(2)}, u32[]{:S(2)}) collective-permute-start(f32[10,40,128]{2,1,0:T(8,128)S(1)} %get-tuple-element.56), channel_id=1, source_target_pairs={{0,8},{1,9},{2,10},{3,11},{4,12},{5,13},{6,14},{7,15},{8,0},{9,1},... | collective-permute-start | bytes 614408 | tf_op jit(solution)/shard_map/ppermute | solution.py:23
  36.5 5.2 %collective-permute-start.7 = (f32[10,40,128]{2,1,0:T(8,128)S(1)}, f32[10,40,128]{2,1,0:T(8,128)S(1)}, u32[]{:S(2)}, u32[]{:S(2)}) collective-permute-start(f32[10,40,128]{2,1,0:T(8,128)S(1)} %get-tuple-element.57), channel_id=1, source_target_pairs={{0,248},{1,249},{2,250},{3,251},{4,252},{5,253},{6,254},{7,255},{8... | collective-permute-start | bytes 614408 | tf_op jit(solution)/shard_map/ppermute | solution.py:23
  43.8 0.7 copy-start.8
  44.5 0.6 copy-start.11
  45.1 14.0 %collective-permute-start.8 = (f32[42,16,128]{2,1,0:T(8,128)}, f32[42,16,128]{2,1,0:T(8,128)}, u32[]{:S(2)}, u32[]{:S(2)}) collective-permute-start(f32[42,16,128]{2,1,0:T(8,128)} %get-tuple-element.65), channel_id=1, source_target_pairs={{0,1},{1,0},{2,3},{3,2},{4,5},{5,4},{6,7},{7,6},{8,9},{9,8},{10,11... | collective-permute-start | bytes 1032200 | tf_op jit(solution)/shard_map/ppermute | solution.py:23
  45.6 13.5 %collective-permute-start.9 = (f32[42,16,128]{2,1,0:T(8,128)}, f32[42,16,128]{2,1,0:T(8,128)}, u32[]{:S(2)}, u32[]{:S(2)}) collective-permute-start(f32[42,16,128]{2,1,0:T(8,128)} %get-tuple-element.66), channel_id=1, source_target_pairs={{0,7},{1,2},{2,1},{3,4},{4,3},{5,6},{6,5},{7,0},{8,15},{9,10},{10,... | collective-permute-start | bytes 1032200 | tf_op jit(solution)/shard_map/ppermute | solution.py:23
  48.2 26.4 %all-to-all-start = ((f32[256,2,128]{2,1,0:T(2,128)}), f32[256,2,128]{2,1,0:T(2,128)S(1)}, u32[]{:S(2)}, u32[]{:S(2)}) async-start(f32[256,2,128]{2,1,0:T(2,128)} %copy-done.8), calls=%async_computation | async-start | bytes 524288 | tf_op jit(solution)/shard_map/all_to_all | solution.py:918
  60.4 3.4 %collective-permute-start.10 = (f32[11,48,128]{2,1,0:T(8,128)S(1)}, f32[11,48,128]{2,1,0:T(8,128)S(1)}, u32[]{:S(2)}, u32[]{:S(2)}) collective-permute-start(f32[11,48,128]{2,1,0:T(8,128)S(1)} %get-tuple-element.68), channel_id=1, source_target_pairs={{0,8},{1,9},{2,10},{3,11},{4,12},{5,13},{6,14},{7,15},{8,0},{9,1},... | collective-permute-start | bytes 811016 | tf_op jit(solution)/shard_map/ppermute | solution.py:23
  62.6 7.6 %collective-permute-start.11 = (f32[11,48,128]{2,1,0:T(8,128)S(1)}, f32[11,48,128]{2,1,0:T(8,128)S(1)}, u32[]{:S(2)}, u32[]{:S(2)}) collective-permute-start(f32[11,48,128]{2,1,0:T(8,128)S(1)} %get-tuple-element.69), channel_id=1, source_target_pairs={{0,248},{1,249},{2,250},{3,251},{4,252},{5,253},{6,254},{7,255},{8... | collective-permute-start | bytes 811016 | tf_op jit(solution)/shard_map/ppermute | solution.py:23
  71.0 40.9 %copy-start.1 = (f32[44,48,128]{2,1,0:T(8,128)}, f32[44,48,128]{2,1,0:T(8,128)S(1)}, u32[]{:S(2)}) copy-start(f32[44,48,128]{2,1,0:T(8,128)S(1)} %shard_map.84.refs_2_) | copy-start | bytes 3244036
  82.0 1.0 copy-start.4
  83.0 2.8 %collective-permute-start.12 = (f32[8,8,128]{2,1,0:T(8,128)S(1)}, f32[8,8,128]{2,1,0:T(8,128)S(1)}, u32[]{:S(2)}, u32[]{:S(2)}) collective-permute-start(f32[8,8,128]{2,1,0:T(8,128)S(1)} %get-tuple-element.72), channel_id=1, source_target_pairs={{0,1},{1,0},{2,3},{3,2},{4,5},{5,4},{6,7},{7,6},{8,9},{9,8},{10,11... | collective-permute-start | bytes 98312 | tf_op jit(solution)/shard_map/ppermute | solution.py:23
  83.7 4.0 %collective-permute-start.13 = (f32[8,8,128]{2,1,0:T(8,128)S(1)}, f32[8,8,128]{2,1,0:T(8,128)S(1)}, u32[]{:S(2)}, u32[]{:S(2)}) collective-permute-start(f32[8,8,128]{2,1,0:T(8,128)S(1)} %get-tuple-element.73), channel_id=1, source_target_pairs={{0,7},{1,2},{2,1},{3,4},{4,3},{5,6},{6,5},{7,0},{8,15},{9,10},{10,... | collective-permute-start | bytes 98312 | tf_op jit(solution)/shard_map/ppermute | solution.py:23
  88.3 3.2 %collective-permute-start.14 = (f32[4,32,128]{2,1,0:T(8,128)S(1)}, f32[4,32,128]{2,1,0:T(8,128)S(1)}, u32[]{:S(2)}, u32[]{:S(2)}) collective-permute-start(f32[4,32,128]{2,1,0:T(8,128)S(1)} %get-tuple-element.74), channel_id=1, source_target_pairs={{0,8},{1,9},{2,10},{3,11},{4,12},{5,13},{6,14},{7,15},{8,0},{9,1},... | collective-permute-start | bytes 196616 | tf_op jit(solution)/shard_map/ppermute | solution.py:23
  90.5 3.7 %collective-permute-start.15 = (f32[4,32,128]{2,1,0:T(8,128)S(1)}, f32[4,32,128]{2,1,0:T(8,128)S(1)}, u32[]{:S(2)}, u32[]{:S(2)}) collective-permute-start(f32[4,32,128]{2,1,0:T(8,128)S(1)} %get-tuple-element.75), channel_id=1, source_target_pairs={{0,248},{1,249},{2,250},{3,251},{4,252},{5,253},{6,254},{7,255},{8... | collective-permute-start | bytes 196616 | tf_op jit(solution)/shard_map/ppermute | solution.py:23
  96.9 25.9 %all-to-all-start.1 = ((f32[256,2,128]{2,1,0:T(2,128)}), f32[256,2,128]{2,1,0:T(2,128)S(1)}, u32[]{:S(2)}, u32[]{:S(2)}) async-start(f32[256,2,128]{2,1,0:T(2,128)} %get-tuple-element.79), calls=%async_computation.1 | async-start | bytes 524288 | tf_op jit(solution)/shard_map/all_to_all | solution.py:918
  107.2 0.9 copy-start.12
  108.1 4.9 %copy-start.5 = (f32[44,48,128]{2,1,0:T(8,128)S(1)}, f32[44,48,128]{2,1,0:T(8,128)}, u32[]{:S(2)}) copy-start(f32[44,48,128]{2,1,0:T(8,128)} %copy-done.4) | copy-start | bytes 3244036
  111.8 1.2 copy-start.2
  114.9 1.0 copy-start.3
  115.9 0.9 copy-start.6
  116.8 0.9 copy-start.7
  117.7 0.7 copy-start.9
  118.4 0.7 copy-start.10
  122.8 0.7 copy-start.18

commit v3 on v2

--- a/solution.py
+++ b/solution.py
@@ -327,12 +327,13 @@
     return jnp.concatenate([hi, lo, hi], axis=0)
 
 
-def sample_kernel(info, vel, cells, offs, c_in, d_in, part, xt, yt, zt):
+def sample_kernel(info, vel, cells, offs, c_in, d_in, part, xt, yt, zt, rv):
     ix, iy, px, py = place(info)
     ok_hi, ok_lo = okf(iy < NGY - 1), okf(iy > 0)
     where, local, off, inv = points(info, cells, offs)
     wz3 = z_table(local, off, inv)
     wx = taps(row_coord(W, 0), local[0], off[0], inv[0])
+    zm = z_masks(1)
     acc = [None] * 3
     for t in range(4):
         slabs = []
@@ -343,6 +344,17 @@
                 lines.append(jnp.concatenate([vel[c, x], hi * ok_hi, lo * ok_lo], axis=0))
             slabs.append(jnp.stack(lines))
         sampled_lines(slabs, wx, t * 8, wz3, acc)
+        for k in range(8):
+            x = t * 8 + k
+            vy = slabs[1][k]
+            total = pltpu.roll(vy, 39, 0)[0:W] - pltpu.roll(vy, 1, 0)[0:W]
+            vz = vel[2, x]
+            total = total + pltpu.roll(vz, 127, 1) * zm[1] - pltpu.roll(vz, 1, 1) * zm[0]
+            if x < W - 1:
+                total = total + vel[0, x + 1]
+            if x > 0:
+                total = total - vel[0, x - 1]
+            rv[x] = -0.5 * total
     for c in range(3):
         part[c] = acc[c]
 
@@ -362,32 +374,18 @@
 
 
 def force_kernel(
-    info, vel, cells, offs, drags, blades, part, xt, yt, zt, c_in, d_in, a_in, b_in,
+    info, cells, offs, drags, blades, part, xt, yt, zt, rv, a_in, b_in,
     g_out, f_out, own_out, c_out, d_out,
-    wide, rv, vt, dom, tmp, tmp1,
+    vt, dom, tmp, tmp1,
 ):
     ix, iy, px, py = place(info)
     ok_hi, ok_lo = okf(iy < NGY - 1), okf(iy > 0)
     okx_hi, okx_lo = okf(ix < NGX - 1), okf(ix > 0)
 
-    def fill(t, u):
-        c = t // W
-        x = t - c * W
-        hi, lo = hi_lo(py, c_in[t], d_in[t])
-        wide[c, x + 4, 0:W, :] = vel[c, x]
-        wide[c, x + 4, W : W + 4, :] = hi * ok_hi
-        wide[c, x + 4, W + 4 : W + 8, :] = lo * ok_lo
-
-    rows(0, 3 * W, 24, fill)
+    slabs = []
     for c in range(3):
-        for k in range(4):
-            e = c * 4 + k
-            hi, lo = hi_lo(px, a_in[e], b_in[e])
-            wide[c, W + 4 + k] = hi * okx_hi
-            wide[c, k] = lo * okx_lo
-
-    start_x = (ix * W).astype(F32)
-    start_y = (iy * W).astype(F32)
+        pairs = [hi_lo(px, a_in[c * 4 + k], b_in[c * 4 + k]) for k in range(4)]
+        slabs.append(jnp.stack([p[1] * okx_lo for p in pairs] + [p[0] * okx_hi for p in pairs]))
     place_of, local, off, inv = points(info, cells, offs)
     (cx, cy, cz), (ox, oy, oz), (nx, ny, nz) = local, off, inv
     z = row_coord(128, 0)
@@ -397,7 +395,6 @@
     wx8 = taps(jnp.where(rim < 4.0, rim - 4.0, rim + (W - 4.0)), cx, ox, nx)
     wy40 = taps(cyc_coord(40, 36), cy, oy, ny)
     acc = [part[c] for c in range(3)]
-    slabs = [jnp.concatenate([wide[c, 0:4], wide[c, W + 4 : W + 8]], axis=0) for c in range(3)]
     sampled_lines(slabs, wx8, 0, wz3, acc)
     sampled = [jnp.sum(acc[c] * wy40, axis=0, keepdims=True) for c in range(3)]
     drag, blade = drags[0], blades[0]
@@ -421,15 +418,8 @@
     fz_wy = force[2] * wy
 
     dom[...] = y_domain(48, W, 8, iy * W, W * NGY)
-    zm = z_masks(1)
-    for x in range(W):
-        vx = wide[0, x + 5, 0:W, :] - wide[0, x + 3, 0:W, :]
-        vy = wide[1, x + 4]
-        vy = pltpu.roll(vy, 39, 0)[0:W] - pltpu.roll(vy, 1, 0)[0:W]
-        vz = wide[2, x + 4, 0:W, :]
-        vz = pltpu.roll(vz, 127, 1) * zm[1] - pltpu.roll(vz, 1, 1) * zm[0]
-        rv[x] = -0.5 * (vx + vy + vz)
-
+    dom[...] = y_domain(48, W, 8, iy * W, W * NGY)
+    edge = {0: 0.5 * slabs[0][3, 0:W], W - 1: -0.5 * slabs[0][4, 0:W]}
     for t in range(6):
         l1, l2 = [], []
         for k in range(7):
@@ -447,7 +437,8 @@
             i = t * 7 + k
             share = r[k] * (dom[...] * x_in(ix * W - 5, i, W * NGX))
             if 5 <= i < W + 5:
-                g_out[i + 4, 0:W, :] = share[0:W] + rv[i - 5]
+                own = share[0:W] + rv[i - 5]
+                g_out[i + 4, 0:W, :] = own + edge[i - 5] if i - 5 in edge else own
                 g_out[i + 4, W:48, :] = share[W:48]
             else:
                 g_out[i + 4] = share
@@ -933,17 +924,17 @@
     c0, d0 = swap_gy(jnp.where(py == 0, top, bottom), jnp.where(py == 0, bottom, top))
     a0, b0 = call(pack_gx, [(12, 40, 128)] * 2, [], info, velocity[:, :4], velocity[:, W - 4 :], c0, d0)
     a0, b0 = swap_gx(a0, b0)
-    part, xt, yt, zt = call(
-        sample_kernel, [(3, 40, P_), (2, 48, P_), (2, 48, P_), (2, P_, 128)], [], info, velocity, point_cells, point_offsets, c0, d0
+    part, xt, yt, zt, rv = call(
+        sample_kernel, [(3, 40, P_), (2, 48, P_), (2, 48, P_), (2, P_, 128), (W, W, 128)], [], info, velocity, point_cells, point_offsets, c0, d0
     )
     g, f, own1, c1, d1 = call(
         force_kernel,
         [(50, 48, 128), (32, 128), (12, 24, 128), (14, 16, 128), (14, 16, 128)],
         [
-            VMEM((3, 40, 40, 128), F32), VMEM((W, W, 128), F32), VMEM((50, 48, 128), F32), VMEM((48, 128), F32),
+            VMEM((50, 48, 128), F32), VMEM((48, 128), F32),
             VMEM((32, 48, 128), F32), VMEM((24, 24, 128), F32),
         ],
-        info, velocity, point_cells, point_offsets, drag, blade_speed, part, xt, yt, zt, c0, d0, a0, b0,
+        info, point_cells, point_offsets, drag, blade_speed, part, xt, yt, zt, rv, a0, b0,
     )
     c1, d1 = swap_gy(c1, d1)
     shares, a1, b1 = call(merge1_gx, [(12, 48, 128), (10, 40, 128), (10, 40, 128)], [], info, own1, f, c1, d1)

time: 132 us -> 131 us (level)
  transfers between devices with their start and end apart: 18 -> 18, of which waited for: 13 -> 13; matrix products, arithmetic and copies ran while one was open for 1% -> 1% of each run, Pallas kernels for 8% -> 9%
where the time goes in v3:
time: 131 us
  starting transfers between devices  47.3 us (36%)
  Pallas kernels  36.5 us (28%)
  waiting for transfers between devices  33.2 us (25%)
  local copies, waits for them, and re-layouts  10.4 us (8%)
  between operations  1.73 us (1%)
  other arithmetic  1.38 us (1%)
    pallas_call x14, Pallas kernels, call(): pl.pallas_call(body, out_shape=[jax.ShapeDtypeStruct(s, F32) for s in out...  36.5 us
    ppermute x16, starting transfers between devices, swap(): return lax.ppermute(x, AXES, perm)  26.2 us
    ppermute x16, waiting for transfers between devices, swap(): return lax.ppermute(x, AXES, perm)  25.9 us
    all_to_all x2, starting transfers between devices, gather3(): return lax.all_to_all(packed, AXES, 0, 0, tiled=True).reshape(NGX, 16, 128)  21.2 us
    unnamed x38, local copies, waits for them, and re-layouts  9.32 us
    all_to_all x2, waiting for transfers between devices, gather3(): return lax.all_to_all(packed, AXES, 0, 0, tiled=True).reshape(NGX, 16, 128)  7.39 us
  transfers between devices with their start and end apart: 18, of which 13 were waited for; matrix products, arithmetic and copies ran while one was open for 1% of the time, Pallas kernels for 9%

profile of v3, /device:TPU:1, one launch (start us, length us, event | category | flops | bytes accessed | tf_op | source)
XLA Modules:
  0.0 130.6 jit_solution(11588609491598916213)
XLA Ops:
  0.7 1.3 slice_select_fusion
  2.0 2.6 %collective-permute-start = (f32[96,4,128]{2,1,0:T(4,128)S(1)}, f32[96,4,128]{2,1,0:T(4,128)S(1)}, u32[]{:S(2)}, u32[]{:S(2)}) collective-permute-start(f32[96,4,128]{2,1,0:T(4,128)S(1)} %bitcast.11), channel_id=1, source_target_pairs={{0,1},{1,0},{2,3},{3,2},{4,5},{5,4},{6,7},{7,6},{8,9},{9,8},{10,11... | collective-permute-start | bytes 589832 | tf_op jit(solution)/shard_map/ppermute | solution.py:23
  4.5 4.7 %collective-permute-start.1 = (f32[96,4,128]{2,1,0:T(4,128)S(1)}, f32[96,4,128]{2,1,0:T(4,128)S(1)}, u32[]{:S(2)}, u32[]{:S(2)}) collective-permute-start(f32[96,4,128]{2,1,0:T(4,128)S(1)} %bitcast.10), channel_id=1, source_target_pairs={{0,7},{1,2},{2,1},{3,4},{4,3},{5,6},{6,5},{7,0},{8,15},{9,10},{10,... | collective-permute-start | bytes 589832 | tf_op jit(solution)/shard_map/ppermute | solution.py:23
  9.9 1.1 fusion
  11.0 2.5 %collective-permute-done.1.refs_5_.refs_4_ = f32[96,4,128]{2,1,0:T(4,128)S(1)} collective-permute-done((f32[96,4,128]{2,1,0:T(4,128)S(1)}, f32[96,4,128]{2,1,0:T(4,128)S(1)}, u32[]{:S(2)}, u32[]{:S(2)}) %collective-permute-start.1) | collective-permute-done | bytes 196640 | tf_op jit(solution)/shard_map/ppermute | solution.py:23
  14.1 1.6 %collective-permute-start.2 = (f32[12,40,128]{2,1,0:T(8,128)S(1)}, f32[12,40,128]{2,1,0:T(8,128)S(1)}, u32[]{:S(2)}, u32[]{:S(2)}) collective-permute-start(f32[12,40,128]{2,1,0:T(8,128)S(1)} %get-tuple-element.51), channel_id=1, source_target_pairs={{0,8},{1,9},{2,10},{3,11},{4,12},{5,13},{6,14},{7,15},{8,0},{9,1},... | collective-permute-start | bytes 737288 | tf_op jit(solution)/shard_map/ppermute | solution.py:23
  15.7 1.3 collective-permute-start.3
  17.0 2.2 %shard_map.77 = (f32[3,40,256]{2,1,0:T(8,128)S(1)}, f32[2,48,256]{2,1,0:T(8,128)S(1)}, f32[2,48,256]{2,1,0:T(8,128)S(1)}, f32[2,256,128]{2,1,0:T(8,128)S(1)}, f32[32,32,128]{2,1,0:T(8,128)S(1)}) custom-call(s32[3]{0:T(128)S(1)} %pad_add_fusion.refs_0_, f32[3,32,32,128]{3,2,1,0:T(8,128)S(1)} %copy-done, s32[3,1,1,256]{3,2,1,0:T(1,128)S(1)} %copy-done.14, ...), custom_call_target="tpu_custom_call" | custom-call | flops 10000000 | bytes 3078156 | tf_op jit(solution)/shard_map/pallas_call | solution.py:102
  19.2 2.2 %collective-permute-done.3.refs_11_ = f32[12,40,128]{2,1,0:T(8,128)S(1)} collective-permute-done((f32[12,40,128]{2,1,0:T(8,128)S(1)}, f32[12,40,128]{2,1,0:T(8,128)S(1)}, u32[]{:S(2)}, u32[]{:S(2)}) %collective-permute-start.3) | collective-permute-done | bytes 245792 | tf_op jit(solution)/shard_map/ppermute | solution.py:23
  21.4 3.7 %shard_map.79 = (f32[50,48,128]{2,1,0:T(8,128)S(1)}, f32[32,128]{1,0:T(8,128)S(1)}, f32[12,24,128]{2,1,0:T(8,128)S(1)}, f32[14,16,128]{2,1,0:T(8,128)S(1)}, f32[14,16,128]{2,1,0:T(8,128)S(1)}) custom-call(s32[3]{0:T(128)S(1)} %pad_add_fusion.refs_0_, s32[3,1,1,256]{3,2,1,0:T(1,128)S(1)} %copy-done.14, f32[3,1,1,256]{3,2,1,0:T(1,128)S(1)} %copy-done.15, ...), custom_call_target="tpu_custom_call" | custom-call | flops 10000000 | bytes 3227660 | tf_op jit(solution)/shard_map/pallas_call | solution.py:102
  25.1 2.8 %collective-permute-start.5 = (f32[14,16,128]{2,1,0:T(8,128)S(1)}, f32[14,16,128]{2,1,0:T(8,128)S(1)}, u32[]{:S(2)}, u32[]{:S(2)}) collective-permute-start(f32[14,16,128]{2,1,0:T(8,128)S(1)} %get-tuple-element.56), channel_id=1, source_target_pairs={{0,7},{1,2},{2,1},{3,4},{4,3},{5,6},{6,5},{7,0},{8,15},{9,10},{10,... | collective-permute-start | bytes 344072 | tf_op jit(solution)/shard_map/ppermute | solution.py:23
  27.9 0.9 collective-permute-done.4.refs_3_
  28.8 1.3 %collective-permute-done.5.refs_4_ = f32[14,16,128]{2,1,0:T(8,128)S(1)} collective-permute-done((f32[14,16,128]{2,1,0:T(8,128)S(1)}, f32[14,16,128]{2,1,0:T(8,128)S(1)}, u32[]{:S(2)}, u32[]{:S(2)}) %collective-permute-start.5) | collective-permute-done | bytes 114720 | tf_op jit(solution)/shard_map/ppermute | solution.py:23
  30.7 4.8 %collective-permute-start.6 = (f32[10,40,128]{2,1,0:T(8,128)S(1)}, f32[10,40,128]{2,1,0:T(8,128)S(1)}, u32[]{:S(2)}, u32[]{:S(2)}) collective-permute-start(f32[10,40,128]{2,1,0:T(8,128)S(1)} %get-tuple-element.58), channel_id=1, source_target_pairs={{0,8},{1,9},{2,10},{3,11},{4,12},{5,13},{6,14},{7,15},{8,0},{9,1},... | collective-permute-start | bytes 614408 | tf_op jit(solution)/shard_map/ppermute | solution.py:23
  35.5 1.4 %shard_map.82 = (f32[42,16,128]{2,1,0:T(8,128)}, f32[42,16,128]{2,1,0:T(8,128)}) custom-call(s32[3]{0:T(128)S(1)} %pad_add_fusion.refs_0_, f32[50,48,128]{2,1,0:T(8,128)S(1)} %get-tuple-element.66.refs_1_), custom_call_target="tpu_custom_call" | custom-call | flops 10000000 | bytes 1916940 | tf_op jit(solution)/shard_map/pallas_call | solution.py:102
  37.0 3.7 %collective-permute-done.7.refs_6_ = f32[10,40,128]{2,1,0:T(8,128)S(1)} collective-permute-done((f32[10,40,128]{2,1,0:T(8,128)S(1)}, f32[10,40,128]{2,1,0:T(8,128)S(1)}, u32[]{:S(2)}, u32[]{:S(2)}) %collective-permute-start.7) | collective-permute-done | bytes 204832 | tf_op jit(solution)/shard_map/ppermute | solution.py:23
  40.7 2.1 %shard_map.81 = (f32[18,48,128]{2,1,0:T(8,128)S(1)}, f32[256,2,128]{2,1,0:T(2,128)S(1)}, f32[9,32,128]{2,1,0:T(8,128)S(1)}) custom-call(s32[3]{0:T(128)S(1)} %pad_add_fusion.refs_0_, f32[12,48,128]{2,1,0:T(8,128)S(1)} %get-tuple-element.57.refs_1_, f32[32,128]{1,0:T(8,128)S(1)} %get-tuple-element.54.refs_2_, ...), custom_call_target="tpu_custom_call" | custom-call | flops 10000000 | bytes 1802252 | tf_op jit(solution)/shard_map/pallas_call | solution.py:102
  42.8 0.7 copy-done.8
  44.6 2.7 %collective-permute-start.9 = (f32[42,16,128]{2,1,0:T(8,128)}, f32[42,16,128]{2,1,0:T(8,128)}, u32[]{:S(2)}, u32[]{:S(2)}) collective-permute-start(f32[42,16,128]{2,1,0:T(8,128)} %get-tuple-element.68), channel_id=1, source_target_pairs={{0,7},{1,2},{2,1},{3,4},{4,3},{5,6},{6,5},{7,0},{8,15},{9,10},{10,... | collective-permute-start | bytes 1032200 | tf_op jit(solution)/shard_map/ppermute | solution.py:23
  47.3 10.9 %all-to-all-start = ((f32[256,2,128]{2,1,0:T(2,128)}), f32[256,2,128]{2,1,0:T(2,128)S(1)}, u32[]{:S(2)}, u32[]{:S(2)}) async-start(f32[256,2,128]{2,1,0:T(2,128)} %copy-done.8), calls=%async_computation | async-start | bytes 524288 | tf_op jit(solution)/shard_map/all_to_all | solution.py:909
  58.2 1.2 shard_map.83
  59.4 2.2 %collective-permute-start.10 = (f32[11,48,128]{2,1,0:T(8,128)S(1)}, f32[11,48,128]{2,1,0:T(8,128)S(1)}, u32[]{:S(2)}, u32[]{:S(2)}) collective-permute-start(f32[11,48,128]{2,1,0:T(8,128)S(1)} %get-tuple-element.70), channel_id=1, source_target_pairs={{0,8},{1,9},{2,10},{3,11},{4,12},{5,13},{6,14},{7,15},{8,0},{9,1},... | collective-permute-start | bytes 811016 | tf_op jit(solution)/shard_map/ppermute | solution.py:23
  61.6 1.2 collective-permute-done.10.refs_2_
  62.8 6.5 %collective-permute-done.11.refs_3_ = f32[11,48,128]{2,1,0:T(8,128)S(1)} collective-permute-done((f32[11,48,128]{2,1,0:T(8,128)S(1)}, f32[11,48,128]{2,1,0:T(8,128)S(1)}, u32[]{:S(2)}, u32[]{:S(2)}) %collective-permute-start.11) | collective-permute-done | bytes 270368 | tf_op jit(solution)/shard_map/ppermute | solution.py:23
  69.3 0.7 shard_map.84.refs_2_
  70.0 3.7 %all-to-all-done = f32[256,2,128]{2,1,0:T(2,128)S(1)} async-done(((f32[256,2,128]{2,1,0:T(2,128)}), f32[256,2,128]{2,1,0:T(2,128)S(1)}, u32[]{:S(2)}, u32[]{:S(2)}) %all-to-all-start) | async-done | bytes 262176 | tf_op jit(solution)/shard_map/all_to_all | solution.py:909
  73.7 7.3 %shard_map.85 = (f32[44,48,128]{2,1,0:T(8,128)S(1)}, f32[8,16,128]{2,1,0:T(8,128)S(1)}, f32[8,8,128]{2,1,0:T(8,128)S(1)}, f32[8,8,128]{2,1,0:T(8,128)S(1)}) custom-call(s32[3]{0:T(128)S(1)} %pad_add_fusion.refs_0_, f32[32,16,128]{2,1,0:T(8,128)S(1)} %bitcast.8, f32[44,48,128]{2,1,0:T(8,128)S(1)} %shard_map.84.refs_2_, ...), custom_call_target="tpu_custom_call" | custom-call | flops 10000000 | bytes 2998284 | tf_op jit(solution)/shard_map/pallas_call | solution.py:102
  81.0 1.0 copy-done.4
  82.0 0.7 collective-permute-start.12
  82.7 2.0 %collective-permute-done.12.refs_2_ = f32[8,8,128]{2,1,0:T(8,128)S(1)} collective-permute-done((f32[8,8,128]{2,1,0:T(8,128)S(1)}, f32[8,8,128]{2,1,0:T(8,128)S(1)}, u32[]{:S(2)}, u32[]{:S(2)}) %collective-permute-start.12) | collective-permute-done | bytes 32800 | tf_op jit(solution)/shard_map/ppermute | solution.py:23
  84.8 1.9 %collective-permute-done.13.refs_3_ = f32[8,8,128]{2,1,0:T(8,128)S(1)} collective-permute-done((f32[8,8,128]{2,1,0:T(8,128)S(1)}, f32[8,8,128]{2,1,0:T(8,128)S(1)}, u32[]{:S(2)}, u32[]{:S(2)}) %collective-permute-start.13) | collective-permute-done | bytes 32800 | tf_op jit(solution)/shard_map/ppermute | solution.py:23
  87.3 2.3 %collective-permute-start.14 = (f32[4,32,128]{2,1,0:T(8,128)S(1)}, f32[4,32,128]{2,1,0:T(8,128)S(1)}, u32[]{:S(2)}, u32[]{:S(2)}) collective-permute-start(f32[4,32,128]{2,1,0:T(8,128)S(1)} %get-tuple-element.76), channel_id=1, source_target_pairs={{0,8},{1,9},{2,10},{3,11},{4,12},{5,13},{6,14},{7,15},{8,0},{9,1},... | collective-permute-start | bytes 196616 | tf_op jit(solution)/shard_map/ppermute | solution.py:23
  89.6 0.9 collective-permute-done.14.refs_4_
  90.5 2.8 %collective-permute-done.15.refs_5_ = f32[4,32,128]{2,1,0:T(8,128)S(1)} collective-permute-done((f32[4,32,128]{2,1,0:T(8,128)S(1)}, f32[4,32,128]{2,1,0:T(8,128)S(1)}, u32[]{:S(2)}, u32[]{:S(2)}) %collective-permute-start.15) | collective-permute-done | bytes 65568 | tf_op jit(solution)/shard_map/ppermute | solution.py:23
  93.3 2.6 %shard_map.87 = (f32[18,48,128]{2,1,0:T(8,128)S(1)}, f32[256,2,128]{2,1,0:T(2,128)}) custom-call(s32[3]{0:T(128)S(1)} %pad_add_fusion.refs_0_, f32[8,16,128]{2,1,0:T(8,128)S(1)} %get-tuple-element.73.refs_1_, f32[8,8,128]{2,1,0:T(8,128)S(1)} %collective-permute-done.12.refs_2_, f32[8,8,128]{2,1,0:T(8,128)S(1)} %collective-permute-done.13.refs_3_, ...), custom_call_target="tpu_custom_call" | custom-call | flops 10000000 | bytes 966668 | tf_op jit(solution)/shard_map/pallas_call | solution.py:102
  95.9 10.3 %all-to-all-start.1 = ((f32[256,2,128]{2,1,0:T(2,128)}), f32[256,2,128]{2,1,0:T(2,128)S(1)}, u32[]{:S(2)}, u32[]{:S(2)}) async-start(f32[256,2,128]{2,1,0:T(2,128)} %get-tuple-element.81), calls=%async_computation.1 | async-start | bytes 524288 | tf_op jit(solution)/shard_map/all_to_all | solution.py:909
  106.2 0.9 copy-done.12
  107.1 3.7 %shard_map.89.refs_8_ = f32[3,32,32,128]{3,2,1,0:T(8,128)S(1)} custom-call(s32[3]{0:T(128)S(1)} %pad_add_fusion.refs_0_, f32[3,32,32,128]{3,2,1,0:T(8,128)S(1)} %copy-done, f32[9,32,128]{2,1,0:T(8,128)S(1)} %copy-done.12), custom_call_target="tpu_custom_call" | custom-call | flops 10000000 | bytes 3293196 | tf_op jit(solution)/shard_map/pallas_call | solution.py:102
  110.9 1.2 copy-done.2
  112.0 1.9 %shard_map.88 = (f32[36,48,128]{2,1,0:T(8,128)S(1)}, f32[36,48,128]{2,1,0:T(8,128)S(1)}, f32[16,24,128]{2,1,0:T(8,128)S(1)}, f32[16,24,128]{2,1,0:T(8,128)S(1)}, f32[44,48,128]{2,1,0:T(8,128)S(1)}) custom-call(s32[3]{0:T(128)S(1)} %pad_add_fusion.refs_0_, f32[18,48,128]{2,1,0:T(8,128)S(1)} %get-tuple-element.82.refs_1_, f32[44,48,128]{2,1,0:T(8,128)S(1)} %copy-done.5), custom_call_target="tpu_custom_call" | custom-call | flops 10000000 | bytes 4767756 | tf_op jit(solution)/shard_map/pallas_call | solution.py:102
  113.9 1.0 copy-done.3
  114.9 0.9 copy-done.6
  115.8 0.9 copy-done.7
  116.8 0.7 copy-done.9
  117.4 0.7 copy-done.10
  118.1 3.7 %all-to-all-done.1 = f32[256,2,128]{2,1,0:T(2,128)S(1)} async-done(((f32[256,2,128]{2,1,0:T(2,128)}), f32[256,2,128]{2,1,0:T(2,128)S(1)}, u32[]{:S(2)}, u32[]{:S(2)}) %all-to-all-start.1) | async-done | bytes 262176 | tf_op jit(solution)/shard_map/all_to_all | solution.py:909
  121.8 0.7 copy-done.18
  122.5 7.9 %shard_map.90 = (f32[3,32,32,128]{3,2,1,0:T(8,128)}, f32[32,32,128]{2,1,0:T(8,128)}) custom-call(s32[3]{0:T(128)} %copy-done.13, f32[32,16,128]{2,1,0:T(8,128)} %bitcast.9, f32[44,48,128]{2,1,0:T(8,128)} %copy-done.1, f32[44,48,128]{2,1,0:T(8,128)} %copy-done.3, f32[36,48,128]{2,1,0:T(8,128)} %copy-done.6, f32[36,48,128]{2,1,0:T(8,128)} %copy-done.7, ...), custom_call_target="tpu_custom_call" | custom-call | flops 10000000 | bytes 8257548 | tf_op jit(solution)/shard_map/pallas_call | solution.py:102
  (43 shorter events, 3.1 us)
Async XLA Ops:
  0.6 16.4 %copy-start = (f32[3,32,32,128]{3,2,1,0:T(8,128)S(1)}, f32[3,32,32,128]{3,2,1,0:T(8,128)}, u32[]{:S(2)}) copy-start(f32[3,32,32,128]{3,2,1,0:T(8,128)} %refs_1_.5) | copy-start | bytes 4718596
  0.6 16.4 %copy-start.15 = (f32[3,1,1,256]{3,2,1,0:T(1,128)S(1)}, f32[3,1,1,256]{3,2,1,0:T(1,128)}, u32[]{:S(2)}) copy-start(f32[3,1,1,256]{3,2,1,0:T(1,128)} %refs_2_.3) | copy-start | bytes 9220
  0.7 16.4 %copy-start.14 = (s32[3,1,1,256]{3,2,1,0:T(1,128)S(1)}, s32[3,1,1,256]{3,2,1,0:T(1,128)}, u32[]{:S(2)}) copy-start(s32[3,1,1,256]{3,2,1,0:T(1,128)} %refs_1_.4) | copy-start | bytes 9220
  2.0 9.0 %collective-permute-start = (f32[96,4,128]{2,1,0:T(4,128)S(1)}, f32[96,4,128]{2,1,0:T(4,128)S(1)}, u32[]{:S(2)}, u32[]{:S(2)}) collective-permute-start(f32[96,4,128]{2,1,0:T(4,128)S(1)} %bitcast.11), channel_id=1, source_target_pairs={{0,1},{1,0},{2,3},{3,2},{4,5},{5,4},{6,7},{7,6},{8,9},{9,8},{10,11... | collective-permute-start | bytes 589832 | tf_op jit(solution)/shard_map/ppermute | solution.py:23
  4.5 9.0 %collective-permute-start.1 = (f32[96,4,128]{2,1,0:T(4,128)S(1)}, f32[96,4,128]{2,1,0:T(4,128)S(1)}, u32[]{:S(2)}, u32[]{:S(2)}) collective-permute-start(f32[96,4,128]{2,1,0:T(4,128)S(1)} %bitcast.10), channel_id=1, source_target_pairs={{0,7},{1,2},{2,1},{3,4},{4,3},{5,6},{6,5},{7,0},{8,15},{9,10},{10,... | collective-permute-start | bytes 589832 | tf_op jit(solution)/shard_map/ppermute | solution.py:23
  9.9 100.9 %copy-start.13 = (s32[3]{0:T(128)}, s32[3]{0:T(128)S(1)}, u32[]{:S(2)}) copy-start(s32[3]{0:T(128)S(1)} %pad_add_fusion.refs_0_) | copy-start | bytes 40
  11.0 10.4 %copy-start.16 = (f32[1,1,256]{2,1,0:T(1,128)S(1)}, f32[1,1,256]{2,1,0:T(1,128)}, u32[]{:S(2)}) copy-start(f32[1,1,256]{2,1,0:T(1,128)} %refs_3_.3) | copy-start | bytes 3076
  11.0 10.4 %copy-start.17 = (f32[1,1,256]{2,1,0:T(1,128)S(1)}, f32[1,1,256]{2,1,0:T(1,128)}, u32[]{:S(2)}) copy-start(f32[1,1,256]{2,1,0:T(1,128)} %refs_4_.1) | copy-start | bytes 3076
  14.1 5.1 %collective-permute-start.2 = (f32[12,40,128]{2,1,0:T(8,128)S(1)}, f32[12,40,128]{2,1,0:T(8,128)S(1)}, u32[]{:S(2)}, u32[]{:S(2)}) collective-permute-start(f32[12,40,128]{2,1,0:T(8,128)S(1)} %get-tuple-element.51), channel_id=1, source_target_pairs={{0,8},{1,9},{2,10},{3,11},{4,12},{5,13},{6,14},{7,15},{8,0},{9,1},... | collective-permute-start | bytes 737288 | tf_op jit(solution)/shard_map/ppermute | solution.py:23
  15.7 5.6 %collective-permute-start.3 = (f32[12,40,128]{2,1,0:T(8,128)S(1)}, f32[12,40,128]{2,1,0:T(8,128)S(1)}, u32[]{:S(2)}, u32[]{:S(2)}) collective-permute-start(f32[12,40,128]{2,1,0:T(8,128)S(1)} %get-tuple-element.52), channel_id=1, source_target_pairs={{0,248},{1,249},{2,250},{3,251},{4,252},{5,253},{6,254},{7,255},{8... | collective-permute-start | bytes 737288 | tf_op jit(solution)/shard_map/ppermute | solution.py:23
  25.0 3.7 %collective-permute-start.4 = (f32[14,16,128]{2,1,0:T(8,128)S(1)}, f32[14,16,128]{2,1,0:T(8,128)S(1)}, u32[]{:S(2)}, u32[]{:S(2)}) collective-permute-start(f32[14,16,128]{2,1,0:T(8,128)S(1)} %get-tuple-element.55), channel_id=1, source_target_pairs={{0,1},{1,0},{2,3},{3,2},{4,5},{5,4},{6,7},{7,6},{8,9},{9,8},{10,11... | collective-permute-start | bytes 344072 | tf_op jit(solution)/shard_map/ppermute | solution.py:23
  25.1 4.9 %collective-permute-start.5 = (f32[14,16,128]{2,1,0:T(8,128)S(1)}, f32[14,16,128]{2,1,0:T(8,128)S(1)}, u32[]{:S(2)}, u32[]{:S(2)}) collective-permute-start(f32[14,16,128]{2,1,0:T(8,128)S(1)} %get-tuple-element.56), channel_id=1, source_target_pairs={{0,7},{1,2},{2,1},{3,4},{4,3},{5,6},{6,5},{7,0},{8,15},{9,10},{10,... | collective-permute-start | bytes 344072 | tf_op jit(solution)/shard_map/ppermute | solution.py:23
  30.7 6.3 %collective-permute-start.6 = (f32[10,40,128]{2,1,0:T(8,128)S(1)}, f32[10,40,128]{2,1,0:T(8,128)S(1)}, u32[]{:S(2)}, u32[]{:S(2)}) collective-permute-start(f32[10,40,128]{2,1,0:T(8,128)S(1)} %get-tuple-element.58), channel_id=1, source_target_pairs={{0,8},{1,9},{2,10},{3,11},{4,12},{5,13},{6,14},{7,15},{8,0},{9,1},... | collective-permute-start | bytes 614408 | tf_op jit(solution)/shard_map/ppermute | solution.py:23
  35.5 5.2 %collective-permute-start.7 = (f32[10,40,128]{2,1,0:T(8,128)S(1)}, f32[10,40,128]{2,1,0:T(8,128)S(1)}, u32[]{:S(2)}, u32[]{:S(2)}) collective-permute-start(f32[10,40,128]{2,1,0:T(8,128)S(1)} %get-tuple-element.59), channel_id=1, source_target_pairs={{0,248},{1,249},{2,250},{3,251},{4,252},{5,253},{6,254},{7,255},{8... | collective-permute-start | bytes 614408 | tf_op jit(solution)/shard_map/ppermute | solution.py:23
  42.8 0.7 copy-start.8
  43.5 0.6 copy-start.11
  44.2 14.0 %collective-permute-start.8 = (f32[42,16,128]{2,1,0:T(8,128)}, f32[42,16,128]{2,1,0:T(8,128)}, u32[]{:S(2)}, u32[]{:S(2)}) collective-permute-start(f32[42,16,128]{2,1,0:T(8,128)} %get-tuple-element.67), channel_id=1, source_target_pairs={{0,1},{1,0},{2,3},{3,2},{4,5},{5,4},{6,7},{7,6},{8,9},{9,8},{10,11... | collective-permute-start | bytes 1032200 | tf_op jit(solution)/shard_map/ppermute | solution.py:23
  44.6 13.5 %collective-permute-start.9 = (f32[42,16,128]{2,1,0:T(8,128)}, f32[42,16,128]{2,1,0:T(8,128)}, u32[]{:S(2)}, u32[]{:S(2)}) collective-permute-start(f32[42,16,128]{2,1,0:T(8,128)} %get-tuple-element.68), channel_id=1, source_target_pairs={{0,7},{1,2},{2,1},{3,4},{4,3},{5,6},{6,5},{7,0},{8,15},{9,10},{10,... | collective-permute-start | bytes 1032200 | tf_op jit(solution)/shard_map/ppermute | solution.py:23
  47.3 26.4 %all-to-all-start = ((f32[256,2,128]{2,1,0:T(2,128)}), f32[256,2,128]{2,1,0:T(2,128)S(1)}, u32[]{:S(2)}, u32[]{:S(2)}) async-start(f32[256,2,128]{2,1,0:T(2,128)} %copy-done.8), calls=%async_computation | async-start | bytes 524288 | tf_op jit(solution)/shard_map/all_to_all | solution.py:909
  59.4 3.4 %collective-permute-start.10 = (f32[11,48,128]{2,1,0:T(8,128)S(1)}, f32[11,48,128]{2,1,0:T(8,128)S(1)}, u32[]{:S(2)}, u32[]{:S(2)}) collective-permute-start(f32[11,48,128]{2,1,0:T(8,128)S(1)} %get-tuple-element.70), channel_id=1, source_target_pairs={{0,8},{1,9},{2,10},{3,11},{4,12},{5,13},{6,14},{7,15},{8,0},{9,1},... | collective-permute-start | bytes 811016 | tf_op jit(solution)/shard_map/ppermute | solution.py:23
  61.6 7.6 %collective-permute-start.11 = (f32[11,48,128]{2,1,0:T(8,128)S(1)}, f32[11,48,128]{2,1,0:T(8,128)S(1)}, u32[]{:S(2)}, u32[]{:S(2)}) collective-permute-start(f32[11,48,128]{2,1,0:T(8,128)S(1)} %get-tuple-element.71), channel_id=1, source_target_pairs={{0,248},{1,249},{2,250},{3,251},{4,252},{5,253},{6,254},{7,255},{8... | collective-permute-start | bytes 811016 | tf_op jit(solution)/shard_map/ppermute | solution.py:23
  70.0 40.9 %copy-start.1 = (f32[44,48,128]{2,1,0:T(8,128)}, f32[44,48,128]{2,1,0:T(8,128)S(1)}, u32[]{:S(2)}) copy-start(f32[44,48,128]{2,1,0:T(8,128)S(1)} %shard_map.84.refs_2_) | copy-start | bytes 3244036
  81.0 1.0 copy-start.4
  82.0 2.8 %collective-permute-start.12 = (f32[8,8,128]{2,1,0:T(8,128)S(1)}, f32[8,8,128]{2,1,0:T(8,128)S(1)}, u32[]{:S(2)}, u32[]{:S(2)}) collective-permute-start(f32[8,8,128]{2,1,0:T(8,128)S(1)} %get-tuple-element.74), channel_id=1, source_target_pairs={{0,1},{1,0},{2,3},{3,2},{4,5},{5,4},{6,7},{7,6},{8,9},{9,8},{10,11... | collective-permute-start | bytes 98312 | tf_op jit(solution)/shard_map/ppermute | solution.py:23
  82.7 4.0 %collective-permute-start.13 = (f32[8,8,128]{2,1,0:T(8,128)S(1)}, f32[8,8,128]{2,1,0:T(8,128)S(1)}, u32[]{:S(2)}, u32[]{:S(2)}) collective-permute-start(f32[8,8,128]{2,1,0:T(8,128)S(1)} %get-tuple-element.75), channel_id=1, source_target_pairs={{0,7},{1,2},{2,1},{3,4},{4,3},{5,6},{6,5},{7,0},{8,15},{9,10},{10,... | collective-permute-start | bytes 98312 | tf_op jit(solution)/shard_map/ppermute | solution.py:23
  87.3 3.2 %collective-permute-start.14 = (f32[4,32,128]{2,1,0:T(8,128)S(1)}, f32[4,32,128]{2,1,0:T(8,128)S(1)}, u32[]{:S(2)}, u32[]{:S(2)}) collective-permute-start(f32[4,32,128]{2,1,0:T(8,128)S(1)} %get-tuple-element.76), channel_id=1, source_target_pairs={{0,8},{1,9},{2,10},{3,11},{4,12},{5,13},{6,14},{7,15},{8,0},{9,1},... | collective-permute-start | bytes 196616 | tf_op jit(solution)/shard_map/ppermute | solution.py:23
  89.6 3.7 %collective-permute-start.15 = (f32[4,32,128]{2,1,0:T(8,128)S(1)}, f32[4,32,128]{2,1,0:T(8,128)S(1)}, u32[]{:S(2)}, u32[]{:S(2)}) collective-permute-start(f32[4,32,128]{2,1,0:T(8,128)S(1)} %get-tuple-element.77), channel_id=1, source_target_pairs={{0,248},{1,249},{2,250},{3,251},{4,252},{5,253},{6,254},{7,255},{8... | collective-permute-start | bytes 196616 | tf_op jit(solution)/shard_map/ppermute | solution.py:23
  95.9 25.9 %all-to-all-start.1 = ((f32[256,2,128]{2,1,0:T(2,128)}), f32[256,2,128]{2,1,0:T(2,128)S(1)}, u32[]{:S(2)}, u32[]{:S(2)}) async-start(f32[256,2,128]{2,1,0:T(2,128)} %get-tuple-element.81), calls=%async_computation.1 | async-start | bytes 524288 | tf_op jit(solution)/shard_map/all_to_all | solution.py:909
  106.2 0.9 copy-start.12
  107.1 4.9 %copy-start.5 = (f32[44,48,128]{2,1,0:T(8,128)S(1)}, f32[44,48,128]{2,1,0:T(8,128)}, u32[]{:S(2)}) copy-start(f32[44,48,128]{2,1,0:T(8,128)} %copy-done.4) | copy-start | bytes 3244036
  110.9 1.2 copy-start.2
  113.9 1.0 copy-start.3
  114.9 0.9 copy-start.6
  115.8 0.9 copy-start.7
  116.8 0.7 copy-start.9
  117.4 0.7 copy-start.10
  121.8 0.7 copy-start.18
